TPU v7x, 768 devices: a whole 4x8x12 slice. The times are simulated.
768 devices in a mesh: replica: 4 (over z_hi, core), fsdp: 192 (over z_lo, x, y).
Axes of the slice: x: 4, y: 8, z: 12 (z_hi: 2, z_lo: 6; z = z_hi * 6 + z_lo), core: 2. Of those that a mesh axis runs over, the one named last changes fastest.
Arguments:
- tokens: bfloat16 [4, 1536, 4096], P('replica', 'fsdp'), may hold values from -6 to 6
- gate_weight: bfloat16 [4096, 24576], P(None, 'fsdp'), may hold values from -0.09375 to 0.09375
- pseudo_grad: bfloat16 [4, 4096, 24576], P('replica', None, 'fsdp'), may hold values from -0.125 to 0.125
- anchor: float32 [4096, 24576], P('replica', 'fsdp'), may hold values from -0.09375 to 0.09375
- momentum: float32 [4096, 24576], P('replica', 'fsdp'), may hold values from -0.09375 to 0.09375
Outputs:
- new_anchor: float32 [4096, 24576], P('replica', 'fsdp')
- new_momentum: float32 [4096, 24576], P('replica', 'fsdp')
- hidden: bfloat16 [4, 1536, 24576], P('replica', None, 'fsdp')
All inputs are finite; a program needn't handle non-finite values.
Results may differ from a plain program's by a relative error of at most 0.015.
Values may be sent and summed in bfloat16 or wider, within the bound.
No kernel may reach another device: no remote copies, remote signals or barrier semaphores. Data moves between devices by JAX's collectives and lax.ppermute only.
A program may use at most 128 MiB of HBM per device.

v0:
```python
import jax
import jax.numpy as jnp
from jax import lax
from jax.sharding import PartitionSpec as P


def per_device(tokens, gate_weight, pseudo_grad, anchor, momentum):
    groups = lax.axis_size("replica")
    gathered = lax.all_gather(tokens[0], "fsdp", axis=0, tiled=True)
    gate = jnp.dot(gathered, gate_weight, preferred_element_type=jnp.float32)
    summed = lax.psum_scatter(
        pseudo_grad[0].astype(jnp.float32).astype(jnp.bfloat16),
        "replica",
        scatter_dimension=0,
        tiled=True,
    ).astype(jnp.float32)
    mean_delta = summed / groups
    new_momentum = 0.9 * momentum + mean_delta
    new_anchor = anchor - 0.7 * (mean_delta + 0.9 * new_momentum)
    up_weight = lax.all_gather(new_anchor.astype(jnp.bfloat16), "replica", axis=0, tiled=True)
    up_part = jnp.dot(gathered, up_weight, preferred_element_type=jnp.float32)
    hidden = (jax.nn.silu(gate) * up_part).astype(jnp.bfloat16)
    return (new_anchor, new_momentum, hidden[None])


def solution(mesh):
    return jax.shard_map(
        per_device,
        mesh=mesh,
        in_specs=(
            P("replica", "fsdp", None),
            P(None, "fsdp"),
            P("replica", None, "fsdp"),
            P("replica", "fsdp"),
            P("replica", "fsdp"),
        ),
        out_specs=(P("replica", "fsdp"), P("replica", "fsdp"), P("replica", None, "fsdp")),
        check_vma=False,
    )
```

profile of v0, /device:TPU:1, one launch (start us, length us, event | category | flops | bytes accessed | tf_op | source)
XLA Modules:
  0.0 1401.4 jit_solution(15654228841941485066)
XLA Ops:
  8.0 0.0 copy-start
  8.0 0.0 reduce-scatter.2.cloned.1.call-start
  8.1 0.7 reduce-scatter.2.cloned.1.call-update
  8.7 0.0 all-gather.6.cloned.1.call-start
  8.8 0.5 all-gather.6.cloned.1.call-update
  9.3 0.0 all-gather.4.cloned.1.call-start
  9.4 67.8 %reduce-scatter.2.cloned.1.call-done = bf16[1024,128]{1,0:T(8,128)(2,1)} async-done(((bf16[4096,128]{1,0:T(8,128)(2,1)}), bf16[1024,128]{1,0:T(8,128)(2,1)}) %reduce-scatter.2.cloned.1.call-update) | async-done | bytes 262160 | tf_op jit(solution)/shard_map/reduce_scatter | solution.py:11
  77.2 2.5 fusion.16
  79.6 0.0 all-gather.4.cloned.1.call-update
  79.7 1119.9 %all-gather.6.cloned.1.call-done = bf16[1,1536,4096]{2,1,0:T(8,128)(2,1)} async-done(((bf16[1,8,4096]{2,1,0:T(8,128)(2,1)}), bf16[1,1536,4096]{2,1,0:T(8,128)(2,1)}) %all-gather.6.cloned.1.call-update) | async-done | bytes 12582928 | tf_op jit(solution)/shard_map/all_gather | solution.py:9
  1199.6 0.0 copy-done
  1199.6 6.4 fusion.2
  1206.0 179.0 %all-gather.4.cloned.1.call-done = bf16[4096,128]{1,0:T(8,128)(2,1)} async-done(((bf16[1024,128]{1,0:T(8,128)(2,1)}), bf16[4096,128]{1,0:T(8,128)(2,1)}) %all-gather.4.cloned.1.call-update) | async-done | bytes 1048592 | tf_op jit(solution)/shard_map/all_gather | solution.py:20
  1385.0 9.0 fusion.13
Async XLA Ops:
  8.0 1191.6 %copy-start = (bf16[4096,128]{1,0:T(8,128)(2,1)S(1)}, bf16[4096,128]{1,0:T(8,128)(2,1)}, u32[]{:S(2)}) copy-start(bf16[4096,128]{1,0:T(8,128)(2,1)} %param.6) | copy-start | bytes 3145732
  8.0 69.2 %reduce-scatter.2.cloned.1.call-start = ((), (), s32[]{:S(2)}) async-start(), calls=%async_computation.1 | async-start | bytes 1310720 | tf_op jit(solution)/shard_map/reduce_scatter | solution.py:11
  8.7 1190.8 %all-gather.6.cloned.1.call-start = ((), (), s32[]{:S(2)}) async-start(), calls=%async_computation.3 | async-start | bytes 12648448 | tf_op jit(solution)/shard_map/all_gather | solution.py:9
  9.3 1375.6 %all-gather.4.cloned.1.call-start = ((), (), s32[]{:S(2)}) async-start(), calls=%async_computation.2 | async-start | bytes 1310720 | tf_op jit(solution)/shard_map/all_gather | solution.py:20
Sparse Core Ops, SparseCore 0:
  12.2 64.9 reduce-scatter.1
Sparse Core Ops, SparseCore 1:
  11.9 1187.6 all-gather.5
  1202.7 182.2 all-gather.3
where the time goes:
time: 1400 us
  waiting for transfers between devices  1370 us (98%)
  between operations  15.5 us (1%)
  matrix products  15.4 us (1%)
    all_gather x1, waiting for transfers between devices, per_device(): gathered = lax.all_gather(tokens[0], 'fsdp', axis=0, tiled=True)  1120 us
    all_gather x1, waiting for transfers between devices, per_device(): lax.all_gather(new_anchor.astype(jnp.bfloat16), 'replica', axis=0, tiled=...  179 us
    reduce_scatter x1, waiting for transfers between devices, per_device(): lax.psum_scatter(pseudo_grad[0].astype(jnp.float32).astype(jnp.bfloat16),...  67.8 us
  transfers between devices with their start and end apart: 3, of which 3 were waited for; matrix products, arithmetic and copies ran while one was open for 1% of the time, Pallas kernels for 0%

commit v1 on v0

v1 whole, which is shorter than its diff:
```python
import jax
import jax.numpy as jnp
from jax import lax
from jax.sharding import Mesh, PartitionSpec as P

ZH, C, Z, X, Y = 2, 2, 6, 4, 8
AXES = ("zh", "c", "z", "x", "y")
BF, F32 = jnp.bfloat16, jnp.float32


def send(value, move, axis):
    sizes = dict(zip(AXES, (ZH, C, Z, X, Y)))
    return lax.ppermute(value, axis, [(i, move(i)) for i in range(sizes[axis])])


def shift(value, axis, by):
    size = dict(zip(AXES, (ZH, C, Z, X, Y)))[axis]
    return send(value, lambda i: (i + by) % size, axis)


def flip(value, axis):
    return send(value, lambda i: i ^ 1, axis)


def pick(value, axis, at):
    return lax.dynamic_index_in_dim(value, at, axis, keepdims=False)


def roll_to(value, axis, by):
    n = value.shape[axis]
    return lax.dynamic_slice_in_dim(jnp.concatenate([value, value], axis), (n - by) % n, n, axis)


def per_device(tokens, gate_weight, pseudo_grad, anchor, momentum):
    zh, c = lax.axis_index("zh"), lax.axis_index("c")
    z, x, y = lax.axis_index("z"), lax.axis_index("x"), lax.axis_index("y")

    grad = pseudo_grad.reshape(2, 2, 1024, 128)
    got = flip(pick(grad, 1, 1 - c), "c")
    pair = pick(grad, 1, c).astype(F32) + got.astype(F32)
    mine, other = pick(pair, 0, zh), pick(pair, 0, 1 - zh)
    base = anchor - 0.567 * momentum
    half_done = (base - 0.3325 * mine).astype(BF)
    new_anchor, new_momentum, up_mine, up_other = [], [], [], []
    ups = []
    for part in range(2):
        rows = slice(512 * part, 512 * part + 512)
        out = jnp.stack([half_done[rows], other[rows].astype(BF)])
        back = flip(out, "zh").astype(F32)
        mean_delta = (mine[rows] + back[1]) / 4
        moved = 0.9 * momentum[rows] + mean_delta
        moved_anchor = anchor[rows] - 0.7 * (mean_delta + 0.9 * moved)
        new_momentum.append(moved)
        new_anchor.append(moved_anchor)
        a = moved_anchor.astype(BF)
        b = (back[0] - 0.3325 * other[rows]).astype(BF)
        ups.append(jnp.where(zh == 0, jnp.stack([a, b]), jnp.stack([b, a])))

    tok = tokens[0].reshape(8, 2, 2, 1024)
    own, away = pick(tok, 2, c), flip(pick(tok, 2, 1 - c), "c")
    tok = jnp.where(c == 0, jnp.stack([own, away]), jnp.stack([away, own]))
    tok = tok.reshape(16, 2048)
    beside = send(tok, lambda i: i ^ 1, "z")
    two = jnp.where(z % 2 == 0, jnp.stack([tok, beside]), jnp.stack([beside, tok]))
    three = jnp.stack([two, shift(two, "z", -2), shift(two, "z", 2)])
    six = roll_to(three, 0, z // 2).reshape(96, 2048)
    f1, b1 = shift(six, "y", 1), shift(six, "y", -1)
    f2, b2 = shift(f1, "y", 1), shift(b1, "y", -1)
    f3, b3 = shift(f2, "y", 1), shift(b2, "y", -1)
    f4, b4 = shift(f3[:48], "y", 1), shift(b3[48:], "y", -1)
    rows = jnp.concatenate([six, b1, b2, b3, f4, b4, f3, f2, f1])

    gate_own = pick(gate_weight.reshape(2, 2, 1024, 128), 1, c).reshape(2048, 128)
    gate_all = jnp.concatenate([gate_own] + [shift(gate_own, "x", -j) for j in (1, 2, 3)], axis=1)
    gate = jnp.dot(rows, gate_all, preferred_element_type=F32)

    up = 0.0
    for part in range(2):
        own = ups[part].reshape(1024, 128)
        columns = jnp.concatenate([own] + [shift(own, "x", -j) for j in (1, 2, 3)], axis=1)
        at = rows.reshape(768, 2, 1024)[:, :, 512 * part : 512 * part + 512].reshape(768, 1024)
        up = up + jnp.dot(at, columns, preferred_element_type=F32)

    def whole(partial):
        parts = partial.reshape(48, 2, 8, 512)
        got = flip(pick(parts, 1, 1 - c).astype(BF), "c")
        return pick(parts, 1, c) + got.astype(F32)

    hidden = (jax.nn.silu(whole(gate)) * whole(up)).astype(BF).reshape(384, 512)
    blocks = [hidden[:, 128 * j : 128 * j + 128] for j in range(4)]
    blocks = [blocks[0]] + [shift(blocks[j], "x", j) for j in (1, 2, 3)]
    result = jnp.stack([blocks[0], blocks[3], blocks[2], blocks[1]]).reshape(4, 8, 6, 8, 128)
    result = roll_to(roll_to(result, 0, x), 1, y)
    result = jnp.transpose(result, (2, 0, 1, 3, 4)).reshape(1, 1536, 128)
    return jnp.concatenate(new_anchor), jnp.concatenate(new_momentum), result


def solution(mesh):
    fine = Mesh(mesh.devices.reshape(ZH, C, Z, X, Y), AXES)
    rep, fsdp = ("zh", "c"), ("z", "x", "y")
    return jax.shard_map(
        lambda t, g, p, a, m: per_device(t, g, p[0], a, m),
        mesh=fine,
        in_specs=(P(rep, fsdp, None), P(None, fsdp), P(rep, None, fsdp), P(rep, fsdp), P(rep, fsdp)),
        out_specs=(P(rep, fsdp), P(rep, fsdp), P(rep, None, fsdp)),
        check_vma=False,
    )
```

time: 1400 us -> 206 us (0.15)
  waiting for transfers between devices: 1370 us -> 39.4 us
  starting transfers between devices: 0.12 us -> 108 us
  local copies, waits for them, and re-layouts: 0.01 us -> 37.4 us
    all_gather x2 -> x0, waiting for transfers between devices: 1300 us -> none  [the longest x1 1120 us: per_device(): gathered = lax.all_gather(tokens[0], 'fsdp', axis=0, tiled=True)]
    ppermute x0 -> x29, starting transfers between devices: none -> 108 us  [send(): return lax.ppermute(value, axis, [(i, move(i)) for i in range(sizes[axis])])]
    reduce_scatter x1 -> x0, waiting for transfers between devices: 67.8 us -> none  [per_device(): lax.psum_scatter(pseudo_grad[0].astype(jnp.float32).astype(jnp.bfloat16),...]
    ppermute x0 -> x29, waiting for transfers between devices: none -> 39.4 us  [send(): return lax.ppermute(value, axis, [(i, move(i)) for i in range(sizes[axis])])]
    unnamed x2 -> x52, local copies, waits for them, and re-layouts: 0.01 us -> 20 us
  transfers between devices with their start and end apart: 3 -> 29, of which waited for: 3 -> 11; matrix products, arithmetic and copies ran while one was open for 1% -> 25% of each run, Pallas kernels for 0% -> 0%
where the time goes in v1:
time: 206 us; the launch traced here: 204 us
  starting transfers between devices  108 us (52%)
  waiting for transfers between devices  39.4 us (19%)
  local copies, waits for them, and re-layouts  37.4 us (18%)
  other arithmetic  10.6 us (5%)
  matrix products  7.25 us (4%)
    ppermute x29, starting transfers between devices, send(): return lax.ppermute(value, axis, [(i, move(i)) for i in range(sizes[axis])])  108 us
    ppermute x29, waiting for transfers between devices, send(): return lax.ppermute(value, axis, [(i, move(i)) for i in range(sizes[axis])])  39.4 us
    unnamed x52, local copies, waits for them, and re-layouts  20 us
    concatenate x11, local copies, waits for them, and re-layouts, per_device(): rows = jnp.concatenate([six, b1, b2, b3, f4, b4, f3, f2, f1])  9.79 us
    dot_general x1, matrix products, per_device(): gate = jnp.dot(rows, gate_all, preferred_element_type=F32)  4.25 us
  transfers between devices with their start and end apart: 29, of which 11 were waited for; matrix products, arithmetic and copies ran while one was open for 25% of the time, Pallas kernels for 0%

profile of v1, /device:TPU:1, one launch (start us, length us, event | category | flops | bytes accessed | tf_op | source)
XLA Modules:
  0.0 204.5 jit_solution(2364270852253777699)
XLA Ops:
  1.5 12.4 %collective-permute-start.3 = (bf16[8,2,1024]{2,0,1:T(8,128)(2,1)S(1)}, bf16[8,2,1024]{2,0,1:T(8,128)(2,1)S(1)}, u32[]{:S(2)}, u32[]{:S(2)}) collective-permute-start(bf16[8,2,1024]{2,0,1:T(8,128)(2,1)S(1)} %get-tuple-element.25), channel_id=1, source_target_pairs={{0,192},{192,0},{1,193},{193,1},{2,194},{194,2},{3,195},{195,3},{4... | collective-permute-start | bytes 98312 | tf_op jit(solution)/shard_map/ppermute | solution.py:13
  24.4 6.8 %collective-permute-start.5 = (bf16[2,16,2048]{2,1,0:T(8,128)(2,1)S(1)}, bf16[2,16,2048]{2,1,0:T(8,128)(2,1)S(1)}, u32[]{:S(2)}, u32[]{:S(2)}) collective-permute-start(bf16[2,16,2048]{2,1,0:T(8,128)(2,1)S(1)} %maximum_select_fusion.3), channel_id=1, source_target_pairs={{0,128},{32,160},{64,0},{96,32},{128,64},{160,96},{1,129},{33,161}... | collective-permute-start | bytes 393224 | tf_op jit(solution)/shard_map/ppermute | solution.py:13
  34.7 10.1 %collective-permute-done.6 = bf16[2,16,2048]{2,1,0:T(8,128)(2,1)S(1)} collective-permute-done((bf16[2,16,2048]{2,1,0:T(8,128)(2,1)S(1)}, bf16[2,16,2048]{2,1,0:T(8,128)(2,1)S(1)}, u32[]{:S(2)}, u32[]{:S(2)}) %collective-permute-start.6) | collective-permute-done | bytes 131104 | tf_op jit(solution)/shard_map/ppermute | solution.py:13
  44.9 5.1 %collective-permute-start.7 = (bf16[96,2048]{1,0:T(8,128)(2,1)S(1)}, bf16[96,2048]{1,0:T(8,128)(2,1)}, u32[]{:S(2)}, u32[]{:S(2)}) collective-permute-start(bf16[96,2048]{1,0:T(8,128)(2,1)S(1)} %bitcast.101), channel_id=1, source_target_pairs={{0,7},{1,0},{2,1},{3,2},{4,3},{5,4},{6,5},{7,6},{8,15},{9,8},{10,9... | collective-permute-start | bytes 1179656 | tf_op jit(solution)/shard_map/ppermute | solution.py:13
  56.2 10.3 %collective-permute-start.2 = (bf16[2,512,128]{2,1,0:T(8,128)(2,1)}, bf16[2,512,128]{2,1,0:T(8,128)(2,1)}, u32[]{:S(2)}, u32[]{:S(2)}) collective-permute-start(bf16[2,512,128]{2,1,0:T(8,128)(2,1)} %pad_maximum_fusion.3), channel_id=1, source_target_pairs={{0,384},{384,0},{1,385},{385,1},{2,386},{386,2},{3,387},{387,3},{4... | collective-permute-start | bytes 786440 | tf_op jit(solution)/shard_map/ppermute | solution.py:13
  73.2 2.5 %collective-permute-start.17 = (bf16[2048,128]{1,0:T(8,128)(2,1)}, bf16[2048,128]{1,0:T(8,128)(2,1)}, u32[]{:S(2)}, u32[]{:S(2)}) collective-permute-start(bf16[2048,128]{1,0:T(8,128)(2,1)} %bitcast.21), channel_id=1, source_target_pairs={{0,8},{8,16},{16,24},{24,0},{1,9},{9,17},{17,25},{25,1},{2,10},{10... | collective-permute-start | bytes 1572872 | tf_op jit(solution)/shard_map/ppermute | solution.py:13
  78.8 17.0 %collective-permute-done.2 = bf16[2,512,128]{2,1,0:T(8,128)(2,1)} collective-permute-done((bf16[2,512,128]{2,1,0:T(8,128)(2,1)}, bf16[2,512,128]{2,1,0:T(8,128)(2,1)}, u32[]{:S(2)}, u32[]{:S(2)}) %collective-permute-start.2) | collective-permute-done | bytes 262176 | tf_op jit(solution)/shard_map/ppermute | solution.py:13
  95.8 4.5 %collective-permute-start.8 = (bf16[96,2048]{1,0:T(8,128)(2,1)}, bf16[96,2048]{1,0:T(8,128)(2,1)}, u32[]{:S(2)}, u32[]{:S(2)}) collective-permute-start(bf16[96,2048]{1,0:T(8,128)(2,1)} %collective-permute-done.7), channel_id=1, source_target_pairs={{0,7},{1,0},{2,1},{3,2},{4,3},{5,4},{6,5},{7,6},{8,15},{9,8},{10,9... | collective-permute-start | bytes 1179656 | tf_op jit(solution)/shard_map/ppermute | solution.py:13
  107.8 5.3 %collective-permute-start.9 = (bf16[96,2048]{1,0:T(8,128)(2,1)}, bf16[96,2048]{1,0:T(8,128)(2,1)S(1)}, u32[]{:S(2)}, u32[]{:S(2)}) collective-permute-start(bf16[96,2048]{1,0:T(8,128)(2,1)} %collective-permute-done.8), channel_id=1, source_target_pairs={{0,7},{1,0},{2,1},{3,2},{4,3},{5,4},{6,5},{7,6},{8,15},{9,8},{10,9... | collective-permute-start | bytes 1179656 | tf_op jit(solution)/shard_map/ppermute | solution.py:13
  122.0 3.5 %collective-permute-done.12 = bf16[96,2048]{1,0:T(8,128)(2,1)S(1)} collective-permute-done((bf16[96,2048]{1,0:T(8,128)(2,1)}, bf16[96,2048]{1,0:T(8,128)(2,1)S(1)}, u32[]{:S(2)}, u32[]{:S(2)}) %collective-permute-start.12) | collective-permute-done | bytes 393248 | tf_op jit(solution)/shard_map/ppermute | solution.py:13
  128.9 4.6 %collective-permute-start.14 = (bf16[48,2048]{1,0:T(8,128)(2,1)}, bf16[48,2048]{1,0:T(8,128)(2,1)S(1)}, u32[]{:S(2)}, u32[]{:S(2)}) collective-permute-start(bf16[48,2048]{1,0:T(8,128)(2,1)} %slice.99), channel_id=1, source_target_pairs={{0,7},{1,0},{2,1},{3,2},{4,3},{5,4},{6,5},{7,6},{8,15},{9,8},{10,9... | collective-permute-start | bytes 589832 | tf_op jit(solution)/shard_map/ppermute | solution.py:13
  135.9 2.2 %collective-permute-start.22 = (bf16[1024,128]{1,0:T(8,128)(2,1)}, bf16[1024,128]{1,0:T(8,128)(2,1)}, u32[]{:S(2)}, u32[]{:S(2)}) collective-permute-start(bf16[1024,128]{1,0:T(8,128)(2,1)} %bitcast.128), channel_id=1, source_target_pairs={{0,24},{8,0},{16,8},{24,16},{1,25},{9,1},{17,9},{25,17},{2,26},{10... | collective-permute-start | bytes 786440 | tf_op jit(solution)/shard_map/ppermute | solution.py:13
  139.1 4.0 %collective-permute-start.23 = (bf16[1024,128]{1,0:T(8,128)(2,1)}, bf16[1024,128]{1,0:T(8,128)(2,1)}, u32[]{:S(2)}, u32[]{:S(2)}) collective-permute-start(bf16[1024,128]{1,0:T(8,128)(2,1)} %bitcast.129), channel_id=1, source_target_pairs={{0,16},{8,24},{16,0},{24,8},{1,17},{9,25},{17,1},{25,9},{2,18},{10... | collective-permute-start | bytes 786440 | tf_op jit(solution)/shard_map/ppermute | solution.py:13
  152.9 2.7 %collective-permute-start.24 = (bf16[1024,128]{1,0:T(8,128)(2,1)}, bf16[1024,128]{1,0:T(8,128)(2,1)S(1)}, u32[]{:S(2)}, u32[]{:S(2)}) collective-permute-start(bf16[1024,128]{1,0:T(8,128)(2,1)} %bitcast.130), channel_id=1, source_target_pairs={{0,8},{8,16},{16,24},{24,0},{1,9},{9,17},{17,25},{25,1},{2,10},{10... | collective-permute-start | bytes 786440 | tf_op jit(solution)/shard_map/ppermute | solution.py:13
  155.6 4.0 %collective-permute-start.19 = (bf16[1024,128]{1,0:T(8,128)(2,1)}, bf16[1024,128]{1,0:T(8,128)(2,1)S(1)}, u32[]{:S(2)}, u32[]{:S(2)}) collective-permute-start(bf16[1024,128]{1,0:T(8,128)(2,1)} %bitcast.132), channel_id=1, source_target_pairs={{0,24},{8,0},{16,8},{24,16},{1,25},{9,1},{17,9},{25,17},{2,26},{10... | collective-permute-start | bytes 786440 | tf_op jit(solution)/shard_map/ppermute | solution.py:13
  161.6 4.2 %fusion = f32[768,512]{1,0:T(8,128)S(1)} fusion(bf16[768,2048]{1,0:T(8,128)(2,1)} %constant_dynamic-update-slice_fusion.2, bf16[2048,128]{1,0:T(8,128)(2,1)} %collective-permute-done.17, bf16[2048,128]{1,0:T(8,128)(2,1)} %collective-permute-done.16, bf16[2048,128]{1,0:T(8,128)(2,1)} %collective-permute-done.15, bf16[2048,128]{1,0:T(8,128)(2,1)} %bitcast.21), kind=kOutput, calls=%fused_computation | convolution fusion | flops 1619001344 | bytes 6815744 | tf_op jit(solution)/shard_map/dot_general | solution.py:75
  165.9 2.2 %fusion.40 = (bf16[768,2,512]{2,1,0:T(2,128)(2,1)S(1)}, bf16[768,2,512]{2,1,0:T(2,128)(2,1)S(1)}) fusion(bf16[768,2,1024]{2,1,0:T(2,128)(2,1)S(1)} %copy-done.1), kind=kLoop, calls=%fused_computation.110 | loop fusion | bytes 6291456 | tf_op jit(solution)/shard_map/slice | solution.py:81
  169.1 2.7 %collective-permute-start.21 = (bf16[1024,128]{1,0:T(8,128)(2,1)S(1)}, bf16[1024,128]{1,0:T(8,128)(2,1)S(1)}, u32[]{:S(2)}, u32[]{:S(2)}) collective-permute-start(bf16[1024,128]{1,0:T(8,128)(2,1)S(1)} %bitcast.134), channel_id=1, source_target_pairs={{0,8},{8,16},{16,24},{24,0},{1,9},{9,17},{17,25},{25,1},{2,10},{10... | collective-permute-start | bytes 786440 | tf_op jit(solution)/shard_map/ppermute | solution.py:13
  171.7 7.6 %collective-permute-start.18 = (bf16[48,8,512]{2,1,0:T(8,128)(2,1)S(1)}, bf16[48,8,512]{2,1,0:T(8,128)(2,1)S(1)}, u32[]{:S(2)}, u32[]{:S(2)}) collective-permute-start(bf16[48,8,512]{2,1,0:T(8,128)(2,1)S(1)} %fusion.26), channel_id=1, source_target_pairs={{0,192},{192,0},{1,193},{193,1},{2,194},{194,2},{3,195},{195,3},{4... | collective-permute-start | bytes 1179656 | tf_op jit(solution)/shard_map/ppermute | solution.py:13
  183.7 4.1 %collective-permute-start.25 = (bf16[48,8,512]{2,1,0:T(8,128)(2,1)S(1)}, bf16[48,8,512]{2,1,0:T(8,128)(2,1)}, u32[]{:S(2)}, u32[]{:S(2)}) collective-permute-start(bf16[48,8,512]{2,1,0:T(8,128)(2,1)S(1)} %fusion.27), channel_id=1, source_target_pairs={{0,192},{192,0},{1,193},{193,1},{2,194},{194,2},{3,195},{195,3},{4... | collective-permute-start | bytes 1179656 | tf_op jit(solution)/shard_map/ppermute | solution.py:13
  191.0 2.9 %collective-permute-start.26 = (bf16[384,128]{1,0:T(8,128)(2,1)S(1)}, bf16[384,128]{1,0:T(8,128)(2,1)S(1)}, u32[]{:S(2)}, u32[]{:S(2)}) collective-permute-start(bf16[384,128]{1,0:T(8,128)(2,1)S(1)} %get-tuple-element.20), channel_id=1, source_target_pairs={{0,24},{8,0},{16,8},{24,16},{1,25},{9,1},{17,9},{25,17},{2,26},{10... | collective-permute-start | bytes 294920 | tf_op jit(solution)/shard_map/ppermute | solution.py:13
  193.9 2.8 %collective-permute-start.27 = (bf16[384,128]{1,0:T(8,128)(2,1)S(1)}, bf16[384,128]{1,0:T(8,128)(2,1)S(1)}, u32[]{:S(2)}, u32[]{:S(2)}) collective-permute-start(bf16[384,128]{1,0:T(8,128)(2,1)S(1)} %get-tuple-element.19), channel_id=1, source_target_pairs={{0,16},{8,24},{16,0},{24,8},{1,17},{9,25},{17,1},{25,9},{2,18},{10... | collective-permute-start | bytes 294920 | tf_op jit(solution)/shard_map/ppermute | solution.py:13
  196.7 2.8 %collective-permute-start.28 = (bf16[384,128]{1,0:T(8,128)(2,1)S(1)}, bf16[384,128]{1,0:T(8,128)(2,1)S(1)}, u32[]{:S(2)}, u32[]{:S(2)}) collective-permute-start(bf16[384,128]{1,0:T(8,128)(2,1)S(1)} %get-tuple-element.18), channel_id=1, source_target_pairs={{0,8},{8,16},{16,24},{24,0},{1,9},{9,17},{17,25},{25,1},{2,10},{10... | collective-permute-start | bytes 294920 | tf_op jit(solution)/shard_map/ppermute | solution.py:13
  200.8 2.5 %collective-permute-done.28 = bf16[384,128]{1,0:T(8,128)(2,1)S(1)} collective-permute-done((bf16[384,128]{1,0:T(8,128)(2,1)S(1)}, bf16[384,128]{1,0:T(8,128)(2,1)S(1)}, u32[]{:S(2)}, u32[]{:S(2)}) %collective-permute-start.28) | collective-permute-done | bytes 98336 | tf_op jit(solution)/shard_map/ppermute | solution.py:13
  (133 shorter events, 76.2 us)
Async XLA Ops:
  1.5 17.1 %collective-permute-start.3 = (bf16[8,2,1024]{2,0,1:T(8,128)(2,1)S(1)}, bf16[8,2,1024]{2,0,1:T(8,128)(2,1)S(1)}, u32[]{:S(2)}, u32[]{:S(2)}) collective-permute-start(bf16[8,2,1024]{2,0,1:T(8,128)(2,1)S(1)} %get-tuple-element.25), channel_id=1, source_target_pairs={{0,192},{192,0},{1,193},{193,1},{2,194},{194,2},{3,195},{195,3},{4... | collective-permute-start | bytes 98312 | tf_op jit(solution)/shard_map/ppermute | solution.py:13
  14.8 138.1 %collective-permute-start.15 = (bf16[2048,128]{1,0:T(8,128)(2,1)}, bf16[2048,128]{1,0:T(8,128)(2,1)}, u32[]{:S(2)}, u32[]{:S(2)}) collective-permute-start(bf16[2048,128]{1,0:T(8,128)(2,1)} %bitcast.21), channel_id=1, source_target_pairs={{0,24},{8,0},{16,8},{24,16},{1,25},{9,1},{17,9},{25,17},{2,26},{10... | collective-permute-start | bytes 1572872 | tf_op jit(solution)/shard_map/ppermute | solution.py:13
  16.7 138.9 %collective-permute-start.16 = (bf16[2048,128]{1,0:T(8,128)(2,1)}, bf16[2048,128]{1,0:T(8,128)(2,1)}, u32[]{:S(2)}, u32[]{:S(2)}) collective-permute-start(bf16[2048,128]{1,0:T(8,128)(2,1)} %bitcast.21), channel_id=1, source_target_pairs={{0,16},{8,24},{16,0},{24,8},{1,17},{9,25},{17,1},{25,9},{2,18},{10... | collective-permute-start | bytes 1572872 | tf_op jit(solution)/shard_map/ppermute | solution.py:13
  21.7 32.3 %collective-permute-start = (bf16[2,1024,128]{2,1,0:T(8,128)(2,1)S(1)}, bf16[2,1024,128]{2,1,0:T(8,128)(2,1)}, u32[]{:S(2)}, u32[]{:S(2)}) collective-permute-start(bf16[2,1024,128]{2,1,0:T(8,128)(2,1)S(1)} %dynamic-slice_bitcast_fusion), channel_id=1, source_target_pairs={{0,192},{192,0},{1,193},{193,1},{2,194},{194,2},{3,195},{195,3},{4... | collective-permute-start | bytes 1572872 | tf_op jit(solution)/shard_map/ppermute | solution.py:13
  24.4 10.2 %collective-permute-start.5 = (bf16[2,16,2048]{2,1,0:T(8,128)(2,1)S(1)}, bf16[2,16,2048]{2,1,0:T(8,128)(2,1)S(1)}, u32[]{:S(2)}, u32[]{:S(2)}) collective-permute-start(bf16[2,16,2048]{2,1,0:T(8,128)(2,1)S(1)} %maximum_select_fusion.3), channel_id=1, source_target_pairs={{0,128},{32,160},{64,0},{96,32},{128,64},{160,96},{1,129},{33,161}... | collective-permute-start | bytes 393224 | tf_op jit(solution)/shard_map/ppermute | solution.py:13
  31.2 13.5 %collective-permute-start.6 = (bf16[2,16,2048]{2,1,0:T(8,128)(2,1)S(1)}, bf16[2,16,2048]{2,1,0:T(8,128)(2,1)S(1)}, u32[]{:S(2)}, u32[]{:S(2)}) collective-permute-start(bf16[2,16,2048]{2,1,0:T(8,128)(2,1)S(1)} %maximum_select_fusion.3), channel_id=1, source_target_pairs={{0,64},{32,96},{64,128},{96,160},{128,0},{160,32},{1,65},{33,97},{... | collective-permute-start | bytes 393224 | tf_op jit(solution)/shard_map/ppermute | solution.py:13
  44.9 22.4 %collective-permute-start.7 = (bf16[96,2048]{1,0:T(8,128)(2,1)S(1)}, bf16[96,2048]{1,0:T(8,128)(2,1)}, u32[]{:S(2)}, u32[]{:S(2)}) collective-permute-start(bf16[96,2048]{1,0:T(8,128)(2,1)S(1)} %bitcast.101), channel_id=1, source_target_pairs={{0,7},{1,0},{2,1},{3,2},{4,3},{5,4},{6,5},{7,6},{8,15},{9,8},{10,9... | collective-permute-start | bytes 1179656 | tf_op jit(solution)/shard_map/ppermute | solution.py:13
  50.0 23.2 %collective-permute-start.10 = (bf16[96,2048]{1,0:T(8,128)(2,1)S(1)}, bf16[96,2048]{1,0:T(8,128)(2,1)}, u32[]{:S(2)}, u32[]{:S(2)}) collective-permute-start(bf16[96,2048]{1,0:T(8,128)(2,1)S(1)} %bitcast.102), channel_id=1, source_target_pairs={{0,1},{1,2},{2,3},{3,4},{4,5},{5,6},{6,7},{7,0},{8,9},{9,10},{10,1... | collective-permute-start | bytes 1179656 | tf_op jit(solution)/shard_map/ppermute | solution.py:13
  56.2 39.6 %collective-permute-start.2 = (bf16[2,512,128]{2,1,0:T(8,128)(2,1)}, bf16[2,512,128]{2,1,0:T(8,128)(2,1)}, u32[]{:S(2)}, u32[]{:S(2)}) collective-permute-start(bf16[2,512,128]{2,1,0:T(8,128)(2,1)} %pad_maximum_fusion.3), channel_id=1, source_target_pairs={{0,384},{384,0},{1,385},{385,1},{2,386},{386,2},{3,387},{387,3},{4... | collective-permute-start | bytes 786440 | tf_op jit(solution)/shard_map/ppermute | solution.py:13
  67.3 34.1 %collective-permute-start.1 = (bf16[2,512,128]{2,1,0:T(8,128)(2,1)}, bf16[2,512,128]{2,1,0:T(8,128)(2,1)}, u32[]{:S(2)}, u32[]{:S(2)}) collective-permute-start(bf16[2,512,128]{2,1,0:T(8,128)(2,1)} %pad_maximum_fusion.2), channel_id=1, source_target_pairs={{0,384},{384,0},{1,385},{385,1},{2,386},{386,2},{3,387},{387,3},{4... | collective-permute-start | bytes 786440 | tf_op jit(solution)/shard_map/ppermute | solution.py:13
  73.2 86.4 %collective-permute-start.17 = (bf16[2048,128]{1,0:T(8,128)(2,1)}, bf16[2048,128]{1,0:T(8,128)(2,1)}, u32[]{:S(2)}, u32[]{:S(2)}) collective-permute-start(bf16[2048,128]{1,0:T(8,128)(2,1)} %bitcast.21), channel_id=1, source_target_pairs={{0,8},{8,16},{16,24},{24,0},{1,9},{9,17},{17,25},{25,1},{2,10},{10... | collective-permute-start | bytes 1572872 | tf_op jit(solution)/shard_map/ppermute | solution.py:13
  95.8 12.0 %collective-permute-start.8 = (bf16[96,2048]{1,0:T(8,128)(2,1)}, bf16[96,2048]{1,0:T(8,128)(2,1)}, u32[]{:S(2)}, u32[]{:S(2)}) collective-permute-start(bf16[96,2048]{1,0:T(8,128)(2,1)} %collective-permute-done.7), channel_id=1, source_target_pairs={{0,7},{1,0},{2,1},{3,2},{4,3},{5,4},{6,5},{7,6},{8,15},{9,8},{10,9... | collective-permute-start | bytes 1179656 | tf_op jit(solution)/shard_map/ppermute | solution.py:13
  101.4 12.6 %collective-permute-start.11 = (bf16[96,2048]{1,0:T(8,128)(2,1)}, bf16[96,2048]{1,0:T(8,128)(2,1)}, u32[]{:S(2)}, u32[]{:S(2)}) collective-permute-start(bf16[96,2048]{1,0:T(8,128)(2,1)} %collective-permute-done.10), channel_id=1, source_target_pairs={{0,1},{1,2},{2,3},{3,4},{4,5},{5,6},{6,7},{7,0},{8,9},{9,10},{10,1... | collective-permute-start | bytes 1179656 | tf_op jit(solution)/shard_map/ppermute | solution.py:13
  107.8 20.4 %collective-permute-start.9 = (bf16[96,2048]{1,0:T(8,128)(2,1)}, bf16[96,2048]{1,0:T(8,128)(2,1)S(1)}, u32[]{:S(2)}, u32[]{:S(2)}) collective-permute-start(bf16[96,2048]{1,0:T(8,128)(2,1)} %collective-permute-done.8), channel_id=1, source_target_pairs={{0,7},{1,0},{2,1},{3,2},{4,3},{5,4},{6,5},{7,6},{8,15},{9,8},{10,9... | collective-permute-start | bytes 1179656 | tf_op jit(solution)/shard_map/ppermute | solution.py:13
  114.0 11.6 %collective-permute-start.12 = (bf16[96,2048]{1,0:T(8,128)(2,1)}, bf16[96,2048]{1,0:T(8,128)(2,1)S(1)}, u32[]{:S(2)}, u32[]{:S(2)}) collective-permute-start(bf16[96,2048]{1,0:T(8,128)(2,1)} %collective-permute-done.11), channel_id=1, source_target_pairs={{0,1},{1,2},{2,3},{3,4},{4,5},{5,6},{6,7},{7,0},{8,9},{9,10},{10,1... | collective-permute-start | bytes 1179656 | tf_op jit(solution)/shard_map/ppermute | solution.py:13
  126.2 9.6 %collective-permute-start.13 = (bf16[48,2048]{1,0:T(8,128)(2,1)}, bf16[48,2048]{1,0:T(8,128)(2,1)S(1)}, u32[]{:S(2)}, u32[]{:S(2)}) collective-permute-start(bf16[48,2048]{1,0:T(8,128)(2,1)} %slice.98), channel_id=1, source_target_pairs={{0,1},{1,2},{2,3},{3,4},{4,5},{5,6},{6,7},{7,0},{8,9},{9,10},{10,1... | collective-permute-start | bytes 589832 | tf_op jit(solution)/shard_map/ppermute | solution.py:13
  128.9 10.2 %collective-permute-start.14 = (bf16[48,2048]{1,0:T(8,128)(2,1)}, bf16[48,2048]{1,0:T(8,128)(2,1)S(1)}, u32[]{:S(2)}, u32[]{:S(2)}) collective-permute-start(bf16[48,2048]{1,0:T(8,128)(2,1)} %slice.99), channel_id=1, source_target_pairs={{0,7},{1,0},{2,1},{3,2},{4,3},{5,4},{6,5},{7,6},{8,15},{9,8},{10,9... | collective-permute-start | bytes 589832 | tf_op jit(solution)/shard_map/ppermute | solution.py:13
  135.9 33.2 %collective-permute-start.22 = (bf16[1024,128]{1,0:T(8,128)(2,1)}, bf16[1024,128]{1,0:T(8,128)(2,1)}, u32[]{:S(2)}, u32[]{:S(2)}) collective-permute-start(bf16[1024,128]{1,0:T(8,128)(2,1)} %bitcast.128), channel_id=1, source_target_pairs={{0,24},{8,0},{16,8},{24,16},{1,25},{9,1},{17,9},{25,17},{2,26},{10... | collective-permute-start | bytes 786440 | tf_op jit(solution)/shard_map/ppermute | solution.py:13
  139.1 32.6 %collective-permute-start.23 = (bf16[1024,128]{1,0:T(8,128)(2,1)}, bf16[1024,128]{1,0:T(8,128)(2,1)}, u32[]{:S(2)}, u32[]{:S(2)}) collective-permute-start(bf16[1024,128]{1,0:T(8,128)(2,1)} %bitcast.129), channel_id=1, source_target_pairs={{0,16},{8,24},{16,0},{24,8},{1,17},{9,25},{17,1},{25,9},{2,18},{10... | collective-permute-start | bytes 786440 | tf_op jit(solution)/shard_map/ppermute | solution.py:13
  152.9 26.5 %collective-permute-start.24 = (bf16[1024,128]{1,0:T(8,128)(2,1)}, bf16[1024,128]{1,0:T(8,128)(2,1)S(1)}, u32[]{:S(2)}, u32[]{:S(2)}) collective-permute-start(bf16[1024,128]{1,0:T(8,128)(2,1)} %bitcast.130), channel_id=1, source_target_pairs={{0,8},{8,16},{16,24},{24,0},{1,9},{9,17},{17,25},{25,1},{2,10},{10... | collective-permute-start | bytes 786440 | tf_op jit(solution)/shard_map/ppermute | solution.py:13
  155.6 25.7 %collective-permute-start.19 = (bf16[1024,128]{1,0:T(8,128)(2,1)}, bf16[1024,128]{1,0:T(8,128)(2,1)S(1)}, u32[]{:S(2)}, u32[]{:S(2)}) collective-permute-start(bf16[1024,128]{1,0:T(8,128)(2,1)} %bitcast.132), channel_id=1, source_target_pairs={{0,24},{8,0},{16,8},{24,16},{1,25},{9,1},{17,9},{25,17},{2,26},{10... | collective-permute-start | bytes 786440 | tf_op jit(solution)/shard_map/ppermute | solution.py:13
  159.7 21.7 %collective-permute-start.20 = (bf16[1024,128]{1,0:T(8,128)(2,1)}, bf16[1024,128]{1,0:T(8,128)(2,1)S(1)}, u32[]{:S(2)}, u32[]{:S(2)}) collective-permute-start(bf16[1024,128]{1,0:T(8,128)(2,1)} %bitcast.133), channel_id=1, source_target_pairs={{0,16},{8,24},{16,0},{24,8},{1,17},{9,25},{17,1},{25,9},{2,18},{10... | collective-permute-start | bytes 786440 | tf_op jit(solution)/shard_map/ppermute | solution.py:13
  169.1 12.4 %collective-permute-start.21 = (bf16[1024,128]{1,0:T(8,128)(2,1)S(1)}, bf16[1024,128]{1,0:T(8,128)(2,1)S(1)}, u32[]{:S(2)}, u32[]{:S(2)}) collective-permute-start(bf16[1024,128]{1,0:T(8,128)(2,1)S(1)} %bitcast.134), channel_id=1, source_target_pairs={{0,8},{8,16},{16,24},{24,0},{1,9},{9,17},{17,25},{25,1},{2,10},{10... | collective-permute-start | bytes 786440 | tf_op jit(solution)/shard_map/ppermute | solution.py:13
  171.7 17.1 %collective-permute-start.18 = (bf16[48,8,512]{2,1,0:T(8,128)(2,1)S(1)}, bf16[48,8,512]{2,1,0:T(8,128)(2,1)S(1)}, u32[]{:S(2)}, u32[]{:S(2)}) collective-permute-start(bf16[48,8,512]{2,1,0:T(8,128)(2,1)S(1)} %fusion.26), channel_id=1, source_target_pairs={{0,192},{192,0},{1,193},{193,1},{2,194},{194,2},{3,195},{195,3},{4... | collective-permute-start | bytes 1179656 | tf_op jit(solution)/shard_map/ppermute | solution.py:13
  (17 other events, 139.7 us)

commit v2 on v0

v2 whole, which is shorter than its diff:
```python
import functools

import jax
import jax.numpy as jnp
from jax import lax
from jax.experimental import pallas as pl
from jax.experimental.pallas import tpu as pltpu
from jax.sharding import Mesh, PartitionSpec as P

SIZES = {"zh": 2, "c": 2, "z": 6, "x": 4, "y": 8}
AXES = tuple(SIZES)
BF, F32 = jnp.bfloat16, jnp.float32
MIB = 1024 * 1024


def shift(value, axis, by):
    n = SIZES[axis]
    return lax.ppermute(value, axis, [(i, (i + by) % n) for i in range(n)])


def flip(value, axis):
    return lax.ppermute(value, axis, [(0, 1), (1, 0)])


def after(value, *others):
    return lax.optimization_barrier((value, *others))[0]


def whole(a):
    return pl.BlockSpec(a.shape, lambda i, at: (0,) * len(a.shape))


def call(body, scalars, arrays, outs, room=60):
    return pl.pallas_call(
        body,
        out_shape=outs,
        grid_spec=pltpu.PrefetchScalarGridSpec(
            num_scalar_prefetch=1,
            grid=(1,),
            in_specs=[whole(a) for a in arrays],
            out_specs=[whole(o) for o in outs],
        ),
        compiler_params=pltpu.CompilerParams(vmem_limit_bytes=room * MIB),
        cost_estimate=pl.CostEstimate(flops=0, bytes_accessed=1024, transcendentals=0),
    )(jnp.stack(scalars).astype(jnp.int32), *arrays)


def like(shape, dtype):
    return jax.ShapeDtypeStruct(shape, dtype)


def prepare_body(at, grad, got, anchor, momentum, out, half_done, mine, other):
    zh, c = at[0], at[1]
    s = grad[zh, c].astype(F32) + got[zh].astype(F32)
    o = grad[1 - zh, c].astype(F32) + got[1 - zh].astype(F32)
    v = (anchor[...] - 0.567 * momentum[...]) - 0.3325 * s
    mine[...] = s
    other[...] = o
    half_done[...] = v
    out[0] = v.astype(BF)
    out[1] = o.astype(BF)


def update_body(at, back, half_done, other, up):
    zh = at[0]
    up[zh] = (half_done[...] - 0.3325 * back[1].astype(F32)).astype(BF)
    up[1 - zh] = (back[0].astype(F32) - 0.3325 * other[...]).astype(BF)


def outer_body(at, mine, back, anchor, momentum, new_anchor, new_momentum):
    mean_delta = (mine[...] + back[1].astype(F32)) * 0.25
    moved = 0.9 * momentum[...] + mean_delta
    new_momentum[...] = moved
    new_anchor[...] = anchor[...] - 0.7 * (mean_delta + 0.9 * moved)


def product_body(at, *refs):
    tokens, weights, keep, give = refs[:9], refs[9:13], refs[13], refs[14]
    c, y = at[0], at[1]
    for half in range(2):
        pieces = tokens[:4] if half == 0 else tokens[4:]
        for pair in range(2):
            rows = jnp.concatenate([p[...] for p in pieces], axis=0)
            block = jnp.concatenate([w[...] for w in weights[2 * pair : 2 * pair + 2]], axis=1)
            total = jnp.dot(rows, block, preferred_element_type=F32)
            columns = slice(256 * pair, 256 * pair + 256)
            for s in range(4):
                low, high = total[96 * s : 96 * s + 48], total[96 * s + 48 : 96 * s + 96]
                place = lax.rem(y + 4 * half + s, 8)
                keep[place, :, columns] = jnp.where(c == 0, low, high)
                give[place, :, columns] = jnp.where(c == 0, high, low).astype(BF)


def product(c, y, tokens, weights):
    return call(product_body, [c, y], [*tokens, *weights], [like((8, 48, 512), F32), like((8, 48, 512), BF)])


def gated_body(at, gate, gate_got, up, up_got, hidden):
    x = at[0]
    for j in range(4):
        columns = slice(128 * j, 128 * j + 128)
        g = gate[:, :, columns] + gate_got[:, :, columns].astype(F32)
        u = up[:, :, columns] + up_got[:, :, columns].astype(F32)
        hidden[lax.rem(x + j, 4)] = (g / (1.0 + jnp.exp(-g)) * u).astype(BF)


def per_device(tokens, gate_weight, pseudo_grad, anchor, momentum):
    zh, c = lax.axis_index("zh"), lax.axis_index("c")
    x, y = lax.axis_index("x"), lax.axis_index("y")

    grad = pseudo_grad.reshape(2, 2, 1024, 128)
    pick = lax.dynamic_index_in_dim(grad, 1 - c, 1, keepdims=False)
    got = flip(pick, "c")
    tokens = after(tokens, pick)
    cut = jnp.transpose(tokens[0].reshape(8, 2, 2, 1024), (2, 0, 1, 3)).reshape(2, 1, 8, 2048)
    cut = jnp.broadcast_to(cut, (2, 6, 8, 2048)).reshape(12, 8, 2048)
    six = lax.all_to_all(cut, ("c", "z"), 0, 0).reshape(96, 2048)
    out, half_done, mine, other = call(
        prepare_body,
        [zh, c],
        [grad, got, anchor, momentum],
        [like((2, 1024, 128), BF)] + [like((1024, 128), F32)] * 3,
    )
    back = flip(out, "zh")
    six = after(six, out)
    f1, b1 = shift(six, "y", 1), shift(six, "y", -1)
    f2, b2 = shift(f1, "y", 1), shift(b1, "y", -1)
    (up,) = call(update_body, [zh], [back, half_done, other], [like((2, 1024, 128), BF)])
    ups = [up.reshape(2048, 128)]
    ups += [shift(ups[0], "x", -j) for j in (1, 2, 3)]
    f2, b2 = after(f2, up), after(b2, up)
    f3, b3 = shift(f2, "y", 1), shift(b2, "y", -1)
    own = lax.dynamic_index_in_dim(gate_weight.reshape(2, 2, 1024, 128), c, 1, keepdims=False).reshape(2048, 128)
    gate_blocks = [own] + [shift(own, "x", -j) for j in (1, 2, 3)]
    f3, b3, *gate_blocks = lax.optimization_barrier((f3, b3, *gate_blocks))
    f4, b4 = shift(f3[:48], "y", 1), shift(b3[48:], "y", -1)
    pieces = [six, b1, b2, b3, f4, b4, f3, f2, f1]

    gate, gate_give = product(c, y, pieces, gate_blocks)
    gate_got = flip(gate_give, "c")
    up, up_give = product(c, y, pieces, ups)
    up_got = flip(up_give, "c")

    (hidden,) = call(gated_body, [x], [gate, gate_got, up, up_got], [like((4, 8, 48, 128), BF)])
    hidden = lax.all_to_all(hidden, "x", 0, 0)
    hidden = jnp.transpose(hidden.reshape(4, 8, 6, 8, 128), (2, 0, 1, 3, 4)).reshape(1, 1536, 128)
    new_anchor, new_momentum = call(
        outer_body, [zh], [mine, back, anchor, momentum], [like((1024, 128), F32)] * 2
    )
    return new_anchor, new_momentum, hidden


def solution(mesh):
    fine = Mesh(mesh.devices.reshape(tuple(SIZES.values())), AXES)
    rep, fsdp = ("zh", "c"), ("z", "x", "y")
    return jax.shard_map(
        lambda t, g, p, a, m: per_device(t, g, p[0], a, m),
        mesh=fine,
        in_specs=(P(rep, fsdp, None), P(None, fsdp), P(rep, None, fsdp), P(rep, fsdp), P(rep, fsdp)),
        out_specs=(P(rep, fsdp), P(rep, fsdp), P(rep, None, fsdp)),
        check_vma=False,
    )
```

time: 1400 us -> 158 us (0.11)
  the two profiles are of different devices: /device:TPU:1 before, /device:TPU:216 now
where the time goes in v2:
time: 158 us; the launch traced here: 157 us
  starting transfers between devices  78.3 us (50%)
  waiting for transfers between devices  45.6 us (29%)
  Pallas kernels  23.3 us (15%)
  local copies, waits for them, and re-layouts  7.58 us (5%)
    ppermute x14, starting transfers between devices, shift(): return lax.ppermute(value, axis, [(i, (i + by) % n) for i in range(n)])  48 us
    ppermute x4, waiting for transfers between devices, flip(): return lax.ppermute(value, axis, [(0, 1), (1, 0)])  25.1 us
    pallas_call x6, Pallas kernels, call(): pl.pallas_call(body, out_shape=outs, grid_spec=pltpu.PrefetchScalarGridSp...  23.3 us
    ppermute x4, starting transfers between devices, flip(): return lax.ppermute(value, axis, [(0, 1), (1, 0)])  17 us
    ppermute x14, waiting for transfers between devices, shift(): return lax.ppermute(value, axis, [(i, (i + by) % n) for i in range(n)])  14.2 us
    all_to_all x1, starting transfers between devices, per_device(): six = lax.all_to_all(cut, ('c', 'z'), 0, 0).reshape(96, 2048)  9.93 us
    all_to_all x1, waiting for transfers between devices, per_device(): hidden = lax.all_to_all(hidden, 'x', 0, 0)  6.27 us
    all_to_all x1, starting transfers between devices, per_device(): hidden = lax.all_to_all(hidden, 'x', 0, 0)  3.46 us
  transfers between devices with their start and end apart: 20, of which 8 were waited for; matrix products, arithmetic and copies ran while one was open for 2% of the time, Pallas kernels for 13%

profile of v2, /device:TPU:216, one launch (start us, length us, event | category | flops | bytes accessed | tf_op | source)
XLA Modules:
  0.0 157.2 jit_solution(16422772899759818324)
XLA Ops:
  2.8 9.9 %all-to-all-start = ((bf16[12,8,2048]{2,1,0:T(8,128)(2,1)}), bf16[12,8,2048]{2,1,0:T(8,128)(2,1)S(1)}, u32[]{:S(2)}, u32[]{:S(2)}) async-start(bf16[12,8,2048]{2,1,0:T(8,128)(2,1)} %bitcast.8), calls=%async_computation | async-start | bytes 786432 | tf_op jit(solution)/shard_map/all_to_all | solution.py:117
  17.3 3.8 %shard_map.76 = (bf16[2,1024,128]{2,1,0:T(8,128)(2,1)}, f32[1024,128]{1,0:T(8,128)}, f32[1024,128]{1,0:T(8,128)}, f32[1024,128]{1,0:T(8,128)}) custom-call(s32[2]{0:T(128)} %pad_add_fusion.at, bf16[2,2,1024,128]{3,2,1,0:T(8,128)(2,1)} %bitcast.28, bf16[2,1024,128]{2,1,0:T(8,128)(2,1)} %copy-done.12, f32[1024,128]{1,0:T(8,128)} %anchor.3, f32[1024,128]{1,0:T(8,128)} %momentum.3), custom_call_target="tpu_custom_call" | custom-call | bytes 1024 | tf_op jit(solution)/shard_map/pallas_call | solution.py:34
  21.0 10.6 %collective-permute-start.1 = (bf16[2,1024,128]{2,1,0:T(8,128)(2,1)}, bf16[2,1024,128]{2,1,0:T(8,128)(2,1)S(1)}, u32[]{:S(2)}, u32[]{:S(2)}) collective-permute-start(bf16[2,1024,128]{2,1,0:T(8,128)(2,1)} %get-tuple-element.24), channel_id=1, source_target_pairs={{0,384},{384,0},{1,385},{385,1},{2,386},{386,2},{3,387},{387,3},{4... | collective-permute-start | bytes 1572872 | tf_op jit(solution)/shard_map/ppermute | solution.py:22
  31.7 4.7 %collective-permute-start.4 = (bf16[96,2048]{1,0:T(8,128)(2,1)S(1)}, bf16[96,2048]{1,0:T(8,128)(2,1)S(1)}, u32[]{:S(2)}, u32[]{:S(2)}) collective-permute-start(bf16[96,2048]{1,0:T(8,128)(2,1)S(1)} %bitcast.23), channel_id=1, source_target_pairs={{0,1},{1,2},{2,3},{3,4},{4,5},{5,6},{6,7},{7,0},{8,9},{9,10},{10,1... | collective-permute-start | bytes 1179656 | tf_op jit(solution)/shard_map/ppermute | solution.py:18
  38.4 3.4 %collective-permute-start.10 = (bf16[2048,128]{1,0:T(8,128)(2,1)S(1)}, bf16[2048,128]{1,0:T(8,128)(2,1)}, u32[]{:S(2)}, u32[]{:S(2)}) collective-permute-start(bf16[2048,128]{1,0:T(8,128)(2,1)S(1)} %bitcast.33), channel_id=1, source_target_pairs={{0,8},{8,16},{16,24},{24,0},{1,9},{9,17},{17,25},{25,1},{2,10},{10... | collective-permute-start | bytes 1572872 | tf_op jit(solution)/shard_map/ppermute | solution.py:18
  41.8 4.6 %collective-permute-start.9 = (bf16[2048,128]{1,0:T(8,128)(2,1)S(1)}, bf16[2048,128]{1,0:T(8,128)(2,1)}, u32[]{:S(2)}, u32[]{:S(2)}) collective-permute-start(bf16[2048,128]{1,0:T(8,128)(2,1)S(1)} %bitcast.34), channel_id=1, source_target_pairs={{0,16},{8,24},{16,0},{24,8},{1,17},{9,25},{17,1},{25,9},{2,18},{10... | collective-permute-start | bytes 1572872 | tf_op jit(solution)/shard_map/ppermute | solution.py:18
  46.5 22.5 %collective-permute-done.1.back = bf16[2,1024,128]{2,1,0:T(8,128)(2,1)S(1)} collective-permute-done((bf16[2,1024,128]{2,1,0:T(8,128)(2,1)}, bf16[2,1024,128]{2,1,0:T(8,128)(2,1)S(1)}, u32[]{:S(2)}, u32[]{:S(2)}) %collective-permute-start.1) | collective-permute-done | bytes 524320 | tf_op jit(solution)/shard_map/ppermute | solution.py:22
  69.0 4.7 %collective-permute-start.8 = (bf16[2048,128]{1,0:T(8,128)(2,1)S(1)}, bf16[2048,128]{1,0:T(8,128)(2,1)}, u32[]{:S(2)}, u32[]{:S(2)}) collective-permute-start(bf16[2048,128]{1,0:T(8,128)(2,1)S(1)} %bitcast.35), channel_id=1, source_target_pairs={{0,24},{8,0},{16,8},{24,16},{1,25},{9,1},{17,9},{25,17},{2,26},{10... | collective-permute-start | bytes 1572872 | tf_op jit(solution)/shard_map/ppermute | solution.py:18
  73.7 4.7 %collective-permute-start.5 = (bf16[96,2048]{1,0:T(8,128)(2,1)S(1)}, bf16[96,2048]{1,0:T(8,128)(2,1)S(1)}, u32[]{:S(2)}, u32[]{:S(2)}) collective-permute-start(bf16[96,2048]{1,0:T(8,128)(2,1)S(1)} %collective-permute-done.4.refs_8_), channel_id=1, source_target_pairs={{0,1},{1,2},{2,3},{3,4},{4,5},{5,6},{6,7},{7,0},{8,9},{9,10},{10,1... | collective-permute-start | bytes 1179656 | tf_op jit(solution)/shard_map/ppermute | solution.py:18
  82.6 3.6 %collective-permute-done.5.refs_7_ = bf16[96,2048]{1,0:T(8,128)(2,1)S(1)} collective-permute-done((bf16[96,2048]{1,0:T(8,128)(2,1)S(1)}, bf16[96,2048]{1,0:T(8,128)(2,1)S(1)}, u32[]{:S(2)}, u32[]{:S(2)}) %collective-permute-start.5) | collective-permute-done | bytes 393248 | tf_op jit(solution)/shard_map/ppermute | solution.py:18
  86.3 5.3 %collective-permute-done.3.refs_2_ = bf16[96,2048]{1,0:T(8,128)(2,1)S(1)} collective-permute-done((bf16[96,2048]{1,0:T(8,128)(2,1)S(1)}, bf16[96,2048]{1,0:T(8,128)(2,1)S(1)}, u32[]{:S(2)}, u32[]{:S(2)}) %collective-permute-start.3) | collective-permute-done | bytes 393248 | tf_op jit(solution)/shard_map/ppermute | solution.py:18
  93.5 5.1 %collective-permute-start.6 = (bf16[96,2048]{1,0:T(8,128)(2,1)S(1)}, bf16[96,2048]{1,0:T(8,128)(2,1)S(1)}, u32[]{:S(2)}, u32[]{:S(2)}) collective-permute-start(bf16[96,2048]{1,0:T(8,128)(2,1)S(1)} %collective-permute-done.5.refs_7_), channel_id=1, source_target_pairs={{0,1},{1,2},{2,3},{3,4},{4,5},{5,6},{6,7},{7,0},{8,9},{9,10},{10,1... | collective-permute-start | bytes 1179656 | tf_op jit(solution)/shard_map/ppermute | solution.py:18
  100.6 4.2 %collective-permute-start.15 = (bf16[2048,128]{1,0:T(8,128)(2,1)}, bf16[2048,128]{1,0:T(8,128)(2,1)S(1)}, u32[]{:S(2)}, u32[]{:S(2)}) collective-permute-start(bf16[2048,128]{1,0:T(8,128)(2,1)} %bitcast.30), channel_id=1, source_target_pairs={{0,16},{8,24},{16,0},{24,8},{1,17},{9,25},{17,1},{25,9},{2,18},{10... | collective-permute-start | bytes 1572872 | tf_op jit(solution)/shard_map/ppermute | solution.py:18
  104.8 3.0 %collective-permute-start.14 = (bf16[2048,128]{1,0:T(8,128)(2,1)}, bf16[2048,128]{1,0:T(8,128)(2,1)}, u32[]{:S(2)}, u32[]{:S(2)}) collective-permute-start(bf16[2048,128]{1,0:T(8,128)(2,1)} %bitcast.31), channel_id=1, source_target_pairs={{0,24},{8,0},{16,8},{24,16},{1,25},{9,1},{17,9},{25,17},{2,26},{10... | collective-permute-start | bytes 1572872 | tf_op jit(solution)/shard_map/ppermute | solution.py:18
  109.3 2.7 %collective-permute-start.11 = (bf16[48,2048]{1,0:T(8,128)(2,1)}, bf16[48,2048]{1,0:T(8,128)(2,1)S(1)}, u32[]{:S(2)}, u32[]{:S(2)}) collective-permute-start(bf16[48,2048]{1,0:T(8,128)(2,1)} %slice.6), channel_id=1, source_target_pairs={{0,1},{1,2},{2,3},{3,4},{4,5},{5,6},{6,7},{7,0},{8,9},{9,10},{10,1... | collective-permute-start | bytes 589832 | tf_op jit(solution)/shard_map/ppermute | solution.py:18
  112.1 3.1 %collective-permute-start.12 = (bf16[48,2048]{1,0:T(8,128)(2,1)}, bf16[48,2048]{1,0:T(8,128)(2,1)S(1)}, u32[]{:S(2)}, u32[]{:S(2)}) collective-permute-start(bf16[48,2048]{1,0:T(8,128)(2,1)} %slice.7), channel_id=1, source_target_pairs={{0,7},{1,0},{2,1},{3,2},{4,3},{5,4},{6,5},{7,6},{8,15},{9,8},{10,9... | collective-permute-start | bytes 589832 | tf_op jit(solution)/shard_map/ppermute | solution.py:18
  117.1 3.9 %collective-permute-done.12.refs_5_ = bf16[48,2048]{1,0:T(8,128)(2,1)S(1)} collective-permute-done((bf16[48,2048]{1,0:T(8,128)(2,1)}, bf16[48,2048]{1,0:T(8,128)(2,1)S(1)}, u32[]{:S(2)}, u32[]{:S(2)}) %collective-permute-start.12) | collective-permute-done | bytes 196640 | tf_op jit(solution)/shard_map/ppermute | solution.py:18
  121.7 6.0 %shard_map.79 = (f32[8,48,512]{2,1,0:T(8,128)}, bf16[8,48,512]{2,1,0:T(8,128)(2,1)}) custom-call(s32[2]{0:T(128)} %pad_add_fusion.1.at, bf16[96,2048]{1,0:T(8,128)(2,1)} %bitcast.25, bf16[96,2048]{1,0:T(8,128)(2,1)} %copy-done.7, bf16[96,2048]{1,0:T(8,128)(2,1)} %copy-done.9, bf16[96,2048]{1,0:T(8,128)(2,1)} %copy-done.2, bf16[48,2048]{1,0:T(8,128)(2,1)} %copy-done.10, ...), custom_call_target="tpu_custom_call" | custom-call | bytes 1024 | tf_op jit(solution)/shard_map/pallas_call | solution.py:34
  130.7 6.0 %shard_map.80 = (f32[8,48,512]{2,1,0:T(8,128)}, bf16[8,48,512]{2,1,0:T(8,128)(2,1)}) custom-call(s32[2]{0:T(128)} %pad_add_fusion.1.at, bf16[96,2048]{1,0:T(8,128)(2,1)} %bitcast.26, bf16[96,2048]{1,0:T(8,128)(2,1)} %copy-done.7, bf16[96,2048]{1,0:T(8,128)(2,1)} %copy-done.9, bf16[96,2048]{1,0:T(8,128)(2,1)} %copy-done.2, bf16[48,2048]{1,0:T(8,128)(2,1)} %copy-done.10, ...), custom_call_target="tpu_custom_call" | custom-call | bytes 1024 | tf_op jit(solution)/shard_map/pallas_call | solution.py:34
  136.7 2.4 %collective-permute-start.17 = (bf16[8,48,512]{2,1,0:T(8,128)(2,1)}, bf16[8,48,512]{2,1,0:T(8,128)(2,1)S(1)}, u32[]{:S(2)}, u32[]{:S(2)}) collective-permute-start(bf16[8,48,512]{2,1,0:T(8,128)(2,1)} %get-tuple-element.42), channel_id=1, source_target_pairs={{0,192},{192,0},{1,193},{193,1},{2,194},{194,2},{3,195},{195,3},{4... | collective-permute-start | bytes 1179656 | tf_op jit(solution)/shard_map/ppermute | solution.py:22
  141.3 2.6 %shard_map.81 = bf16[4,8,48,128]{3,2,1,0:T(8,128)(2,1)} custom-call(s32[1]{0:T(128)} %bitcast.4.at, f32[8,48,512]{2,1,0:T(8,128)} %get-tuple-element.39.gate, bf16[8,48,512]{2,1,0:T(8,128)(2,1)} %copy-done.15, f32[8,48,512]{2,1,0:T(8,128)} %get-tuple-element.41.up, bf16[8,48,512]{2,1,0:T(8,128)(2,1)} %copy-done.16), custom_call_target="tpu_custom_call" | custom-call | bytes 1024 | tf_op jit(solution)/shard_map/pallas_call | solution.py:34
  144.0 3.5 %all-to-all-start.1 = ((bf16[4,8,48,128]{3,2,1,0:T(8,128)(2,1)}), bf16[4,8,48,128]{3,2,1,0:T(8,128)(2,1)S(1)}, u32[]{:S(2)}, u32[]{:S(2)}) async-start(bf16[4,8,48,128]{3,2,1,0:T(8,128)(2,1)} %shard_map.81), calls=%async_computation.1 | async-start | bytes 786432 | tf_op jit(solution)/shard_map/all_to_all | solution.py:145
  147.5 2.6 %shard_map.77 = (f32[1024,128]{1,0:T(8,128)}, f32[1024,128]{1,0:T(8,128)}) custom-call(s32[1]{0:T(128)} %bitcast.at, f32[1024,128]{1,0:T(8,128)} %get-tuple-element.23.mine, bf16[2,1024,128]{2,1,0:T(8,128)(2,1)} %copy-done.4, f32[1024,128]{1,0:T(8,128)} %anchor.3, f32[1024,128]{1,0:T(8,128)} %momentum.3), custom_call_target="tpu_custom_call" | custom-call | bytes 1024 | tf_op jit(solution)/shard_map/pallas_call | solution.py:34
  150.0 6.3 %all-to-all-done.1 = bf16[4,8,48,128]{3,2,1,0:T(8,128)(2,1)S(1)} async-done(((bf16[4,8,48,128]{3,2,1,0:T(8,128)(2,1)}), bf16[4,8,48,128]{3,2,1,0:T(8,128)(2,1)S(1)}, u32[]{:S(2)}, u32[]{:S(2)}) %all-to-all-start.1) | async-done | bytes 393248 | tf_op jit(solution)/shard_map/all_to_all | solution.py:145
  (68 shorter events, 26.7 us)
Async XLA Ops:
  0.6 37.7 %copy-start = (bf16[4096,128]{1,0:T(8,128)(2,1)S(1)}, bf16[4096,128]{1,0:T(8,128)(2,1)}, u32[]{:S(2)}) copy-start(bf16[4096,128]{1,0:T(8,128)(2,1)} %param.6) | copy-start | bytes 3145732
  2.8 28.9 %all-to-all-start = ((bf16[12,8,2048]{2,1,0:T(8,128)(2,1)}), bf16[12,8,2048]{2,1,0:T(8,128)(2,1)S(1)}, u32[]{:S(2)}, u32[]{:S(2)}) async-start(bf16[12,8,2048]{2,1,0:T(8,128)(2,1)} %bitcast.8), calls=%async_computation | async-start | bytes 786432 | tf_op jit(solution)/shard_map/all_to_all | solution.py:117
  12.7 3.8 %collective-permute-start = (bf16[2,1024,128]{2,1,0:T(8,128)(2,1)S(1)}, bf16[2,1024,128]{2,1,0:T(8,128)(2,1)S(1)}, u32[]{:S(2)}, u32[]{:S(2)}) collective-permute-start(bf16[2,1024,128]{2,1,0:T(8,128)(2,1)S(1)} %dynamic-slice_bitcast_fusion), channel_id=1, source_target_pairs={{0,192},{192,0},{1,193},{193,1},{2,194},{194,2},{3,195},{195,3},{4... | collective-permute-start | bytes 1572872 | tf_op jit(solution)/shard_map/ppermute | solution.py:22
  21.0 47.9 %collective-permute-start.1 = (bf16[2,1024,128]{2,1,0:T(8,128)(2,1)}, bf16[2,1024,128]{2,1,0:T(8,128)(2,1)S(1)}, u32[]{:S(2)}, u32[]{:S(2)}) collective-permute-start(bf16[2,1024,128]{2,1,0:T(8,128)(2,1)} %get-tuple-element.24), channel_id=1, source_target_pairs={{0,384},{384,0},{1,385},{385,1},{2,386},{386,2},{3,387},{387,3},{4... | collective-permute-start | bytes 1572872 | tf_op jit(solution)/shard_map/ppermute | solution.py:22
  31.7 41.9 %collective-permute-start.4 = (bf16[96,2048]{1,0:T(8,128)(2,1)S(1)}, bf16[96,2048]{1,0:T(8,128)(2,1)S(1)}, u32[]{:S(2)}, u32[]{:S(2)}) collective-permute-start(bf16[96,2048]{1,0:T(8,128)(2,1)S(1)} %bitcast.23), channel_id=1, source_target_pairs={{0,1},{1,2},{2,3},{3,4},{4,5},{5,6},{6,7},{7,0},{8,9},{9,10},{10,1... | collective-permute-start | bytes 1179656 | tf_op jit(solution)/shard_map/ppermute | solution.py:18
  36.4 42.0 %collective-permute-start.2 = (bf16[96,2048]{1,0:T(8,128)(2,1)S(1)}, bf16[96,2048]{1,0:T(8,128)(2,1)S(1)}, u32[]{:S(2)}, u32[]{:S(2)}) collective-permute-start(bf16[96,2048]{1,0:T(8,128)(2,1)S(1)} %bitcast.24), channel_id=1, source_target_pairs={{0,7},{1,0},{2,1},{3,2},{4,3},{5,4},{6,5},{7,6},{8,15},{9,8},{10,9... | collective-permute-start | bytes 1179656 | tf_op jit(solution)/shard_map/ppermute | solution.py:18
  38.4 82.6 %copy-start.5 = (bf16[2,1,1024,128]{3,2,1,0:T(8,128)(2,1)}, bf16[2,1,1024,128]{3,2,1,0:T(8,128)(2,1)S(1)}, u32[]{:S(2)}) copy-start(bf16[2,1,1024,128]{3,2,1,0:T(8,128)(2,1)S(1)} %constant_dynamic-slice_fusion) | copy-start | bytes 1572868
  38.4 60.2 %collective-permute-start.10 = (bf16[2048,128]{1,0:T(8,128)(2,1)S(1)}, bf16[2048,128]{1,0:T(8,128)(2,1)}, u32[]{:S(2)}, u32[]{:S(2)}) collective-permute-start(bf16[2048,128]{1,0:T(8,128)(2,1)S(1)} %bitcast.33), channel_id=1, source_target_pairs={{0,8},{8,16},{16,24},{24,0},{1,9},{9,17},{17,25},{25,1},{2,10},{10... | collective-permute-start | bytes 1572872 | tf_op jit(solution)/shard_map/ppermute | solution.py:18
  41.8 58.8 %collective-permute-start.9 = (bf16[2048,128]{1,0:T(8,128)(2,1)S(1)}, bf16[2048,128]{1,0:T(8,128)(2,1)}, u32[]{:S(2)}, u32[]{:S(2)}) collective-permute-start(bf16[2048,128]{1,0:T(8,128)(2,1)S(1)} %bitcast.34), channel_id=1, source_target_pairs={{0,16},{8,24},{16,0},{24,8},{1,17},{9,25},{17,1},{25,9},{2,18},{10... | collective-permute-start | bytes 1572872 | tf_op jit(solution)/shard_map/ppermute | solution.py:18
  69.0 35.8 %collective-permute-start.8 = (bf16[2048,128]{1,0:T(8,128)(2,1)S(1)}, bf16[2048,128]{1,0:T(8,128)(2,1)}, u32[]{:S(2)}, u32[]{:S(2)}) collective-permute-start(bf16[2048,128]{1,0:T(8,128)(2,1)S(1)} %bitcast.35), channel_id=1, source_target_pairs={{0,24},{8,0},{16,8},{24,16},{1,25},{9,1},{17,9},{25,17},{2,26},{10... | collective-permute-start | bytes 1572872 | tf_op jit(solution)/shard_map/ppermute | solution.py:18
  73.7 12.6 %collective-permute-start.5 = (bf16[96,2048]{1,0:T(8,128)(2,1)S(1)}, bf16[96,2048]{1,0:T(8,128)(2,1)S(1)}, u32[]{:S(2)}, u32[]{:S(2)}) collective-permute-start(bf16[96,2048]{1,0:T(8,128)(2,1)S(1)} %collective-permute-done.4.refs_8_), channel_id=1, source_target_pairs={{0,1},{1,2},{2,3},{3,4},{4,5},{5,6},{6,7},{7,0},{8,9},{9,10},{10,1... | collective-permute-start | bytes 1179656 | tf_op jit(solution)/shard_map/ppermute | solution.py:18
  78.4 13.2 %collective-permute-start.3 = (bf16[96,2048]{1,0:T(8,128)(2,1)S(1)}, bf16[96,2048]{1,0:T(8,128)(2,1)S(1)}, u32[]{:S(2)}, u32[]{:S(2)}) collective-permute-start(bf16[96,2048]{1,0:T(8,128)(2,1)S(1)} %collective-permute-done.2.refs_1_), channel_id=1, source_target_pairs={{0,7},{1,0},{2,1},{3,2},{4,3},{5,4},{6,5},{7,6},{8,15},{9,8},{10,9... | collective-permute-start | bytes 1179656 | tf_op jit(solution)/shard_map/ppermute | solution.py:18
  86.3 25.8 %copy-start.8 = (bf16[96,2048]{1,0:T(8,128)(2,1)}, bf16[96,2048]{1,0:T(8,128)(2,1)S(1)}, u32[]{:S(2)}) copy-start(bf16[96,2048]{1,0:T(8,128)(2,1)S(1)} %collective-permute-done.5.refs_7_) | copy-start | bytes 1179652
  91.6 29.5 %copy-start.9 = (bf16[96,2048]{1,0:T(8,128)(2,1)}, bf16[96,2048]{1,0:T(8,128)(2,1)S(1)}, u32[]{:S(2)}) copy-start(bf16[96,2048]{1,0:T(8,128)(2,1)S(1)} %collective-permute-done.3.refs_2_) | copy-start | bytes 1179652
  91.6 16.3 %collective-permute-start.7 = (bf16[96,2048]{1,0:T(8,128)(2,1)S(1)}, bf16[96,2048]{1,0:T(8,128)(2,1)S(1)}, u32[]{:S(2)}, u32[]{:S(2)}) collective-permute-start(bf16[96,2048]{1,0:T(8,128)(2,1)S(1)} %collective-permute-done.3.refs_2_), channel_id=1, source_target_pairs={{0,7},{1,0},{2,1},{3,2},{4,3},{5,4},{6,5},{7,6},{8,15},{9,8},{10,9... | collective-permute-start | bytes 1179656 | tf_op jit(solution)/shard_map/ppermute | solution.py:18
  93.5 14.4 %collective-permute-start.6 = (bf16[96,2048]{1,0:T(8,128)(2,1)S(1)}, bf16[96,2048]{1,0:T(8,128)(2,1)S(1)}, u32[]{:S(2)}, u32[]{:S(2)}) collective-permute-start(bf16[96,2048]{1,0:T(8,128)(2,1)S(1)} %collective-permute-done.5.refs_7_), channel_id=1, source_target_pairs={{0,1},{1,2},{2,3},{3,4},{4,5},{5,6},{6,7},{7,0},{8,9},{9,10},{10,1... | collective-permute-start | bytes 1179656 | tf_op jit(solution)/shard_map/ppermute | solution.py:18
  98.7 31.0 %collective-permute-start.16 = (bf16[2048,128]{1,0:T(8,128)(2,1)}, bf16[2048,128]{1,0:T(8,128)(2,1)S(1)}, u32[]{:S(2)}, u32[]{:S(2)}) collective-permute-start(bf16[2048,128]{1,0:T(8,128)(2,1)} %bitcast.29), channel_id=1, source_target_pairs={{0,8},{8,16},{16,24},{24,0},{1,9},{9,17},{17,25},{25,1},{2,10},{10... | collective-permute-start | bytes 1572872 | tf_op jit(solution)/shard_map/ppermute | solution.py:18
  100.6 29.1 %collective-permute-start.15 = (bf16[2048,128]{1,0:T(8,128)(2,1)}, bf16[2048,128]{1,0:T(8,128)(2,1)S(1)}, u32[]{:S(2)}, u32[]{:S(2)}) collective-permute-start(bf16[2048,128]{1,0:T(8,128)(2,1)} %bitcast.30), channel_id=1, source_target_pairs={{0,16},{8,24},{16,0},{24,8},{1,17},{9,25},{17,1},{25,9},{2,18},{10... | collective-permute-start | bytes 1572872 | tf_op jit(solution)/shard_map/ppermute | solution.py:18
  104.8 24.9 %collective-permute-start.14 = (bf16[2048,128]{1,0:T(8,128)(2,1)}, bf16[2048,128]{1,0:T(8,128)(2,1)}, u32[]{:S(2)}, u32[]{:S(2)}) collective-permute-start(bf16[2048,128]{1,0:T(8,128)(2,1)} %bitcast.31), channel_id=1, source_target_pairs={{0,24},{8,0},{16,8},{24,16},{1,25},{9,1},{17,9},{25,17},{2,26},{10... | collective-permute-start | bytes 1572872 | tf_op jit(solution)/shard_map/ppermute | solution.py:18
  109.3 7.8 %collective-permute-start.11 = (bf16[48,2048]{1,0:T(8,128)(2,1)}, bf16[48,2048]{1,0:T(8,128)(2,1)S(1)}, u32[]{:S(2)}, u32[]{:S(2)}) collective-permute-start(bf16[48,2048]{1,0:T(8,128)(2,1)} %slice.6), channel_id=1, source_target_pairs={{0,1},{1,2},{2,3},{3,4},{4,5},{5,6},{6,7},{7,0},{8,9},{9,10},{10,1... | collective-permute-start | bytes 589832 | tf_op jit(solution)/shard_map/ppermute | solution.py:18
  112.1 9.0 %collective-permute-start.12 = (bf16[48,2048]{1,0:T(8,128)(2,1)}, bf16[48,2048]{1,0:T(8,128)(2,1)S(1)}, u32[]{:S(2)}, u32[]{:S(2)}) collective-permute-start(bf16[48,2048]{1,0:T(8,128)(2,1)} %slice.7), channel_id=1, source_target_pairs={{0,7},{1,0},{2,1},{3,2},{4,3},{5,4},{6,5},{7,6},{8,15},{9,8},{10,9... | collective-permute-start | bytes 589832 | tf_op jit(solution)/shard_map/ppermute | solution.py:18
  127.8 11.3 %collective-permute-start.13 = (bf16[8,48,512]{2,1,0:T(8,128)(2,1)}, bf16[8,48,512]{2,1,0:T(8,128)(2,1)S(1)}, u32[]{:S(2)}, u32[]{:S(2)}) collective-permute-start(bf16[8,48,512]{2,1,0:T(8,128)(2,1)} %get-tuple-element.40), channel_id=1, source_target_pairs={{0,192},{192,0},{1,193},{193,1},{2,194},{194,2},{3,195},{195,3},{4... | collective-permute-start | bytes 1179656 | tf_op jit(solution)/shard_map/ppermute | solution.py:22
  136.7 3.9 %collective-permute-start.17 = (bf16[8,48,512]{2,1,0:T(8,128)(2,1)}, bf16[8,48,512]{2,1,0:T(8,128)(2,1)S(1)}, u32[]{:S(2)}, u32[]{:S(2)}) collective-permute-start(bf16[8,48,512]{2,1,0:T(8,128)(2,1)} %get-tuple-element.42), channel_id=1, source_target_pairs={{0,192},{192,0},{1,193},{193,1},{2,194},{194,2},{3,195},{195,3},{4... | collective-permute-start | bytes 1179656 | tf_op jit(solution)/shard_map/ppermute | solution.py:22
  144.0 12.3 %all-to-all-start.1 = ((bf16[4,8,48,128]{3,2,1,0:T(8,128)(2,1)}), bf16[4,8,48,128]{3,2,1,0:T(8,128)(2,1)S(1)}, u32[]{:S(2)}, u32[]{:S(2)}) async-start(bf16[4,8,48,128]{3,2,1,0:T(8,128)(2,1)} %shard_map.81), calls=%async_computation.1 | async-start | bytes 786432 | tf_op jit(solution)/shard_map/all_to_all | solution.py:145
  (14 other events, 44.8 us)

commit v3 on v2

v3 whole, which is shorter than its diff:
```python
import functools

import jax
import jax.numpy as jnp
from jax import lax
from jax.experimental import pallas as pl
from jax.experimental.pallas import tpu as pltpu
from jax.sharding import Mesh, PartitionSpec as P

SIZES = {"zh": 2, "c": 2, "z": 6, "x": 4, "y": 8}
AXES = tuple(SIZES)
BF, F32 = jnp.bfloat16, jnp.float32
MIB = 1024 * 1024
PARTS = 2
ROWS = 1024 // PARTS


def shift(value, axis, by):
    n = SIZES[axis]
    return lax.ppermute(value, axis, [(i, (i + by) % n) for i in range(n)])


def flip(value, axis):
    return lax.ppermute(value, axis, [(0, 1), (1, 0)])


def after(value, *others):
    return lax.optimization_barrier((value, *others))[0]


def whole(a):
    return pl.BlockSpec(a.shape, lambda i: (0,) * len(a.shape))


def like(shape, dtype):
    return jax.ShapeDtypeStruct(shape, dtype)


def call(body, arrays, outs, held=False, scratch=()):
    return pl.pallas_call(
        body,
        out_shape=outs,
        grid=(1,),
        in_specs=[pl.BlockSpec(memory_space=pl.ANY) if held else whole(a) for a in arrays],
        out_specs=[whole(o) for o in outs],
        scratch_shapes=list(scratch),
        compiler_params=pltpu.CompilerParams(vmem_limit_bytes=60 * MIB),
        cost_estimate=pl.CostEstimate(flops=0, bytes_accessed=1024, transcendentals=0),
    )(*arrays)


def prepare_body(grad, got, anchor, momentum, *outs):
    parts, (half_done, mine, other) = outs[:PARTS], outs[PARTS:]
    zh, c = lax.axis_index("zh"), lax.axis_index("c")
    s = grad[zh, c].astype(F32) + got[zh].astype(F32)
    o = grad[1 - zh, c].astype(F32) + got[1 - zh].astype(F32)
    v = (anchor[...] - 0.567 * momentum[...]) - 0.3325 * s
    mine[...] = s
    other[...] = o
    half_done[...] = v
    for part, ref in enumerate(parts):
        rows = slice(ROWS * part, ROWS * part + ROWS)
        ref[0] = v[rows].astype(BF)
        ref[1] = o[rows].astype(BF)


def update_body(part, back, half_done, other, up):
    zh = lax.axis_index("zh")
    rows = pl.ds(ROWS * part, ROWS)
    here = (half_done[rows] - 0.3325 * back[1].astype(F32)).astype(BF)
    there = (back[0].astype(F32) - 0.3325 * other[rows]).astype(BF)
    for x in range(4):
        up[x, zh] = here
        up[x, 1 - zh] = there


def outer_body(*refs):
    backs, (mine, anchor, momentum, new_anchor, new_momentum) = refs[:PARTS], refs[PARTS:]
    for part, ref in enumerate(backs):
        rows = pl.ds(ROWS * part, ROWS)
        mean_delta = (mine[rows] + ref[1].astype(F32)) * 0.25
        moved = 0.9 * momentum[rows] + mean_delta
        new_momentum[rows] = moved
        new_anchor[rows] = anchor[rows] - 0.7 * (mean_delta + 0.9 * moved)


def product_body(spans, *refs):
    tokens, weights = refs[:9], refs[9 : 9 + len(spans)]
    keep, give, rows, columns, sems = refs[9 + len(spans) :]
    c, y = lax.axis_index("c"), lax.axis_index("y")
    weight_copies, token_copies = [], []
    for pair in range(2):
        for x in (2 * pair, 2 * pair + 1):
            for source, runs in zip(weights, spans):
                for at, row, length in runs:
                    target = columns.at[pl.ds(at, length), pl.ds(128 * x, 128)]
                    weight_copies.append((pair, source.at[x, pl.ds(row, length)], target))
    for s, (piece, offset, length) in enumerate(
        [(t, 96 * s, 96) for s, t in enumerate(tokens[:4])]
        + [(tokens[4], 384, 48), (tokens[5], 432, 48)]
        + [(t, 96 * s, 96) for s, t in zip((5, 6, 7), tokens[6:])]
    ):
        place = lax.rem(y + offset // 96, 8) * 96 + offset % 96
        token_copies.append((0, piece, rows.at[pl.ds(pl.multiple_of(place, 16), length)]))
    order = [w for w in weight_copies if w[0] == 0] + token_copies + [w for w in weight_copies if w[0] == 1]
    copies = []
    for i, (pair, source, target) in enumerate(order):
        copy = pltpu.make_async_copy(source, target, sems.at[i])
        copy.start()
        copies.append((pair, copy))
    for pair in range(2):
        for at, copy in copies:
            if at == pair:
                copy.wait()
        span = slice(256 * pair, 256 * pair + 256)
        for half in range(2):
            total = jnp.dot(rows[384 * half : 384 * half + 384], columns[:, span], preferred_element_type=F32)
            for s in range(4):
                low, high = total[96 * s : 96 * s + 48], total[96 * s + 48 : 96 * s + 96]
                keep[4 * half + s, :, span] = jnp.where(c == 0, low, high)
                give[4 * half + s, :, span] = jnp.where(c == 0, high, low).astype(BF)


def product(spans, tokens, weights):
    count = 9 + 4 * sum(len(s) for s in spans)
    return call(
        functools.partial(product_body, spans),
        [*tokens, *weights],
        [like((8, 48, 512), F32), like((8, 48, 512), BF)],
        True,
        [pltpu.VMEM((768, 2048), BF), pltpu.VMEM((2048, 512), BF), pltpu.SemaphoreType.DMA((count,))],
    )


def gated_body(gate, gate_got, up, up_got, hidden):
    for x in range(4):
        columns = slice(128 * x, 128 * x + 128)
        g = gate[:, :, columns] + gate_got[:, :, columns].astype(F32)
        u = up[:, :, columns] + up_got[:, :, columns].astype(F32)
        hidden[x] = (g / (1.0 + jnp.exp(-g)) * u).astype(BF)


def per_device(tokens, gate_weight, pseudo_grad, anchor, momentum):
    c = lax.axis_index("c")

    grad = pseudo_grad.reshape(2, 2, 1024, 128)
    pick = lax.dynamic_index_in_dim(grad, 1 - c, 1, keepdims=False)
    got = flip(pick, "c")
    *parts, half_done, mine, other = call(
        prepare_body,
        [grad, got, anchor, momentum],
        [like((2, ROWS, 128), BF)] * PARTS + [like((1024, 128), F32)] * 3,
    )
    tokens = after(tokens, pick)
    cut = jnp.transpose(tokens[0].reshape(8, 2, 2, 1024), (2, 0, 1, 3)).reshape(2, 1, 8, 2048)
    cut = jnp.broadcast_to(cut, (2, 6, 8, 2048)).reshape(12, 8, 2048)
    six = lax.all_to_all(cut, ("c", "z"), 0, 0).reshape(96, 2048)
    six = after(six, parts[0])
    own = lax.dynamic_index_in_dim(gate_weight.reshape(2, 2, 1024, 128), c, 1, keepdims=False).reshape(1, 2048, 128)
    own = after(jnp.broadcast_to(own, (4, 2048, 128)), six)

    def update(part):
        (up,) = call(functools.partial(update_body, part), [backs[part], half_done, other], [like((4, 2, ROWS, 128), BF)])
        return up.reshape(4, 2 * ROWS, 128)

    first = [shift(six, "y", by) for by in (2, -2, 1, -1)] + [flip(parts[0], "zh")]
    f2, b2, f1, b1, back, gate_all = lax.optimization_barrier((*first, lax.all_to_all(own, "x", 0, 0)))
    backs = [back]
    second = [shift(f1, "y", 2), shift(b1, "y", -2), shift(f2[:48], "y", 2), shift(b2[48:], "y", -2), flip(parts[1], "zh")]
    f3, b3, f4, b4, back, up = lax.optimization_barrier((*second, lax.all_to_all(update(0), "x", 0, 0)))
    backs.append(back)
    ups = [up, lax.all_to_all(update(1), "x", 0, 0)]
    pieces = [six, b1, b2, b3, f4, b4, f3, f2, f1]
    gate, gate_give = product((((0, 0, 2048),),), pieces, [gate_all])
    gate_got = flip(gate_give, "c")
    spans = tuple(((ROWS * p, 0, ROWS), (1024 + ROWS * p, ROWS, ROWS)) for p in range(PARTS))
    up, up_give = product(spans, pieces, ups)
    up_got = flip(up_give, "c")

    (hidden,) = call(gated_body, [gate, gate_got, up, up_got], [like((4, 8, 48, 128), BF)])
    hidden = lax.all_to_all(hidden, "x", 0, 0)
    hidden = jnp.transpose(hidden.reshape(4, 8, 6, 8, 128), (2, 0, 1, 3, 4)).reshape(1, 1536, 128)
    new_anchor, new_momentum = call(outer_body, [*backs, mine, anchor, momentum], [like((1024, 128), F32)] * 2)
    return new_anchor, new_momentum, hidden


def solution(mesh):
    fine = Mesh(mesh.devices.reshape(tuple(SIZES.values())), AXES)
    rep, fsdp = ("zh", "c"), ("z", "x", "y")
    return jax.shard_map(
        lambda t, g, p, a, m: per_device(t, g, p[0], a, m),
        mesh=fine,
        in_specs=(P(rep, fsdp, None), P(None, fsdp), P(rep, None, fsdp), P(rep, fsdp), P(rep, fsdp)),
        out_specs=(P(rep, fsdp), P(rep, fsdp), P(rep, None, fsdp)),
        check_vma=False,
    )
```

time: 158 us -> 175 us (1.11)
  the two profiles are of different devices: /device:TPU:216 before, /device:TPU:72 now
where the time goes in v3:
time: 175 us; the launch traced here: 173 us
  starting transfers between devices  82.7 us (47%)
  waiting for transfers between devices  54.2 us (31%)
  Pallas kernels  24.9 us (14%)
  local copies, waits for them, and re-layouts  10.7 us (6%)
    ppermute x8, starting transfers between devices, shift(): return lax.ppermute(value, axis, [(i, (i + by) % n) for i in range(n)])  28.9 us
    ppermute x5, starting transfers between devices, flip(): return lax.ppermute(value, axis, [(0, 1), (1, 0)])  25.3 us
    ppermute x5, waiting for transfers between devices, flip(): return lax.ppermute(value, axis, [(0, 1), (1, 0)])  24.9 us
    pallas_call x7, Pallas kernels, call(): pl.pallas_call(body, out_shape=outs, grid=(1,), in_specs=[pl.BlockSpec(me...  24.9 us
    all_to_all x1, starting transfers between devices, per_device(): six = lax.all_to_all(cut, ('c', 'z'), 0, 0).reshape(96, 2048)  11.7 us
    ppermute x8, waiting for transfers between devices, shift(): return lax.ppermute(value, axis, [(i, (i + by) % n) for i in range(n)])  8.47 us
    all_to_all x1, waiting for transfers between devices, per_device(): ups = [up, lax.all_to_all(update(1), 'x', 0, 0)]  7.43 us
    all_to_all x1, waiting for transfers between devices, per_device(): six = lax.all_to_all(cut, ('c', 'z'), 0, 0).reshape(96, 2048)  7.38 us
  transfers between devices with their start and end apart: 18, of which 9 were waited for; matrix products, arithmetic and copies ran while one was open for 1% of the time, Pallas kernels for 9%

profile of v3, /device:TPU:72, one launch (start us, length us, event | category | flops | bytes accessed | tf_op | source)
XLA Modules:
  0.0 173.4 jit_solution(13515650527551819973)
XLA Ops:
  3.6 11.7 %all-to-all-start = ((bf16[12,8,2048]{2,1,0:T(8,128)(2,1)}), bf16[12,8,2048]{2,1,0:T(8,128)(2,1)S(1)}, u32[]{:S(2)}, u32[]{:S(2)}) async-start(bf16[12,8,2048]{2,1,0:T(8,128)(2,1)} %bitcast.4), calls=%async_computation | async-start | bytes 786432 | tf_op jit(solution)/shard_map/all_to_all | solution.py:157
  19.9 3.1 %shard_map.76 = (bf16[2,512,128]{2,1,0:T(8,128)(2,1)}, bf16[2,512,128]{2,1,0:T(8,128)(2,1)}, f32[1024,128]{1,0:T(8,128)}, f32[1024,128]{1,0:T(8,128)}, f32[1024,128]{1,0:T(8,128)}) custom-call(bf16[2,2,1024,128]{3,2,1,0:T(8,128)(2,1)} %bitcast.27, bf16[2,1024,128]{2,1,0:T(8,128)(2,1)} %copy-done.14, f32[1024,128]{1,0:T(8,128)} %refs_3_.1, f32[1024,128]{1,0:T(8,128)} %refs_4_.1), custom_call_target="tpu_custom_call" | custom-call | bytes 1024 | tf_op jit(solution)/shard_map/pallas_call | solution.py:40
  23.0 7.4 %all-to-all-done = bf16[12,8,2048]{2,1,0:T(8,128)(2,1)S(1)} async-done(((bf16[12,8,2048]{2,1,0:T(8,128)(2,1)}), bf16[12,8,2048]{2,1,0:T(8,128)(2,1)S(1)}, u32[]{:S(2)}, u32[]{:S(2)}) %all-to-all-start) | async-done | bytes 393248 | tf_op jit(solution)/shard_map/all_to_all | solution.py:157
  32.0 4.3 %all-to-all-start.1 = ((bf16[4,2048,128]{2,1,0:T(8,128)(2,1)}), bf16[4,2048,128]{2,1,0:T(8,128)(2,1)S(1)}, u32[]{:S(2)}, u32[]{:S(2)}) async-start(bf16[4,2048,128]{2,1,0:T(8,128)(2,1)} %broadcast_in_dim.17), calls=%async_computation.1 | async-start | bytes 4194304 | tf_op jit(solution)/shard_map/all_to_all | solution.py:167
  38.7 3.5 %collective-permute-start.3 = (bf16[96,2048]{1,0:T(8,128)(2,1)S(1)}, bf16[96,2048]{1,0:T(8,128)(2,1)S(1)}, u32[]{:S(2)}, u32[]{:S(2)}) collective-permute-start(bf16[96,2048]{1,0:T(8,128)(2,1)S(1)} %bitcast.21), channel_id=1, source_target_pairs={{0,1},{1,2},{2,3},{3,4},{4,5},{5,6},{6,7},{7,0},{8,9},{9,10},{10,1... | collective-permute-start | bytes 1179656 | tf_op jit(solution)/shard_map/ppermute | solution.py:20
  42.2 6.5 %collective-permute-start.2 = (bf16[96,2048]{1,0:T(8,128)(2,1)S(1)}, bf16[96,2048]{1,0:T(8,128)(2,1)S(1)}, u32[]{:S(2)}, u32[]{:S(2)}) collective-permute-start(bf16[96,2048]{1,0:T(8,128)(2,1)S(1)} %bitcast.22), channel_id=1, source_target_pairs={{0,6},{1,7},{2,0},{3,1},{4,2},{5,3},{6,4},{7,5},{8,14},{9,15},{10,... | collective-permute-start | bytes 1179656 | tf_op jit(solution)/shard_map/ppermute | solution.py:20
  50.6 9.4 %collective-permute-start.5 = (bf16[2,512,128]{2,1,0:T(8,128)(2,1)}, bf16[2,512,128]{2,1,0:T(8,128)(2,1)S(1)}, u32[]{:S(2)}, u32[]{:S(2)}) collective-permute-start(bf16[2,512,128]{2,1,0:T(8,128)(2,1)} %get-tuple-element.30), channel_id=1, source_target_pairs={{0,384},{384,0},{1,385},{385,1},{2,386},{386,2},{3,387},{387,3},{4... | collective-permute-start | bytes 786440 | tf_op jit(solution)/shard_map/ppermute | solution.py:24
  60.0 18.6 %collective-permute-done.5.back.refs_0_ = bf16[2,512,128]{2,1,0:T(8,128)(2,1)S(1)} collective-permute-done((bf16[2,512,128]{2,1,0:T(8,128)(2,1)}, bf16[2,512,128]{2,1,0:T(8,128)(2,1)S(1)}, u32[]{:S(2)}, u32[]{:S(2)}) %collective-permute-start.5) | collective-permute-done | bytes 262176 | tf_op jit(solution)/shard_map/ppermute | solution.py:24
  80.4 3.2 %shard_map.77 = bf16[4,2,512,128]{3,2,1,0:T(8,128)(2,1)} custom-call(bf16[2,512,128]{2,1,0:T(8,128)(2,1)} %copy-done.10, f32[1024,128]{1,0:T(8,128)} %get-tuple-element.39.half_done, f32[1024,128]{1,0:T(8,128)} %get-tuple-element.40.other), custom_call_target="tpu_custom_call" | custom-call | bytes 1024 | tf_op jit(solution)/shard_map/pallas_call | solution.py:40
  83.6 4.5 %all-to-all-start.2 = ((bf16[4,1024,128]{2,1,0:T(8,128)(2,1)}), bf16[4,1024,128]{2,1,0:T(8,128)(2,1)}, u32[]{:S(2)}, u32[]{:S(2)}) async-start(bf16[4,1024,128]{2,1,0:T(8,128)(2,1)} %bitcast.18), calls=%async_computation.2 | async-start | bytes 2097152 | tf_op jit(solution)/shard_map/all_to_all | solution.py:170
  88.1 5.0 %collective-permute-start.6 = (bf16[96,2048]{1,0:T(8,128)(2,1)}, bf16[96,2048]{1,0:T(8,128)(2,1)S(1)}, u32[]{:S(2)}, u32[]{:S(2)}) collective-permute-start(bf16[96,2048]{1,0:T(8,128)(2,1)} %copy-done.7), channel_id=1, source_target_pairs={{0,2},{1,3},{2,4},{3,5},{4,6},{5,7},{6,0},{7,1},{8,10},{9,11},{10,... | collective-permute-start | bytes 1179656 | tf_op jit(solution)/shard_map/ppermute | solution.py:20
  93.1 2.9 %collective-permute-start.7 = (bf16[96,2048]{1,0:T(8,128)(2,1)}, bf16[96,2048]{1,0:T(8,128)(2,1)S(1)}, u32[]{:S(2)}, u32[]{:S(2)}) collective-permute-start(bf16[96,2048]{1,0:T(8,128)(2,1)} %copy-done.6), channel_id=1, source_target_pairs={{0,6},{1,7},{2,0},{3,1},{4,2},{5,3},{6,4},{7,5},{8,14},{9,15},{10,... | collective-permute-start | bytes 1179656 | tf_op jit(solution)/shard_map/ppermute | solution.py:20
  96.1 9.9 %collective-permute-start.10 = (bf16[2,512,128]{2,1,0:T(8,128)(2,1)}, bf16[2,512,128]{2,1,0:T(8,128)(2,1)S(1)}, u32[]{:S(2)}, u32[]{:S(2)}) collective-permute-start(bf16[2,512,128]{2,1,0:T(8,128)(2,1)} %get-tuple-element.38), channel_id=1, source_target_pairs={{0,384},{384,0},{1,385},{385,1},{2,386},{386,2},{3,387},{387,3},{4... | collective-permute-start | bytes 786440 | tf_op jit(solution)/shard_map/ppermute | solution.py:24
  107.0 4.5 %collective-permute-start.9 = (bf16[48,2048]{1,0:T(8,128)(2,1)S(1)}, bf16[48,2048]{1,0:T(8,128)(2,1)S(1)}, u32[]{:S(2)}, u32[]{:S(2)}) collective-permute-start(bf16[48,2048]{1,0:T(8,128)(2,1)S(1)} %slice.7), channel_id=1, source_target_pairs={{0,6},{1,7},{2,0},{3,1},{4,2},{5,3},{6,4},{7,5},{8,14},{9,15},{10,... | collective-permute-start | bytes 589832 | tf_op jit(solution)/shard_map/ppermute | solution.py:20
  113.7 2.7 %collective-permute-done.10.refs_1_.back = bf16[2,512,128]{2,1,0:T(8,128)(2,1)S(1)} collective-permute-done((bf16[2,512,128]{2,1,0:T(8,128)(2,1)}, bf16[2,512,128]{2,1,0:T(8,128)(2,1)S(1)}, u32[]{:S(2)}, u32[]{:S(2)}) %collective-permute-start.10) | collective-permute-done | bytes 262176 | tf_op jit(solution)/shard_map/ppermute | solution.py:24
  119.0 5.9 %collective-permute-done.8.refs_4_ = bf16[48,2048]{1,0:T(8,128)(2,1)S(1)} collective-permute-done((bf16[48,2048]{1,0:T(8,128)(2,1)S(1)}, bf16[48,2048]{1,0:T(8,128)(2,1)S(1)}, u32[]{:S(2)}, u32[]{:S(2)}) %collective-permute-start.8) | collective-permute-done | bytes 196640 | tf_op jit(solution)/shard_map/ppermute | solution.py:20
  125.0 2.7 %shard_map.80 = bf16[4,2,512,128]{3,2,1,0:T(8,128)(2,1)} custom-call(bf16[2,512,128]{2,1,0:T(8,128)(2,1)} %copy-done.11, f32[1024,128]{1,0:T(8,128)} %get-tuple-element.39.half_done, f32[1024,128]{1,0:T(8,128)} %get-tuple-element.40.other), custom_call_target="tpu_custom_call" | custom-call | bytes 1024 | tf_op jit(solution)/shard_map/pallas_call | solution.py:40
  127.7 4.5 %all-to-all-start.3 = ((bf16[4,1024,128]{2,1,0:T(8,128)(2,1)}), bf16[4,1024,128]{2,1,0:T(8,128)(2,1)S(1)}, u32[]{:S(2)}, u32[]{:S(2)}) async-start(bf16[4,1024,128]{2,1,0:T(8,128)(2,1)} %bitcast.19), calls=%async_computation.3 | async-start | bytes 2097152 | tf_op jit(solution)/shard_map/all_to_all | solution.py:172
  132.2 5.2 %shard_map.79 = (f32[8,48,512]{2,1,0:T(8,128)}, bf16[8,48,512]{2,1,0:T(8,128)(2,1)}) custom-call(bf16[96,2048]{1,0:T(8,128)(2,1)} %bitcast.24, bf16[96,2048]{1,0:T(8,128)(2,1)} %copy-done.6, bf16[96,2048]{1,0:T(8,128)(2,1)} %copy-done.4, bf16[96,2048]{1,0:T(8,128)(2,1)} %copy-done.9, bf16[48,2048]{1,0:T(8,128)(2,1)} %copy-done.13, ...), custom_call_target="tpu_custom_call" | custom-call | bytes 1024 | tf_op jit(solution)/shard_map/pallas_call | solution.py:40
  139.4 7.4 %all-to-all-done.3.refs_10_ = bf16[4,1024,128]{2,1,0:T(8,128)(2,1)S(1)} async-done(((bf16[4,1024,128]{2,1,0:T(8,128)(2,1)}), bf16[4,1024,128]{2,1,0:T(8,128)(2,1)S(1)}, u32[]{:S(2)}, u32[]{:S(2)}) %all-to-all-start.3) | async-done | bytes 1048608 | tf_op jit(solution)/shard_map/all_to_all | solution.py:172
  147.8 5.4 %shard_map.81 = (f32[8,48,512]{2,1,0:T(8,128)}, bf16[8,48,512]{2,1,0:T(8,128)(2,1)}) custom-call(bf16[96,2048]{1,0:T(8,128)(2,1)} %bitcast.25, bf16[96,2048]{1,0:T(8,128)(2,1)} %copy-done.6, bf16[96,2048]{1,0:T(8,128)(2,1)} %copy-done.4, bf16[96,2048]{1,0:T(8,128)(2,1)} %copy-done.9, bf16[48,2048]{1,0:T(8,128)(2,1)} %copy-done.13, ...), custom_call_target="tpu_custom_call" | custom-call | bytes 1024 | tf_op jit(solution)/shard_map/pallas_call | solution.py:40
  160.4 3.5 %all-to-all-start.4 = ((bf16[4,8,48,128]{3,2,1,0:T(8,128)(2,1)}), bf16[4,8,48,128]{3,2,1,0:T(8,128)(2,1)S(1)}, u32[]{:S(2)}, u32[]{:S(2)}) async-start(bf16[4,8,48,128]{3,2,1,0:T(8,128)(2,1)} %shard_map.82), calls=%async_computation.4 | async-start | bytes 786432 | tf_op jit(solution)/shard_map/all_to_all | solution.py:181
  163.9 2.6 %shard_map.78 = (f32[1024,128]{1,0:T(8,128)}, f32[1024,128]{1,0:T(8,128)}) custom-call(bf16[2,512,128]{2,1,0:T(8,128)(2,1)} %copy-done.10, bf16[2,512,128]{2,1,0:T(8,128)(2,1)} %copy-done.11, f32[1024,128]{1,0:T(8,128)} %get-tuple-element.42.refs_2_, f32[1024,128]{1,0:T(8,128)} %refs_3_.1, f32[1024,128]{1,0:T(8,128)} %refs_4_.1), custom_call_target="tpu_custom_call" | custom-call | bytes 1024 | tf_op jit(solution)/shard_map/pallas_call | solution.py:40
  166.5 6.0 %all-to-all-done.4 = bf16[4,8,48,128]{3,2,1,0:T(8,128)(2,1)S(1)} async-done(((bf16[4,8,48,128]{3,2,1,0:T(8,128)(2,1)}), bf16[4,8,48,128]{3,2,1,0:T(8,128)(2,1)S(1)}, u32[]{:S(2)}, u32[]{:S(2)}) %all-to-all-start.4) | async-done | bytes 393248 | tf_op jit(solution)/shard_map/all_to_all | solution.py:181
  (62 shorter events, 31.8 us)
Async XLA Ops:
  0.6 16.7 %copy-start = (bf16[4096,128]{1,0:T(8,128)(2,1)S(1)}, bf16[4096,128]{1,0:T(8,128)(2,1)}, u32[]{:S(2)}) copy-start(bf16[4096,128]{1,0:T(8,128)(2,1)} %param.6) | copy-start | bytes 3145732
  3.6 26.8 %all-to-all-start = ((bf16[12,8,2048]{2,1,0:T(8,128)(2,1)}), bf16[12,8,2048]{2,1,0:T(8,128)(2,1)S(1)}, u32[]{:S(2)}, u32[]{:S(2)}) async-start(bf16[12,8,2048]{2,1,0:T(8,128)(2,1)} %bitcast.4), calls=%async_computation | async-start | bytes 786432 | tf_op jit(solution)/shard_map/all_to_all | solution.py:157
  15.3 3.8 %collective-permute-start = (bf16[2,1024,128]{2,1,0:T(8,128)(2,1)S(1)}, bf16[2,1024,128]{2,1,0:T(8,128)(2,1)S(1)}, u32[]{:S(2)}, u32[]{:S(2)}) collective-permute-start(bf16[2,1024,128]{2,1,0:T(8,128)(2,1)S(1)} %dynamic-slice_bitcast_fusion), channel_id=1, source_target_pairs={{0,192},{192,0},{1,193},{193,1},{2,194},{194,2},{3,195},{195,3},{4... | collective-permute-start | bytes 1572872 | tf_op jit(solution)/shard_map/ppermute | solution.py:24
  30.4 18.3 %copy-start.3 = (bf16[12,8,2048]{2,1,0:T(8,128)(2,1)}, bf16[12,8,2048]{2,1,0:T(8,128)(2,1)S(1)}, u32[]{:S(2)}) copy-start(bf16[12,8,2048]{2,1,0:T(8,128)(2,1)S(1)} %all-to-all-done) | copy-start | bytes 1179652
  32.0 48.4 %all-to-all-start.1 = ((bf16[4,2048,128]{2,1,0:T(8,128)(2,1)}), bf16[4,2048,128]{2,1,0:T(8,128)(2,1)S(1)}, u32[]{:S(2)}, u32[]{:S(2)}) async-start(bf16[4,2048,128]{2,1,0:T(8,128)(2,1)} %broadcast_in_dim.17), calls=%async_computation.1 | async-start | bytes 4194304 | tf_op jit(solution)/shard_map/all_to_all | solution.py:167
  36.3 42.4 %collective-permute-start.4 = (bf16[96,2048]{1,0:T(8,128)(2,1)S(1)}, bf16[96,2048]{1,0:T(8,128)(2,1)S(1)}, u32[]{:S(2)}, u32[]{:S(2)}) collective-permute-start(bf16[96,2048]{1,0:T(8,128)(2,1)S(1)} %bitcast.20), channel_id=1, source_target_pairs={{0,7},{1,0},{2,1},{3,2},{4,3},{5,4},{6,5},{7,6},{8,15},{9,8},{10,9... | collective-permute-start | bytes 1179656 | tf_op jit(solution)/shard_map/ppermute | solution.py:20
  38.7 40.0 %collective-permute-start.3 = (bf16[96,2048]{1,0:T(8,128)(2,1)S(1)}, bf16[96,2048]{1,0:T(8,128)(2,1)S(1)}, u32[]{:S(2)}, u32[]{:S(2)}) collective-permute-start(bf16[96,2048]{1,0:T(8,128)(2,1)S(1)} %bitcast.21), channel_id=1, source_target_pairs={{0,1},{1,2},{2,3},{3,4},{4,5},{5,6},{6,7},{7,0},{8,9},{9,10},{10,1... | collective-permute-start | bytes 1179656 | tf_op jit(solution)/shard_map/ppermute | solution.py:20
  42.2 36.5 %collective-permute-start.2 = (bf16[96,2048]{1,0:T(8,128)(2,1)S(1)}, bf16[96,2048]{1,0:T(8,128)(2,1)S(1)}, u32[]{:S(2)}, u32[]{:S(2)}) collective-permute-start(bf16[96,2048]{1,0:T(8,128)(2,1)S(1)} %bitcast.22), channel_id=1, source_target_pairs={{0,6},{1,7},{2,0},{3,1},{4,2},{5,3},{6,4},{7,5},{8,14},{9,15},{10,... | collective-permute-start | bytes 1179656 | tf_op jit(solution)/shard_map/ppermute | solution.py:20
  48.6 31.8 %collective-permute-start.1 = (bf16[96,2048]{1,0:T(8,128)(2,1)S(1)}, bf16[96,2048]{1,0:T(8,128)(2,1)}, u32[]{:S(2)}, u32[]{:S(2)}) collective-permute-start(bf16[96,2048]{1,0:T(8,128)(2,1)S(1)} %bitcast.23), channel_id=1, source_target_pairs={{0,2},{1,3},{2,4},{3,5},{4,6},{5,7},{6,0},{7,1},{8,10},{9,11},{10,... | collective-permute-start | bytes 1179656 | tf_op jit(solution)/shard_map/ppermute | solution.py:20
  50.6 28.1 %collective-permute-start.5 = (bf16[2,512,128]{2,1,0:T(8,128)(2,1)}, bf16[2,512,128]{2,1,0:T(8,128)(2,1)S(1)}, u32[]{:S(2)}, u32[]{:S(2)}) collective-permute-start(bf16[2,512,128]{2,1,0:T(8,128)(2,1)} %get-tuple-element.30), channel_id=1, source_target_pairs={{0,384},{384,0},{1,385},{385,1},{2,386},{386,2},{3,387},{387,3},{4... | collective-permute-start | bytes 786440 | tf_op jit(solution)/shard_map/ppermute | solution.py:24
  80.4 3.2 %copy-start.1 = (bf16[4,2048,128]{2,1,0:T(8,128)(2,1)}, bf16[4,2048,128]{2,1,0:T(8,128)(2,1)S(1)}, u32[]{:S(2)}) copy-start(bf16[4,2048,128]{2,1,0:T(8,128)(2,1)S(1)} %all-to-all-done.1.refs_9_) | copy-start | bytes 6291460
  80.4 26.5 %copy-start.5 = (bf16[96,2048]{1,0:T(8,128)(2,1)S(1)}, bf16[96,2048]{1,0:T(8,128)(2,1)}, u32[]{:S(2)}) copy-start(bf16[96,2048]{1,0:T(8,128)(2,1)} %copy-done.4) | copy-start | bytes 1179652
  83.6 41.4 %all-to-all-start.2 = ((bf16[4,1024,128]{2,1,0:T(8,128)(2,1)}), bf16[4,1024,128]{2,1,0:T(8,128)(2,1)}, u32[]{:S(2)}, u32[]{:S(2)}) async-start(bf16[4,1024,128]{2,1,0:T(8,128)(2,1)} %bitcast.18), calls=%async_computation.2 | async-start | bytes 2097152 | tf_op jit(solution)/shard_map/all_to_all | solution.py:170
  88.1 36.8 %collective-permute-start.6 = (bf16[96,2048]{1,0:T(8,128)(2,1)}, bf16[96,2048]{1,0:T(8,128)(2,1)S(1)}, u32[]{:S(2)}, u32[]{:S(2)}) collective-permute-start(bf16[96,2048]{1,0:T(8,128)(2,1)} %copy-done.7), channel_id=1, source_target_pairs={{0,2},{1,3},{2,4},{3,5},{4,6},{5,7},{6,0},{7,1},{8,10},{9,11},{10,... | collective-permute-start | bytes 1179656 | tf_op jit(solution)/shard_map/ppermute | solution.py:20
  93.1 31.8 %collective-permute-start.7 = (bf16[96,2048]{1,0:T(8,128)(2,1)}, bf16[96,2048]{1,0:T(8,128)(2,1)S(1)}, u32[]{:S(2)}, u32[]{:S(2)}) collective-permute-start(bf16[96,2048]{1,0:T(8,128)(2,1)} %copy-done.6), channel_id=1, source_target_pairs={{0,6},{1,7},{2,0},{3,1},{4,2},{5,3},{6,4},{7,5},{8,14},{9,15},{10,... | collective-permute-start | bytes 1179656 | tf_op jit(solution)/shard_map/ppermute | solution.py:20
  96.1 20.4 %collective-permute-start.10 = (bf16[2,512,128]{2,1,0:T(8,128)(2,1)}, bf16[2,512,128]{2,1,0:T(8,128)(2,1)S(1)}, u32[]{:S(2)}, u32[]{:S(2)}) collective-permute-start(bf16[2,512,128]{2,1,0:T(8,128)(2,1)} %get-tuple-element.38), channel_id=1, source_target_pairs={{0,384},{384,0},{1,385},{385,1},{2,386},{386,2},{3,387},{387,3},{4... | collective-permute-start | bytes 786440 | tf_op jit(solution)/shard_map/ppermute | solution.py:24
  107.0 12.0 %collective-permute-start.9 = (bf16[48,2048]{1,0:T(8,128)(2,1)S(1)}, bf16[48,2048]{1,0:T(8,128)(2,1)S(1)}, u32[]{:S(2)}, u32[]{:S(2)}) collective-permute-start(bf16[48,2048]{1,0:T(8,128)(2,1)S(1)} %slice.7), channel_id=1, source_target_pairs={{0,6},{1,7},{2,0},{3,1},{4,2},{5,3},{6,4},{7,5},{8,14},{9,15},{10,... | collective-permute-start | bytes 589832 | tf_op jit(solution)/shard_map/ppermute | solution.py:20
  111.5 13.4 %collective-permute-start.8 = (bf16[48,2048]{1,0:T(8,128)(2,1)S(1)}, bf16[48,2048]{1,0:T(8,128)(2,1)S(1)}, u32[]{:S(2)}, u32[]{:S(2)}) collective-permute-start(bf16[48,2048]{1,0:T(8,128)(2,1)S(1)} %slice.6), channel_id=1, source_target_pairs={{0,2},{1,3},{2,4},{3,5},{4,6},{5,7},{6,0},{7,1},{8,10},{9,11},{10,... | collective-permute-start | bytes 589832 | tf_op jit(solution)/shard_map/ppermute | solution.py:20
  116.5 8.5 %copy-start.11 = (bf16[2,512,128]{2,1,0:T(8,128)(2,1)}, bf16[2,512,128]{2,1,0:T(8,128)(2,1)S(1)}, u32[]{:S(2)}) copy-start(bf16[2,512,128]{2,1,0:T(8,128)(2,1)S(1)} %collective-permute-done.10.refs_1_.back) | copy-start | bytes 786436
  119.0 8.7 %copy-start.12 = (bf16[48,2048]{1,0:T(8,128)(2,1)}, bf16[48,2048]{1,0:T(8,128)(2,1)S(1)}, u32[]{:S(2)}) copy-start(bf16[48,2048]{1,0:T(8,128)(2,1)S(1)} %collective-permute-done.9.refs_5_) | copy-start | bytes 589828
  127.7 19.1 %all-to-all-start.3 = ((bf16[4,1024,128]{2,1,0:T(8,128)(2,1)}), bf16[4,1024,128]{2,1,0:T(8,128)(2,1)S(1)}, u32[]{:S(2)}, u32[]{:S(2)}) async-start(bf16[4,1024,128]{2,1,0:T(8,128)(2,1)} %bitcast.19), calls=%async_computation.3 | async-start | bytes 2097152 | tf_op jit(solution)/shard_map/all_to_all | solution.py:172
  137.4 17.7 %collective-permute-start.11 = (bf16[8,48,512]{2,1,0:T(8,128)(2,1)}, bf16[8,48,512]{2,1,0:T(8,128)(2,1)S(1)}, u32[]{:S(2)}, u32[]{:S(2)}) collective-permute-start(bf16[8,48,512]{2,1,0:T(8,128)(2,1)} %get-tuple-element.51), channel_id=1, source_target_pairs={{0,192},{192,0},{1,193},{193,1},{2,194},{194,2},{3,195},{195,3},{4... | collective-permute-start | bytes 1179656 | tf_op jit(solution)/shard_map/ppermute | solution.py:24
  153.2 3.8 %collective-permute-start.12 = (bf16[8,48,512]{2,1,0:T(8,128)(2,1)}, bf16[8,48,512]{2,1,0:T(8,128)(2,1)S(1)}, u32[]{:S(2)}, u32[]{:S(2)}) collective-permute-start(bf16[8,48,512]{2,1,0:T(8,128)(2,1)} %get-tuple-element.54), channel_id=1, source_target_pairs={{0,192},{192,0},{1,193},{193,1},{2,194},{194,2},{3,195},{195,3},{4... | collective-permute-start | bytes 1179656 | tf_op jit(solution)/shard_map/ppermute | solution.py:24
  160.4 12.1 %all-to-all-start.4 = ((bf16[4,8,48,128]{3,2,1,0:T(8,128)(2,1)}), bf16[4,8,48,128]{3,2,1,0:T(8,128)(2,1)S(1)}, u32[]{:S(2)}, u32[]{:S(2)}) async-start(bf16[4,8,48,128]{3,2,1,0:T(8,128)(2,1)} %shard_map.82), calls=%async_computation.4 | async-start | bytes 786432 | tf_op jit(solution)/shard_map/all_to_all | solution.py:181
  (11 other events, 16.0 us)

commit v4 on v3

--- a/solution.py
+++ b/solution.py
@@ -11,7 +11,7 @@
 AXES = tuple(SIZES)
 BF, F32 = jnp.bfloat16, jnp.float32
 MIB = 1024 * 1024
-PARTS = 2
+PARTS = 1
 ROWS = 1024 // PARTS
 
 
@@ -22,6 +22,16 @@
 
 def flip(value, axis):
     return lax.ppermute(value, axis, [(0, 1), (1, 0)])
+
+
+def along(value):
+    pairs = []
+    for zh in range(2):
+        for c in range(2):
+            for z in range(6):
+                to = (6 * zh + z + (3 if c == 0 else -3)) % 12
+                pairs.append(((2 * zh + c) * 6 + z, (2 * (to // 6) + c) * 6 + to % 6))
+    return lax.ppermute(value, ("zh", "c", "z"), pairs)
 
 
 def after(value, *others):
@@ -88,37 +98,34 @@
     tokens, weights = refs[:9], refs[9 : 9 + len(spans)]
     keep, give, rows, columns, sems = refs[9 + len(spans) :]
     c, y = lax.axis_index("c"), lax.axis_index("y")
-    weight_copies, token_copies = [], []
+    weight_copies, token_copies = ([], []), ([], [])
+    for x in range(4):
+        for source, runs in zip(weights, spans):
+            for at, row, length in runs:
+                target = columns.at[pl.ds(at, length), pl.ds(128 * x, 128)]
+                weight_copies[x // 2].append((source.at[x, pl.ds(row, length)], target))
+    for piece, at, length in zip(tokens, (0, 96, 192, 288, 384, 432, 480, 576, 672), (96, 96, 96, 96, 48, 48, 96, 96, 96)):
+        token_copies[at // 384].append((piece, rows.at[pl.ds(at, length)]))
+    count, stages = 0, []
+    for stage in (weight_copies[0] + token_copies[0], token_copies[1], weight_copies[1]):
+        copies = []
+        for source, target in stage:
+            copy = pltpu.make_async_copy(source, target, sems.at[count])
+            copy.start()
+            copies.append(copy)
+            count += 1
+        stages.append(copies)
     for pair in range(2):
-        for x in (2 * pair, 2 * pair + 1):
-            for source, runs in zip(weights, spans):
-                for at, row, length in runs:
-                    target = columns.at[pl.ds(at, length), pl.ds(128 * x, 128)]
-                    weight_copies.append((pair, source.at[x, pl.ds(row, length)], target))
-    for s, (piece, offset, length) in enumerate(
-        [(t, 96 * s, 96) for s, t in enumerate(tokens[:4])]
-        + [(tokens[4], 384, 48), (tokens[5], 432, 48)]
-        + [(t, 96 * s, 96) for s, t in zip((5, 6, 7), tokens[6:])]
-    ):
-        place = lax.rem(y + offset // 96, 8) * 96 + offset % 96
-        token_copies.append((0, piece, rows.at[pl.ds(pl.multiple_of(place, 16), length)]))
-    order = [w for w in weight_copies if w[0] == 0] + token_copies + [w for w in weight_copies if w[0] == 1]
-    copies = []
-    for i, (pair, source, target) in enumerate(order):
-        copy = pltpu.make_async_copy(source, target, sems.at[i])
-        copy.start()
-        copies.append((pair, copy))
-    for pair in range(2):
-        for at, copy in copies:
-            if at == pair:
-                copy.wait()
         span = slice(256 * pair, 256 * pair + 256)
         for half in range(2):
+            for copy in stages[2 * pair + half] if pair + half < 2 or half == 0 else ():
+                copy.wait()
             total = jnp.dot(rows[384 * half : 384 * half + 384], columns[:, span], preferred_element_type=F32)
             for s in range(4):
                 low, high = total[96 * s : 96 * s + 48], total[96 * s + 48 : 96 * s + 96]
-                keep[4 * half + s, :, span] = jnp.where(c == 0, low, high)
-                give[4 * half + s, :, span] = jnp.where(c == 0, high, low).astype(BF)
+                place = lax.rem(y + 4 * half + s, 8)
+                keep[place, :, span] = jnp.where(c == 0, low, high)
+                give[place, :, span] = jnp.where(c == 0, high, low).astype(BF)
 
 
 def product(spans, tokens, weights):
@@ -163,14 +170,16 @@
         (up,) = call(functools.partial(update_body, part), [backs[part], half_done, other], [like((4, 2, ROWS, 128), BF)])
         return up.reshape(4, 2 * ROWS, 128)
 
-    first = [shift(six, "y", by) for by in (2, -2, 1, -1)] + [flip(parts[0], "zh")]
-    f2, b2, f1, b1, back, gate_all = lax.optimization_barrier((*first, lax.all_to_all(own, "x", 0, 0)))
+    gate_all = lax.all_to_all(own, "x", 0, 0)
+    f1, b1 = shift(six, "y", 1), shift(six, "y", -1)
+    f1, b1, back = lax.optimization_barrier((f1, b1, along(parts[0])))
+    f2, b2 = shift(f1, "y", 1), shift(b1, "y", -1)
+    f2, b2, back, gate_all = lax.optimization_barrier((f2, b2, along(back), gate_all))
     backs = [back]
-    second = [shift(f1, "y", 2), shift(b1, "y", -2), shift(f2[:48], "y", 2), shift(b2[48:], "y", -2), flip(parts[1], "zh")]
-    f3, b3, f4, b4, back, up = lax.optimization_barrier((*second, lax.all_to_all(update(0), "x", 0, 0)))
-    backs.append(back)
-    ups = [up, lax.all_to_all(update(1), "x", 0, 0)]
+    f3, b3 = shift(f2, "y", 1), shift(b2, "y", -1)
+    f4, b4 = shift(f3[:48], "y", 1), shift(b3[48:], "y", -1)
     pieces = [six, b1, b2, b3, f4, b4, f3, f2, f1]
+    ups = [lax.all_to_all(update(0), "x", 0, 0)]
     gate, gate_give = product((((0, 0, 2048),),), pieces, [gate_all])
     gate_got = flip(gate_give, "c")
     spans = tuple(((ROWS * p, 0, ROWS), (1024 + ROWS * p, ROWS, ROWS)) for p in range(PARTS))

time: 175 us -> 161 us (0.920)
  the two profiles are of different devices: /device:TPU:72 before, /device:TPU:1 now
where the time goes in v4:
time: 161 us; the launch traced here: 159 us
  starting transfers between devices  76.7 us (48%)
  waiting for transfers between devices  49 us (30%)
  Pallas kernels  23.6 us (15%)
  local copies, waits for them, and re-layouts  8.44 us (5%)
    ppermute x8, starting transfers between devices, shift(): return lax.ppermute(value, axis, [(i, (i + by) % n) for i in range(n)])  28.1 us
    pallas_call x6, Pallas kernels, call(): pl.pallas_call(body, out_shape=outs, grid=(1,), in_specs=[pl.BlockSpec(me...  23.6 us
    ppermute x8, waiting for transfers between devices, shift(): return lax.ppermute(value, axis, [(i, (i + by) % n) for i in range(n)])  21.2 us
    ppermute x2, starting transfers between devices, along(): return lax.ppermute(value, ('zh', 'c', 'z'), pairs)  14.5 us
    all_to_all x1, starting transfers between devices, per_device(): six = lax.all_to_all(cut, ('c', 'z'), 0, 0).reshape(96, 2048)  14 us
    ppermute x2, waiting for transfers between devices, along(): return lax.ppermute(value, ('zh', 'c', 'z'), pairs)  10.6 us
    all_to_all x1, waiting for transfers between devices, per_device(): six = lax.all_to_all(cut, ('c', 'z'), 0, 0).reshape(96, 2048)  8.38 us
    ppermute x3, starting transfers between devices, flip(): return lax.ppermute(value, axis, [(0, 1), (1, 0)])  7.63 us
  transfers between devices with their start and end apart: 17, of which 10 were waited for; matrix products, arithmetic and copies ran while one was open for 0% of the time, Pallas kernels for 11%

profile of v4, /device:TPU:1, one launch (start us, length us, event | category | flops | bytes accessed | tf_op | source)
XLA Modules:
  0.0 158.6 jit_solution(696924002252448548)
XLA Ops:
  3.6 14.0 %all-to-all-start = ((bf16[12,8,2048]{2,1,0:T(8,128)(2,1)}), bf16[12,8,2048]{2,1,0:T(8,128)(2,1)S(1)}, u32[]{:S(2)}, u32[]{:S(2)}) async-start(bf16[12,8,2048]{2,1,0:T(8,128)(2,1)} %bitcast.4), calls=%async_computation | async-start | bytes 786432 | tf_op jit(solution)/shard_map/all_to_all | solution.py:164
  22.1 3.1 %shard_map.76 = (bf16[2,1024,128]{2,1,0:T(8,128)(2,1)}, f32[1024,128]{1,0:T(8,128)}, f32[1024,128]{1,0:T(8,128)}, f32[1024,128]{1,0:T(8,128)}) custom-call(bf16[2,2,1024,128]{3,2,1,0:T(8,128)(2,1)} %bitcast.23, bf16[2,1024,128]{2,1,0:T(8,128)(2,1)} %copy-done.11, f32[1024,128]{1,0:T(8,128)} %refs_2_.1, f32[1024,128]{1,0:T(8,128)} %refs_3_.1), custom_call_target="tpu_custom_call" | custom-call | bytes 1024 | tf_op jit(solution)/shard_map/pallas_call | solution.py:50
  25.2 8.4 %all-to-all-done = bf16[12,8,2048]{2,1,0:T(8,128)(2,1)S(1)} async-done(((bf16[12,8,2048]{2,1,0:T(8,128)(2,1)}), bf16[12,8,2048]{2,1,0:T(8,128)(2,1)S(1)}, u32[]{:S(2)}, u32[]{:S(2)}) %all-to-all-start) | async-done | bytes 393248 | tf_op jit(solution)/shard_map/all_to_all | solution.py:164
  35.2 3.7 %all-to-all-start.1 = ((bf16[4,2048,128]{2,1,0:T(8,128)(2,1)}), bf16[4,2048,128]{2,1,0:T(8,128)(2,1)S(1)}, u32[]{:S(2)}, u32[]{:S(2)}) async-start(bf16[4,2048,128]{2,1,0:T(8,128)(2,1)} %broadcast_in_dim.17), calls=%async_computation.1 | async-start | bytes 4194304 | tf_op jit(solution)/shard_map/all_to_all | solution.py:173
  38.9 7.5 %collective-permute-start.3 = (bf16[2,1024,128]{2,1,0:T(8,128)(2,1)}, bf16[2,1024,128]{2,1,0:T(8,128)(2,1)S(1)}, u32[]{:S(2)}, u32[]{:S(2)}) collective-permute-start(bf16[2,1024,128]{2,1,0:T(8,128)(2,1)} %get-tuple-element.24), channel_id=1, source_target_pairs={{0,96},{32,128},{64,160},{96,384},{128,416},{160,448},{192,672},{2... | collective-permute-start | bytes 1572872 | tf_op jit(solution)/shard_map/ppermute | solution.py:34
  46.4 3.2 %collective-permute-start.1 = (bf16[96,2048]{1,0:T(8,128)(2,1)S(1)}, bf16[96,2048]{1,0:T(8,128)(2,1)S(1)}, u32[]{:S(2)}, u32[]{:S(2)}) collective-permute-start(bf16[96,2048]{1,0:T(8,128)(2,1)S(1)} %bitcast.18), channel_id=1, source_target_pairs={{0,1},{1,2},{2,3},{3,4},{4,5},{5,6},{6,7},{7,0},{8,9},{9,10},{10,1... | collective-permute-start | bytes 1179656 | tf_op jit(solution)/shard_map/ppermute | solution.py:20
  49.6 3.8 %collective-permute-start.2 = (bf16[96,2048]{1,0:T(8,128)(2,1)S(1)}, bf16[96,2048]{1,0:T(8,128)(2,1)S(1)}, u32[]{:S(2)}, u32[]{:S(2)}) collective-permute-start(bf16[96,2048]{1,0:T(8,128)(2,1)S(1)} %bitcast.19), channel_id=1, source_target_pairs={{0,7},{1,0},{2,1},{3,2},{4,3},{5,4},{6,5},{7,6},{8,15},{9,8},{10,9... | collective-permute-start | bytes 1179656 | tf_op jit(solution)/shard_map/ppermute | solution.py:20
  53.4 10.6 %collective-permute-done.3 = bf16[2,1024,128]{2,1,0:T(8,128)(2,1)S(1)} collective-permute-done((bf16[2,1024,128]{2,1,0:T(8,128)(2,1)}, bf16[2,1024,128]{2,1,0:T(8,128)(2,1)S(1)}, u32[]{:S(2)}, u32[]{:S(2)}) %collective-permute-start.3) | collective-permute-done | bytes 524320 | tf_op jit(solution)/shard_map/ppermute | solution.py:34
  64.1 7.0 %collective-permute-start.6 = (bf16[2,1024,128]{2,1,0:T(8,128)(2,1)S(1)}, bf16[2,1024,128]{2,1,0:T(8,128)(2,1)}, u32[]{:S(2)}, u32[]{:S(2)}) collective-permute-start(bf16[2,1024,128]{2,1,0:T(8,128)(2,1)S(1)} %collective-permute-done.3), channel_id=1, source_target_pairs={{0,96},{32,128},{64,160},{96,384},{128,416},{160,448},{192,672},{2... | collective-permute-start | bytes 1572872 | tf_op jit(solution)/shard_map/ppermute | solution.py:34
  71.1 3.2 %collective-permute-start.4 = (bf16[96,2048]{1,0:T(8,128)(2,1)S(1)}, bf16[96,2048]{1,0:T(8,128)(2,1)S(1)}, u32[]{:S(2)}, u32[]{:S(2)}) collective-permute-start(bf16[96,2048]{1,0:T(8,128)(2,1)S(1)} %collective-permute-done.1.refs_8_), channel_id=1, source_target_pairs={{0,1},{1,2},{2,3},{3,4},{4,5},{5,6},{6,7},{7,0},{8,9},{9,10},{10,1... | collective-permute-start | bytes 1179656 | tf_op jit(solution)/shard_map/ppermute | solution.py:20
  74.3 3.8 %collective-permute-start.5 = (bf16[96,2048]{1,0:T(8,128)(2,1)S(1)}, bf16[96,2048]{1,0:T(8,128)(2,1)S(1)}, u32[]{:S(2)}, u32[]{:S(2)}) collective-permute-start(bf16[96,2048]{1,0:T(8,128)(2,1)S(1)} %collective-permute-done.2.refs_1_), channel_id=1, source_target_pairs={{0,7},{1,0},{2,1},{3,2},{4,3},{5,4},{6,5},{7,6},{8,15},{9,8},{10,9... | collective-permute-start | bytes 1179656 | tf_op jit(solution)/shard_map/ppermute | solution.py:20
  78.1 5.9 %collective-permute-done.4.refs_7_ = bf16[96,2048]{1,0:T(8,128)(2,1)S(1)} collective-permute-done((bf16[96,2048]{1,0:T(8,128)(2,1)S(1)}, bf16[96,2048]{1,0:T(8,128)(2,1)S(1)}, u32[]{:S(2)}, u32[]{:S(2)}) %collective-permute-start.4) | collective-permute-done | bytes 393248 | tf_op jit(solution)/shard_map/ppermute | solution.py:20
  86.4 3.7 %shard_map.79 = bf16[4,2,1024,128]{3,2,1,0:T(8,128)(2,1)} custom-call(bf16[2,1024,128]{2,1,0:T(8,128)(2,1)} %collective-permute-done.6.refs_0_.back, f32[1024,128]{1,0:T(8,128)} %get-tuple-element.39.half_done, f32[1024,128]{1,0:T(8,128)} %get-tuple-element.40.other), custom_call_target="tpu_custom_call" | custom-call | bytes 1024 | tf_op jit(solution)/shard_map/pallas_call | solution.py:50
  90.1 4.5 %all-to-all-start.2 = ((bf16[4,2048,128]{2,1,0:T(8,128)(2,1)}), bf16[4,2048,128]{2,1,0:T(8,128)(2,1)}, u32[]{:S(2)}, u32[]{:S(2)}) async-start(bf16[4,2048,128]{2,1,0:T(8,128)(2,1)} %bitcast.17), calls=%async_computation.2 | async-start | bytes 4194304 | tf_op jit(solution)/shard_map/all_to_all | solution.py:182
  94.6 4.9 %collective-permute-start.7 = (bf16[96,2048]{1,0:T(8,128)(2,1)}, bf16[96,2048]{1,0:T(8,128)(2,1)S(1)}, u32[]{:S(2)}, u32[]{:S(2)}) collective-permute-start(bf16[96,2048]{1,0:T(8,128)(2,1)} %copy-done.8), channel_id=1, source_target_pairs={{0,7},{1,0},{2,1},{3,2},{4,3},{5,4},{6,5},{7,6},{8,15},{9,8},{10,9... | collective-permute-start | bytes 1179656 | tf_op jit(solution)/shard_map/ppermute | solution.py:20
  101.5 7.0 %collective-permute-done.7.refs_3_ = bf16[96,2048]{1,0:T(8,128)(2,1)S(1)} collective-permute-done((bf16[96,2048]{1,0:T(8,128)(2,1)}, bf16[96,2048]{1,0:T(8,128)(2,1)S(1)}, u32[]{:S(2)}, u32[]{:S(2)}) %collective-permute-start.7) | collective-permute-done | bytes 393248 | tf_op jit(solution)/shard_map/ppermute | solution.py:20
  108.5 5.3 %collective-permute-start.10 = (bf16[48,2048]{1,0:T(8,128)(2,1)S(1)}, bf16[48,2048]{1,0:T(8,128)(2,1)S(1)}, u32[]{:S(2)}, u32[]{:S(2)}) collective-permute-start(bf16[48,2048]{1,0:T(8,128)(2,1)S(1)} %slice.9), channel_id=1, source_target_pairs={{0,7},{1,0},{2,1},{3,2},{4,3},{5,4},{6,5},{7,6},{8,15},{9,8},{10,9... | collective-permute-start | bytes 589832 | tf_op jit(solution)/shard_map/ppermute | solution.py:20
  117.5 5.0 %collective-permute-done.9.refs_4_ = bf16[48,2048]{1,0:T(8,128)(2,1)S(1)} collective-permute-done((bf16[48,2048]{1,0:T(8,128)(2,1)S(1)}, bf16[48,2048]{1,0:T(8,128)(2,1)S(1)}, u32[]{:S(2)}, u32[]{:S(2)}) %collective-permute-start.9) | collective-permute-done | bytes 196640 | tf_op jit(solution)/shard_map/ppermute | solution.py:20
  123.2 5.7 %shard_map.78 = (f32[8,48,512]{2,1,0:T(8,128)}, bf16[8,48,512]{2,1,0:T(8,128)(2,1)}) custom-call(bf16[96,2048]{1,0:T(8,128)(2,1)} %bitcast.20, bf16[96,2048]{1,0:T(8,128)(2,1)} %copy-done.6, bf16[96,2048]{1,0:T(8,128)(2,1)} %copy-done.8, bf16[96,2048]{1,0:T(8,128)(2,1)} %copy-done.3, bf16[48,2048]{1,0:T(8,128)(2,1)} %copy-done.10, ...), custom_call_target="tpu_custom_call" | custom-call | bytes 1024 | tf_op jit(solution)/shard_map/pallas_call | solution.py:50
  129.0 3.7 %collective-permute-start.11 = (bf16[8,48,512]{2,1,0:T(8,128)(2,1)}, bf16[8,48,512]{2,1,0:T(8,128)(2,1)S(1)}, u32[]{:S(2)}, u32[]{:S(2)}) collective-permute-start(bf16[8,48,512]{2,1,0:T(8,128)(2,1)} %get-tuple-element.38), channel_id=1, source_target_pairs={{0,192},{192,0},{1,193},{193,1},{2,194},{194,2},{3,195},{195,3},{4... | collective-permute-start | bytes 1179656 | tf_op jit(solution)/shard_map/ppermute | solution.py:24
  132.6 5.8 %shard_map.80 = (f32[8,48,512]{2,1,0:T(8,128)}, bf16[8,48,512]{2,1,0:T(8,128)(2,1)}) custom-call(bf16[96,2048]{1,0:T(8,128)(2,1)} %bitcast.21, bf16[96,2048]{1,0:T(8,128)(2,1)} %copy-done.6, bf16[96,2048]{1,0:T(8,128)(2,1)} %copy-done.8, bf16[96,2048]{1,0:T(8,128)(2,1)} %copy-done.3, bf16[48,2048]{1,0:T(8,128)(2,1)} %copy-done.10, ...), custom_call_target="tpu_custom_call" | custom-call | bytes 1024 | tf_op jit(solution)/shard_map/pallas_call | solution.py:50
  143.0 2.7 %shard_map.81 = bf16[4,8,48,128]{3,2,1,0:T(8,128)(2,1)} custom-call(f32[8,48,512]{2,1,0:T(8,128)} %get-tuple-element.37.gate, bf16[8,48,512]{2,1,0:T(8,128)(2,1)} %copy-done.12, f32[8,48,512]{2,1,0:T(8,128)} %get-tuple-element.41.up, bf16[8,48,512]{2,1,0:T(8,128)(2,1)} %copy-done.13), custom_call_target="tpu_custom_call" | custom-call | bytes 1024 | tf_op jit(solution)/shard_map/pallas_call | solution.py:50
  145.7 4.3 %all-to-all-start.3 = ((bf16[4,8,48,128]{3,2,1,0:T(8,128)(2,1)}), bf16[4,8,48,128]{3,2,1,0:T(8,128)(2,1)S(1)}, u32[]{:S(2)}, u32[]{:S(2)}) async-start(bf16[4,8,48,128]{3,2,1,0:T(8,128)(2,1)} %shard_map.81), calls=%async_computation.3 | async-start | bytes 786432 | tf_op jit(solution)/shard_map/all_to_all | solution.py:190
  152.5 5.2 %all-to-all-done.3 = bf16[4,8,48,128]{3,2,1,0:T(8,128)(2,1)S(1)} async-done(((bf16[4,8,48,128]{3,2,1,0:T(8,128)(2,1)}), bf16[4,8,48,128]{3,2,1,0:T(8,128)(2,1)S(1)}, u32[]{:S(2)}, u32[]{:S(2)}) %all-to-all-start.3) | async-done | bytes 393248 | tf_op jit(solution)/shard_map/all_to_all | solution.py:190
  (53 shorter events, 25.7 us)
Async XLA Ops:
  0.6 18.9 %copy-start = (bf16[4096,128]{1,0:T(8,128)(2,1)S(1)}, bf16[4096,128]{1,0:T(8,128)(2,1)}, u32[]{:S(2)}) copy-start(bf16[4096,128]{1,0:T(8,128)(2,1)} %param.6) | copy-start | bytes 3145732
  3.6 30.0 %all-to-all-start = ((bf16[12,8,2048]{2,1,0:T(8,128)(2,1)}), bf16[12,8,2048]{2,1,0:T(8,128)(2,1)S(1)}, u32[]{:S(2)}, u32[]{:S(2)}) async-start(bf16[12,8,2048]{2,1,0:T(8,128)(2,1)} %bitcast.4), calls=%async_computation | async-start | bytes 786432 | tf_op jit(solution)/shard_map/all_to_all | solution.py:164
  17.5 3.8 %collective-permute-start = (bf16[2,1024,128]{2,1,0:T(8,128)(2,1)S(1)}, bf16[2,1024,128]{2,1,0:T(8,128)(2,1)S(1)}, u32[]{:S(2)}, u32[]{:S(2)}) collective-permute-start(bf16[2,1024,128]{2,1,0:T(8,128)(2,1)S(1)} %dynamic-slice_bitcast_fusion), channel_id=1, source_target_pairs={{0,192},{192,0},{1,193},{193,1},{2,194},{194,2},{3,195},{195,3},{4... | collective-permute-start | bytes 1572872 | tf_op jit(solution)/shard_map/ppermute | solution.py:24
  33.6 16.0 %copy-start.2 = (bf16[12,8,2048]{2,1,0:T(8,128)(2,1)}, bf16[12,8,2048]{2,1,0:T(8,128)(2,1)S(1)}, u32[]{:S(2)}) copy-start(bf16[12,8,2048]{2,1,0:T(8,128)(2,1)S(1)} %all-to-all-done) | copy-start | bytes 1179652
  35.2 51.1 %all-to-all-start.1 = ((bf16[4,2048,128]{2,1,0:T(8,128)(2,1)}), bf16[4,2048,128]{2,1,0:T(8,128)(2,1)S(1)}, u32[]{:S(2)}, u32[]{:S(2)}) async-start(bf16[4,2048,128]{2,1,0:T(8,128)(2,1)} %broadcast_in_dim.17), calls=%async_computation.1 | async-start | bytes 4194304 | tf_op jit(solution)/shard_map/all_to_all | solution.py:173
  38.9 25.2 %collective-permute-start.3 = (bf16[2,1024,128]{2,1,0:T(8,128)(2,1)}, bf16[2,1024,128]{2,1,0:T(8,128)(2,1)S(1)}, u32[]{:S(2)}, u32[]{:S(2)}) collective-permute-start(bf16[2,1024,128]{2,1,0:T(8,128)(2,1)} %get-tuple-element.24), channel_id=1, source_target_pairs={{0,96},{32,128},{64,160},{96,384},{128,416},{160,448},{192,672},{2... | collective-permute-start | bytes 1572872 | tf_op jit(solution)/shard_map/ppermute | solution.py:34
  46.4 17.7 %collective-permute-start.1 = (bf16[96,2048]{1,0:T(8,128)(2,1)S(1)}, bf16[96,2048]{1,0:T(8,128)(2,1)S(1)}, u32[]{:S(2)}, u32[]{:S(2)}) collective-permute-start(bf16[96,2048]{1,0:T(8,128)(2,1)S(1)} %bitcast.18), channel_id=1, source_target_pairs={{0,1},{1,2},{2,3},{3,4},{4,5},{5,6},{6,7},{7,0},{8,9},{9,10},{10,1... | collective-permute-start | bytes 1179656 | tf_op jit(solution)/shard_map/ppermute | solution.py:20
  49.6 14.5 %collective-permute-start.2 = (bf16[96,2048]{1,0:T(8,128)(2,1)S(1)}, bf16[96,2048]{1,0:T(8,128)(2,1)S(1)}, u32[]{:S(2)}, u32[]{:S(2)}) collective-permute-start(bf16[96,2048]{1,0:T(8,128)(2,1)S(1)} %bitcast.19), channel_id=1, source_target_pairs={{0,7},{1,0},{2,1},{3,2},{4,3},{5,4},{6,5},{7,6},{8,15},{9,8},{10,9... | collective-permute-start | bytes 1179656 | tf_op jit(solution)/shard_map/ppermute | solution.py:20
  64.1 21.5 %copy-start.5 = (bf16[96,2048]{1,0:T(8,128)(2,1)}, bf16[96,2048]{1,0:T(8,128)(2,1)S(1)}, u32[]{:S(2)}) copy-start(bf16[96,2048]{1,0:T(8,128)(2,1)S(1)} %collective-permute-done.1.refs_8_) | copy-start | bytes 1179652
  64.1 21.5 %copy-start.6 = (bf16[96,2048]{1,0:T(8,128)(2,1)}, bf16[96,2048]{1,0:T(8,128)(2,1)S(1)}, u32[]{:S(2)}) copy-start(bf16[96,2048]{1,0:T(8,128)(2,1)S(1)} %collective-permute-done.2.refs_1_) | copy-start | bytes 1179652
  64.1 22.3 %collective-permute-start.6 = (bf16[2,1024,128]{2,1,0:T(8,128)(2,1)S(1)}, bf16[2,1024,128]{2,1,0:T(8,128)(2,1)}, u32[]{:S(2)}, u32[]{:S(2)}) collective-permute-start(bf16[2,1024,128]{2,1,0:T(8,128)(2,1)S(1)} %collective-permute-done.3), channel_id=1, source_target_pairs={{0,96},{32,128},{64,160},{96,384},{128,416},{160,448},{192,672},{2... | collective-permute-start | bytes 1572872 | tf_op jit(solution)/shard_map/ppermute | solution.py:34
  71.1 12.9 %collective-permute-start.4 = (bf16[96,2048]{1,0:T(8,128)(2,1)S(1)}, bf16[96,2048]{1,0:T(8,128)(2,1)S(1)}, u32[]{:S(2)}, u32[]{:S(2)}) collective-permute-start(bf16[96,2048]{1,0:T(8,128)(2,1)S(1)} %collective-permute-done.1.refs_8_), channel_id=1, source_target_pairs={{0,1},{1,2},{2,3},{3,4},{4,5},{5,6},{6,7},{7,0},{8,9},{9,10},{10,1... | collective-permute-start | bytes 1179656 | tf_op jit(solution)/shard_map/ppermute | solution.py:20
  74.3 11.3 %collective-permute-start.5 = (bf16[96,2048]{1,0:T(8,128)(2,1)S(1)}, bf16[96,2048]{1,0:T(8,128)(2,1)S(1)}, u32[]{:S(2)}, u32[]{:S(2)}) collective-permute-start(bf16[96,2048]{1,0:T(8,128)(2,1)S(1)} %collective-permute-done.2.refs_1_), channel_id=1, source_target_pairs={{0,7},{1,0},{2,1},{3,2},{4,3},{5,4},{6,5},{7,6},{8,15},{9,8},{10,9... | collective-permute-start | bytes 1179656 | tf_op jit(solution)/shard_map/ppermute | solution.py:20
  84.0 15.6 %copy-start.7 = (bf16[96,2048]{1,0:T(8,128)(2,1)}, bf16[96,2048]{1,0:T(8,128)(2,1)S(1)}, u32[]{:S(2)}) copy-start(bf16[96,2048]{1,0:T(8,128)(2,1)S(1)} %collective-permute-done.4.refs_7_) | copy-start | bytes 1179652
  90.1 42.5 %all-to-all-start.2 = ((bf16[4,2048,128]{2,1,0:T(8,128)(2,1)}), bf16[4,2048,128]{2,1,0:T(8,128)(2,1)}, u32[]{:S(2)}, u32[]{:S(2)}) async-start(bf16[4,2048,128]{2,1,0:T(8,128)(2,1)} %bitcast.17), calls=%async_computation.2 | async-start | bytes 4194304 | tf_op jit(solution)/shard_map/all_to_all | solution.py:182
  94.6 13.9 %collective-permute-start.7 = (bf16[96,2048]{1,0:T(8,128)(2,1)}, bf16[96,2048]{1,0:T(8,128)(2,1)S(1)}, u32[]{:S(2)}, u32[]{:S(2)}) collective-permute-start(bf16[96,2048]{1,0:T(8,128)(2,1)} %copy-done.8), channel_id=1, source_target_pairs={{0,7},{1,0},{2,1},{3,2},{4,3},{5,4},{6,5},{7,6},{8,15},{9,8},{10,9... | collective-permute-start | bytes 1179656 | tf_op jit(solution)/shard_map/ppermute | solution.py:20
  99.5 14.3 %collective-permute-start.8 = (bf16[96,2048]{1,0:T(8,128)(2,1)S(1)}, bf16[96,2048]{1,0:T(8,128)(2,1)S(1)}, u32[]{:S(2)}, u32[]{:S(2)}) collective-permute-start(bf16[96,2048]{1,0:T(8,128)(2,1)S(1)} %collective-permute-done.4.refs_7_), channel_id=1, source_target_pairs={{0,1},{1,2},{2,3},{3,4},{4,5},{5,6},{6,7},{7,0},{8,9},{9,10},{10,1... | collective-permute-start | bytes 1179656 | tf_op jit(solution)/shard_map/ppermute | solution.py:20
  108.5 14.1 %copy-start.3 = (bf16[96,2048]{1,0:T(8,128)(2,1)}, bf16[96,2048]{1,0:T(8,128)(2,1)S(1)}, u32[]{:S(2)}) copy-start(bf16[96,2048]{1,0:T(8,128)(2,1)S(1)} %collective-permute-done.7.refs_3_) | copy-start | bytes 1179652
  108.5 9.0 %collective-permute-start.10 = (bf16[48,2048]{1,0:T(8,128)(2,1)S(1)}, bf16[48,2048]{1,0:T(8,128)(2,1)S(1)}, u32[]{:S(2)}, u32[]{:S(2)}) collective-permute-start(bf16[48,2048]{1,0:T(8,128)(2,1)S(1)} %slice.9), channel_id=1, source_target_pairs={{0,7},{1,0},{2,1},{3,2},{4,3},{5,4},{6,5},{7,6},{8,15},{9,8},{10,9... | collective-permute-start | bytes 589832 | tf_op jit(solution)/shard_map/ppermute | solution.py:20
  113.8 8.7 %copy-start.4 = (bf16[96,2048]{1,0:T(8,128)(2,1)}, bf16[96,2048]{1,0:T(8,128)(2,1)S(1)}, u32[]{:S(2)}) copy-start(bf16[96,2048]{1,0:T(8,128)(2,1)S(1)} %collective-permute-done.8.refs_6_) | copy-start | bytes 1179652
  113.9 8.7 %collective-permute-start.9 = (bf16[48,2048]{1,0:T(8,128)(2,1)S(1)}, bf16[48,2048]{1,0:T(8,128)(2,1)S(1)}, u32[]{:S(2)}, u32[]{:S(2)}) collective-permute-start(bf16[48,2048]{1,0:T(8,128)(2,1)S(1)} %slice.8), channel_id=1, source_target_pairs={{0,1},{1,2},{2,3},{3,4},{4,5},{5,6},{6,7},{7,0},{8,9},{9,10},{10,1... | collective-permute-start | bytes 589832 | tf_op jit(solution)/shard_map/ppermute | solution.py:20
  129.0 11.4 %collective-permute-start.11 = (bf16[8,48,512]{2,1,0:T(8,128)(2,1)}, bf16[8,48,512]{2,1,0:T(8,128)(2,1)S(1)}, u32[]{:S(2)}, u32[]{:S(2)}) collective-permute-start(bf16[8,48,512]{2,1,0:T(8,128)(2,1)} %get-tuple-element.38), channel_id=1, source_target_pairs={{0,192},{192,0},{1,193},{193,1},{2,194},{194,2},{3,195},{195,3},{4... | collective-permute-start | bytes 1179656 | tf_op jit(solution)/shard_map/ppermute | solution.py:24
  138.4 3.8 %collective-permute-start.12 = (bf16[8,48,512]{2,1,0:T(8,128)(2,1)}, bf16[8,48,512]{2,1,0:T(8,128)(2,1)S(1)}, u32[]{:S(2)}, u32[]{:S(2)}) collective-permute-start(bf16[8,48,512]{2,1,0:T(8,128)(2,1)} %get-tuple-element.42), channel_id=1, source_target_pairs={{0,192},{192,0},{1,193},{193,1},{2,194},{194,2},{3,195},{195,3},{4... | collective-permute-start | bytes 1179656 | tf_op jit(solution)/shard_map/ppermute | solution.py:24
  145.7 12.1 %all-to-all-start.3 = ((bf16[4,8,48,128]{3,2,1,0:T(8,128)(2,1)}), bf16[4,8,48,128]{3,2,1,0:T(8,128)(2,1)S(1)}, u32[]{:S(2)}, u32[]{:S(2)}) async-start(bf16[4,8,48,128]{3,2,1,0:T(8,128)(2,1)} %shard_map.81), calls=%async_computation.3 | async-start | bytes 786432 | tf_op jit(solution)/shard_map/all_to_all | solution.py:190
  (7 other events, 13.6 us)

commit v5 on v3

--- a/solution.py
+++ b/solution.py
@@ -11,7 +11,7 @@
 AXES = tuple(SIZES)
 BF, F32 = jnp.bfloat16, jnp.float32
 MIB = 1024 * 1024
-PARTS = 2
+PARTS = 1
 ROWS = 1024 // PARTS
 
 
@@ -22,6 +22,16 @@
 
 def flip(value, axis):
     return lax.ppermute(value, axis, [(0, 1), (1, 0)])
+
+
+def along(value, hops):
+    pairs = []
+    for zh in range(2):
+        for c in range(2):
+            for z in range(6):
+                to = (6 * zh + z + (hops if c == 0 else -hops)) % 12
+                pairs.append(((2 * zh + c) * 6 + z, (2 * (to // 6) + c) * 6 + to % 6))
+    return lax.ppermute(value, ("zh", "c", "z"), pairs)
 
 
 def after(value, *others):
@@ -84,33 +94,29 @@
         new_anchor[rows] = anchor[rows] - 0.7 * (mean_delta + 0.9 * moved)
 
 
-def product_body(spans, *refs):
-    tokens, weights = refs[:9], refs[9 : 9 + len(spans)]
-    keep, give, rows, columns, sems = refs[9 + len(spans) :]
-    c, y = lax.axis_index("c"), lax.axis_index("y")
-    weight_copies, token_copies = [], []
-    for pair in range(2):
-        for x in (2 * pair, 2 * pair + 1):
-            for source, runs in zip(weights, spans):
-                for at, row, length in runs:
-                    target = columns.at[pl.ds(at, length), pl.ds(128 * x, 128)]
-                    weight_copies.append((pair, source.at[x, pl.ds(row, length)], target))
-    for s, (piece, offset, length) in enumerate(
-        [(t, 96 * s, 96) for s, t in enumerate(tokens[:4])]
-        + [(tokens[4], 384, 48), (tokens[5], 432, 48)]
-        + [(t, 96 * s, 96) for s, t in zip((5, 6, 7), tokens[6:])]
-    ):
-        place = lax.rem(y + offset // 96, 8) * 96 + offset % 96
-        token_copies.append((0, piece, rows.at[pl.ds(pl.multiple_of(place, 16), length)]))
-    order = [w for w in weight_copies if w[0] == 0] + token_copies + [w for w in weight_copies if w[0] == 1]
+def product_body(*refs):
+    tokens, weights = refs[:9], refs[9:-5]
+    keep, give, rows, columns, sems = refs[-5:]
+    c, x, y = lax.axis_index("c"), lax.axis_index("x"), lax.axis_index("y")
     copies = []
-    for i, (pair, source, target) in enumerate(order):
+    if len(weights) == 4:
+        for j, source in enumerate(weights):
+            copies.append((0, source, columns.at[:, pl.ds(pl.multiple_of(128 * lax.rem(x + j, 4), 128), 128)]))
+    else:
+        for j in range(4):
+            copies.append((j // 2, weights[0].at[j], columns.at[:, pl.ds(128 * j, 128)]))
+    for piece, at, length in zip(tokens, (0, 96, 192, 288, 384, 432, 480, 576, 672), (96, 96, 96, 96, 48, 48, 96, 96, 96)):
+        place = lax.rem(y + at // 96, 8) * 96 + at % 96
+        copies.append((0, piece, rows.at[pl.ds(pl.multiple_of(place, 16), length)]))
+    copies.sort(key=lambda entry: entry[0])
+    started = []
+    for i, (stage, source, target) in enumerate(copies):
         copy = pltpu.make_async_copy(source, target, sems.at[i])
         copy.start()
-        copies.append((pair, copy))
+        started.append((stage, copy))
     for pair in range(2):
-        for at, copy in copies:
-            if at == pair:
+        for stage, copy in started:
+            if stage == pair:
                 copy.wait()
         span = slice(256 * pair, 256 * pair + 256)
         for half in range(2):
@@ -121,14 +127,13 @@
                 give[4 * half + s, :, span] = jnp.where(c == 0, high, low).astype(BF)
 
 
-def product(spans, tokens, weights):
-    count = 9 + 4 * sum(len(s) for s in spans)
+def product(tokens, weights):
     return call(
-        functools.partial(product_body, spans),
+        product_body,
         [*tokens, *weights],
         [like((8, 48, 512), F32), like((8, 48, 512), BF)],
         True,
-        [pltpu.VMEM((768, 2048), BF), pltpu.VMEM((2048, 512), BF), pltpu.SemaphoreType.DMA((count,))],
+        [pltpu.VMEM((768, 2048), BF), pltpu.VMEM((2048, 512), BF), pltpu.SemaphoreType.DMA((13,))],
     )
 
 
@@ -155,32 +160,27 @@
     cut = jnp.transpose(tokens[0].reshape(8, 2, 2, 1024), (2, 0, 1, 3)).reshape(2, 1, 8, 2048)
     cut = jnp.broadcast_to(cut, (2, 6, 8, 2048)).reshape(12, 8, 2048)
     six = lax.all_to_all(cut, ("c", "z"), 0, 0).reshape(96, 2048)
-    six = after(six, parts[0])
-    own = lax.dynamic_index_in_dim(gate_weight.reshape(2, 2, 1024, 128), c, 1, keepdims=False).reshape(1, 2048, 128)
-    own = after(jnp.broadcast_to(own, (4, 2048, 128)), six)
+    own = lax.dynamic_index_in_dim(gate_weight.reshape(2, 2, 1024, 128), c, 1, keepdims=False).reshape(2048, 128)
 
-    def update(part):
-        (up,) = call(functools.partial(update_body, part), [backs[part], half_done, other], [like((4, 2, ROWS, 128), BF)])
-        return up.reshape(4, 2 * ROWS, 128)
-
-    first = [shift(six, "y", by) for by in (2, -2, 1, -1)] + [flip(parts[0], "zh")]
-    f2, b2, f1, b1, back, gate_all = lax.optimization_barrier((*first, lax.all_to_all(own, "x", 0, 0)))
-    backs = [back]
-    second = [shift(f1, "y", 2), shift(b1, "y", -2), shift(f2[:48], "y", 2), shift(b2[48:], "y", -2), flip(parts[1], "zh")]
-    f3, b3, f4, b4, back, up = lax.optimization_barrier((*second, lax.all_to_all(update(0), "x", 0, 0)))
-    backs.append(back)
-    ups = [up, lax.all_to_all(update(1), "x", 0, 0)]
+    back = along(parts[0], 3)
+    six, back = lax.optimization_barrier((six, back))
+    first = (shift(six, "y", 1), shift(six, "y", -1), along(back, 3), shift(own, "x", -1), shift(own, "x", 1))
+    f1, b1, back, g1, g3 = lax.optimization_barrier(first)
+    (up,) = call(functools.partial(update_body, 0), [back, half_done, other], [like((4, 2, 1024, 128), BF)])
+    up_all = lax.all_to_all(up.reshape(4, 2048, 128), "x", 0, 0)
+    f2, b2, g2 = lax.optimization_barrier((shift(f1, "y", 1), shift(b1, "y", -1), shift(own, "x", 2)))
+    f3, b3 = shift(f2, "y", 1), shift(b2, "y", -1)
+    f4, b4 = shift(f2[:48], "y", 2), shift(b2[48:], "y", -2)
     pieces = [six, b1, b2, b3, f4, b4, f3, f2, f1]
-    gate, gate_give = product((((0, 0, 2048),),), pieces, [gate_all])
+    gate, gate_give = product(pieces, [own, g1, g2, g3])
     gate_got = flip(gate_give, "c")
-    spans = tuple(((ROWS * p, 0, ROWS), (1024 + ROWS * p, ROWS, ROWS)) for p in range(PARTS))
-    up, up_give = product(spans, pieces, ups)
+    up, up_give = product(pieces, [up_all])
     up_got = flip(up_give, "c")
 
     (hidden,) = call(gated_body, [gate, gate_got, up, up_got], [like((4, 8, 48, 128), BF)])
     hidden = lax.all_to_all(hidden, "x", 0, 0)
     hidden = jnp.transpose(hidden.reshape(4, 8, 6, 8, 128), (2, 0, 1, 3, 4)).reshape(1, 1536, 128)
-    new_anchor, new_momentum = call(outer_body, [*backs, mine, anchor, momentum], [like((1024, 128), F32)] * 2)
+    new_anchor, new_momentum = call(outer_body, [back, mine, anchor, momentum], [like((1024, 128), F32)] * 2)
     return new_anchor, new_momentum, hidden
 
 

time: 175 us -> 185 us (1.057)
  the two profiles are of different devices: /device:TPU:72 before, /device:TPU:1 now
where the time goes in v5:
time: 185 us; the launch traced here: 182 us
  starting transfers between devices  84.5 us (46%)
  waiting for transfers between devices  65.1 us (35%)
  Pallas kernels  21.9 us (12%)
  local copies, waits for them, and re-layouts  9.88 us (5%)
    ppermute x11, waiting for transfers between devices, shift(): return lax.ppermute(value, axis, [(i, (i + by) % n) for i in range(n)])  43.4 us
    ppermute x11, starting transfers between devices, shift(): return lax.ppermute(value, axis, [(i, (i + by) % n) for i in range(n)])  39.6 us
    pallas_call x6, Pallas kernels, call(): pl.pallas_call(body, out_shape=outs, grid=(1,), in_specs=[pl.BlockSpec(me...  21.9 us
    ppermute x2, starting transfers between devices, along(): return lax.ppermute(value, ('zh', 'c', 'z'), pairs)  16.5 us
    all_to_all x1, starting transfers between devices, per_device(): six = lax.all_to_all(cut, ('c', 'z'), 0, 0).reshape(96, 2048)  14 us
    ppermute x2, waiting for transfers between devices, along(): return lax.ppermute(value, ('zh', 'c', 'z'), pairs)  12.6 us
    ppermute x3, starting transfers between devices, flip(): return lax.ppermute(value, axis, [(0, 1), (1, 0)])  6.75 us
    unnamed x36, local copies, waits for them, and re-layouts  6.06 us
  transfers between devices with their start and end apart: 19, of which 9 were waited for; matrix products, arithmetic and copies ran while one was open for 0% of the time, Pallas kernels for 9%

profile of v5, /device:TPU:1, one launch (start us, length us, event | category | flops | bytes accessed | tf_op | source)
XLA Modules:
  0.0 182.4 jit_solution(2616021915613575051)
XLA Ops:
  3.6 14.0 %all-to-all-start = ((bf16[12,8,2048]{2,1,0:T(8,128)(2,1)}), bf16[12,8,2048]{2,1,0:T(8,128)(2,1)S(1)}, u32[]{:S(2)}, u32[]{:S(2)}) async-start(bf16[12,8,2048]{2,1,0:T(8,128)(2,1)} %bitcast.4), calls=%async_computation | async-start | bytes 786432 | tf_op jit(solution)/shard_map/all_to_all | solution.py:162
  22.1 3.1 %shard_map.76 = (bf16[2,1024,128]{2,1,0:T(8,128)(2,1)}, f32[1024,128]{1,0:T(8,128)}, f32[1024,128]{1,0:T(8,128)}, f32[1024,128]{1,0:T(8,128)}) custom-call(bf16[2,2,1024,128]{3,2,1,0:T(8,128)(2,1)} %bitcast.25, bf16[2,1024,128]{2,1,0:T(8,128)(2,1)} %copy-done.15, f32[1024,128]{1,0:T(8,128)} %refs_2_.1, f32[1024,128]{1,0:T(8,128)} %refs_3_.1), custom_call_target="tpu_custom_call" | custom-call | bytes 1024 | tf_op jit(solution)/shard_map/pallas_call | solution.py:50
  25.2 9.6 %collective-permute-start.1 = (bf16[2,1024,128]{2,1,0:T(8,128)(2,1)}, bf16[2,1024,128]{2,1,0:T(8,128)(2,1)S(1)}, u32[]{:S(2)}, u32[]{:S(2)}) collective-permute-start(bf16[2,1024,128]{2,1,0:T(8,128)(2,1)} %get-tuple-element.25), channel_id=1, source_target_pairs={{0,96},{32,128},{64,160},{96,384},{128,416},{160,448},{192,672},{2... | collective-permute-start | bytes 1572872 | tf_op jit(solution)/shard_map/ppermute | solution.py:34
  34.9 4.4 %collective-permute-start.5 = (bf16[2048,128]{1,0:T(8,128)(2,1)S(1)}, bf16[2048,128]{1,0:T(8,128)(2,1)S(1)}, u32[]{:S(2)}, u32[]{:S(2)}) collective-permute-start(bf16[2048,128]{1,0:T(8,128)(2,1)S(1)} %bitcast.26), channel_id=1, source_target_pairs={{0,24},{8,0},{16,8},{24,16},{1,25},{9,1},{17,9},{25,17},{2,26},{10... | collective-permute-start | bytes 1572872 | tf_op jit(solution)/shard_map/ppermute | solution.py:20
  41.2 11.3 %collective-permute-done.1 = bf16[2,1024,128]{2,1,0:T(8,128)(2,1)S(1)} collective-permute-done((bf16[2,1024,128]{2,1,0:T(8,128)(2,1)}, bf16[2,1024,128]{2,1,0:T(8,128)(2,1)S(1)}, u32[]{:S(2)}, u32[]{:S(2)}) %collective-permute-start.1) | collective-permute-done | bytes 524320 | tf_op jit(solution)/shard_map/ppermute | solution.py:34
  52.5 6.9 %collective-permute-start.4 = (bf16[2,1024,128]{2,1,0:T(8,128)(2,1)S(1)}, bf16[2,1024,128]{2,1,0:T(8,128)(2,1)S(1)}, u32[]{:S(2)}, u32[]{:S(2)}) collective-permute-start(bf16[2,1024,128]{2,1,0:T(8,128)(2,1)S(1)} %collective-permute-done.1), channel_id=1, source_target_pairs={{0,96},{32,128},{64,160},{96,384},{128,416},{160,448},{192,672},{2... | collective-permute-start | bytes 1572872 | tf_op jit(solution)/shard_map/ppermute | solution.py:34
  59.5 3.2 %collective-permute-start.2 = (bf16[96,2048]{1,0:T(8,128)(2,1)S(1)}, bf16[96,2048]{1,0:T(8,128)(2,1)S(1)}, u32[]{:S(2)}, u32[]{:S(2)}) collective-permute-start(bf16[96,2048]{1,0:T(8,128)(2,1)S(1)} %bitcast.20), channel_id=1, source_target_pairs={{0,1},{1,2},{2,3},{3,4},{4,5},{5,6},{6,7},{7,0},{8,9},{9,10},{10,1... | collective-permute-start | bytes 1179656 | tf_op jit(solution)/shard_map/ppermute | solution.py:20
  62.7 3.8 %collective-permute-start.3 = (bf16[96,2048]{1,0:T(8,128)(2,1)S(1)}, bf16[96,2048]{1,0:T(8,128)(2,1)S(1)}, u32[]{:S(2)}, u32[]{:S(2)}) collective-permute-start(bf16[96,2048]{1,0:T(8,128)(2,1)S(1)} %bitcast.21), channel_id=1, source_target_pairs={{0,7},{1,0},{2,1},{3,2},{4,3},{5,4},{6,5},{7,6},{8,15},{9,8},{10,9... | collective-permute-start | bytes 1179656 | tf_op jit(solution)/shard_map/ppermute | solution.py:20
  66.5 5.8 %collective-permute-done.2.refs_8_ = bf16[96,2048]{1,0:T(8,128)(2,1)S(1)} collective-permute-done((bf16[96,2048]{1,0:T(8,128)(2,1)S(1)}, bf16[96,2048]{1,0:T(8,128)(2,1)S(1)}, u32[]{:S(2)}, u32[]{:S(2)}) %collective-permute-start.2) | collective-permute-done | bytes 393248 | tf_op jit(solution)/shard_map/ppermute | solution.py:20
  76.2 2.9 %shard_map.79 = bf16[4,2,1024,128]{3,2,1,0:T(8,128)(2,1)} custom-call(bf16[2,1024,128]{2,1,0:T(8,128)(2,1)} %copy-done.6, f32[1024,128]{1,0:T(8,128)} %get-tuple-element.41.half_done, f32[1024,128]{1,0:T(8,128)} %get-tuple-element.42.other), custom_call_target="tpu_custom_call" | custom-call | bytes 1024 | tf_op jit(solution)/shard_map/pallas_call | solution.py:50
  79.2 4.2 %all-to-all-start.1 = ((bf16[4,2048,128]{2,1,0:T(8,128)(2,1)}), bf16[4,2048,128]{2,1,0:T(8,128)(2,1)S(1)}, u32[]{:S(2)}, u32[]{:S(2)}) async-start(bf16[4,2048,128]{2,1,0:T(8,128)(2,1)} %bitcast.19), calls=%async_computation.1 | async-start | bytes 4194304 | tf_op jit(solution)/shard_map/all_to_all | solution.py:170
  83.4 4.9 %collective-permute-start.9 = (bf16[2048,128]{1,0:T(8,128)(2,1)}, bf16[2048,128]{1,0:T(8,128)(2,1)S(1)}, u32[]{:S(2)}, u32[]{:S(2)}) collective-permute-start(bf16[2048,128]{1,0:T(8,128)(2,1)} %bitcast.28), channel_id=1, source_target_pairs={{0,16},{8,24},{16,0},{24,8},{1,17},{9,25},{17,1},{25,9},{2,18},{10... | collective-permute-start | bytes 1572872 | tf_op jit(solution)/shard_map/ppermute | solution.py:20
  88.3 3.2 %collective-permute-start.7 = (bf16[96,2048]{1,0:T(8,128)(2,1)}, bf16[96,2048]{1,0:T(8,128)(2,1)S(1)}, u32[]{:S(2)}, u32[]{:S(2)}) collective-permute-start(bf16[96,2048]{1,0:T(8,128)(2,1)} %copy-done.7), channel_id=1, source_target_pairs={{0,1},{1,2},{2,3},{3,4},{4,5},{5,6},{6,7},{7,0},{8,9},{9,10},{10,1... | collective-permute-start | bytes 1179656 | tf_op jit(solution)/shard_map/ppermute | solution.py:20
  91.5 3.8 %collective-permute-start.8 = (bf16[96,2048]{1,0:T(8,128)(2,1)}, bf16[96,2048]{1,0:T(8,128)(2,1)S(1)}, u32[]{:S(2)}, u32[]{:S(2)}) collective-permute-start(bf16[96,2048]{1,0:T(8,128)(2,1)} %copy-done.8), channel_id=1, source_target_pairs={{0,7},{1,0},{2,1},{3,2},{4,3},{5,4},{6,5},{7,6},{8,15},{9,8},{10,9... | collective-permute-start | bytes 1179656 | tf_op jit(solution)/shard_map/ppermute | solution.py:20
  95.3 24.8 %collective-permute-done.9.refs_11_ = bf16[2048,128]{1,0:T(8,128)(2,1)S(1)} collective-permute-done((bf16[2048,128]{1,0:T(8,128)(2,1)}, bf16[2048,128]{1,0:T(8,128)(2,1)S(1)}, u32[]{:S(2)}, u32[]{:S(2)}) %collective-permute-start.9) | collective-permute-done | bytes 524320 | tf_op jit(solution)/shard_map/ppermute | solution.py:20
  120.9 5.1 %collective-permute-start.10 = (bf16[96,2048]{1,0:T(8,128)(2,1)S(1)}, bf16[96,2048]{1,0:T(8,128)(2,1)S(1)}, u32[]{:S(2)}, u32[]{:S(2)}) collective-permute-start(bf16[96,2048]{1,0:T(8,128)(2,1)S(1)} %collective-permute-done.8.refs_2_), channel_id=1, source_target_pairs={{0,7},{1,0},{2,1},{3,2},{4,3},{5,4},{6,5},{7,6},{8,15},{9,8},{10,9... | collective-permute-start | bytes 1179656 | tf_op jit(solution)/shard_map/ppermute | solution.py:20
  128.0 4.7 %collective-permute-start.11 = (bf16[48,2048]{1,0:T(8,128)(2,1)S(1)}, bf16[48,2048]{1,0:T(8,128)(2,1)S(1)}, u32[]{:S(2)}, u32[]{:S(2)}) collective-permute-start(bf16[48,2048]{1,0:T(8,128)(2,1)S(1)} %slice.6), channel_id=1, source_target_pairs={{0,2},{1,3},{2,4},{3,5},{4,6},{5,7},{6,0},{7,1},{8,10},{9,11},{10,... | collective-permute-start | bytes 589832 | tf_op jit(solution)/shard_map/ppermute | solution.py:20
  132.7 2.7 %collective-permute-start.12 = (bf16[48,2048]{1,0:T(8,128)(2,1)S(1)}, bf16[48,2048]{1,0:T(8,128)(2,1)S(1)}, u32[]{:S(2)}, u32[]{:S(2)}) collective-permute-start(bf16[48,2048]{1,0:T(8,128)(2,1)S(1)} %slice.7), channel_id=1, source_target_pairs={{0,6},{1,7},{2,0},{3,1},{4,2},{5,3},{6,4},{7,5},{8,14},{9,15},{10,... | collective-permute-start | bytes 589832 | tf_op jit(solution)/shard_map/ppermute | solution.py:20
  135.4 11.1 %collective-permute-done.11.refs_4_ = bf16[48,2048]{1,0:T(8,128)(2,1)S(1)} collective-permute-done((bf16[48,2048]{1,0:T(8,128)(2,1)S(1)}, bf16[48,2048]{1,0:T(8,128)(2,1)S(1)}, u32[]{:S(2)}, u32[]{:S(2)}) %collective-permute-start.11) | collective-permute-done | bytes 196640 | tf_op jit(solution)/shard_map/ppermute | solution.py:20
  148.0 5.4 %shard_map.78 = (f32[8,48,512]{2,1,0:T(8,128)}, bf16[8,48,512]{2,1,0:T(8,128)(2,1)}) custom-call(bf16[96,2048]{1,0:T(8,128)(2,1)} %bitcast.22, bf16[96,2048]{1,0:T(8,128)(2,1)} %copy-done.8, bf16[96,2048]{1,0:T(8,128)(2,1)} %copy-done.4, bf16[96,2048]{1,0:T(8,128)(2,1)} %copy-done.9, bf16[48,2048]{1,0:T(8,128)(2,1)} %copy-done.10, ...), custom_call_target="tpu_custom_call" | custom-call | bytes 1024 | tf_op jit(solution)/shard_map/pallas_call | solution.py:50
  153.4 2.8 %collective-permute-start.14 = (bf16[8,48,512]{2,1,0:T(8,128)(2,1)}, bf16[8,48,512]{2,1,0:T(8,128)(2,1)S(1)}, u32[]{:S(2)}, u32[]{:S(2)}) collective-permute-start(bf16[8,48,512]{2,1,0:T(8,128)(2,1)} %get-tuple-element.40), channel_id=1, source_target_pairs={{0,192},{192,0},{1,193},{193,1},{2,194},{194,2},{3,195},{195,3},{4... | collective-permute-start | bytes 1179656 | tf_op jit(solution)/shard_map/ppermute | solution.py:24
  157.6 5.2 %shard_map.80 = (f32[8,48,512]{2,1,0:T(8,128)}, bf16[8,48,512]{2,1,0:T(8,128)(2,1)}) custom-call(bf16[96,2048]{1,0:T(8,128)(2,1)} %bitcast.23, bf16[96,2048]{1,0:T(8,128)(2,1)} %copy-done.8, bf16[96,2048]{1,0:T(8,128)(2,1)} %copy-done.4, bf16[96,2048]{1,0:T(8,128)(2,1)} %copy-done.9, bf16[48,2048]{1,0:T(8,128)(2,1)} %copy-done.10, ...), custom_call_target="tpu_custom_call" | custom-call | bytes 1024 | tf_op jit(solution)/shard_map/pallas_call | solution.py:50
  170.0 3.5 %all-to-all-start.2 = ((bf16[4,8,48,128]{3,2,1,0:T(8,128)(2,1)}), bf16[4,8,48,128]{3,2,1,0:T(8,128)(2,1)S(1)}, u32[]{:S(2)}, u32[]{:S(2)}) async-start(bf16[4,8,48,128]{3,2,1,0:T(8,128)(2,1)} %shard_map.81), calls=%async_computation.2 | async-start | bytes 786432 | tf_op jit(solution)/shard_map/all_to_all | solution.py:181
  176.1 5.4 %all-to-all-done.2 = bf16[4,8,48,128]{3,2,1,0:T(8,128)(2,1)S(1)} async-done(((bf16[4,8,48,128]{3,2,1,0:T(8,128)(2,1)}), bf16[4,8,48,128]{3,2,1,0:T(8,128)(2,1)S(1)}, u32[]{:S(2)}, u32[]{:S(2)}) %all-to-all-start.2) | async-done | bytes 393248 | tf_op jit(solution)/shard_map/all_to_all | solution.py:181
  (64 shorter events, 29.6 us)
Async XLA Ops:
  0.6 34.2 %copy-start = (bf16[4096,128]{1,0:T(8,128)(2,1)S(1)}, bf16[4096,128]{1,0:T(8,128)(2,1)}, u32[]{:S(2)}) copy-start(bf16[4096,128]{1,0:T(8,128)(2,1)} %param.6) | copy-start | bytes 3145732
  3.6 49.0 %all-to-all-start = ((bf16[12,8,2048]{2,1,0:T(8,128)(2,1)}), bf16[12,8,2048]{2,1,0:T(8,128)(2,1)S(1)}, u32[]{:S(2)}, u32[]{:S(2)}) async-start(bf16[12,8,2048]{2,1,0:T(8,128)(2,1)} %bitcast.4), calls=%async_computation | async-start | bytes 786432 | tf_op jit(solution)/shard_map/all_to_all | solution.py:162
  17.5 3.8 %collective-permute-start = (bf16[2,1024,128]{2,1,0:T(8,128)(2,1)S(1)}, bf16[2,1024,128]{2,1,0:T(8,128)(2,1)S(1)}, u32[]{:S(2)}, u32[]{:S(2)}) collective-permute-start(bf16[2,1024,128]{2,1,0:T(8,128)(2,1)S(1)} %dynamic-slice_bitcast_fusion), channel_id=1, source_target_pairs={{0,192},{192,0},{1,193},{193,1},{2,194},{194,2},{3,195},{195,3},{4... | collective-permute-start | bytes 1572872 | tf_op jit(solution)/shard_map/ppermute | solution.py:24
  25.2 27.3 %collective-permute-start.1 = (bf16[2,1024,128]{2,1,0:T(8,128)(2,1)}, bf16[2,1024,128]{2,1,0:T(8,128)(2,1)S(1)}, u32[]{:S(2)}, u32[]{:S(2)}) collective-permute-start(bf16[2,1024,128]{2,1,0:T(8,128)(2,1)} %get-tuple-element.25), channel_id=1, source_target_pairs={{0,96},{32,128},{64,160},{96,384},{128,416},{160,448},{192,672},{2... | collective-permute-start | bytes 1572872 | tf_op jit(solution)/shard_map/ppermute | solution.py:34
  34.9 44.3 %copy-start.5 = (bf16[2,1,1024,128]{3,2,1,0:T(8,128)(2,1)}, bf16[2,1,1024,128]{3,2,1,0:T(8,128)(2,1)S(1)}, u32[]{:S(2)}) copy-start(bf16[2,1,1024,128]{3,2,1,0:T(8,128)(2,1)S(1)} %constant_dynamic-slice_fusion) | copy-start | bytes 1572868
  34.9 31.6 %collective-permute-start.5 = (bf16[2048,128]{1,0:T(8,128)(2,1)S(1)}, bf16[2048,128]{1,0:T(8,128)(2,1)S(1)}, u32[]{:S(2)}, u32[]{:S(2)}) collective-permute-start(bf16[2048,128]{1,0:T(8,128)(2,1)S(1)} %bitcast.26), channel_id=1, source_target_pairs={{0,24},{8,0},{16,8},{24,16},{1,25},{9,1},{17,9},{25,17},{2,26},{10... | collective-permute-start | bytes 1572872 | tf_op jit(solution)/shard_map/ppermute | solution.py:20
  39.3 27.2 %collective-permute-start.6 = (bf16[2048,128]{1,0:T(8,128)(2,1)S(1)}, bf16[2048,128]{1,0:T(8,128)(2,1)S(1)}, u32[]{:S(2)}, u32[]{:S(2)}) collective-permute-start(bf16[2048,128]{1,0:T(8,128)(2,1)S(1)} %bitcast.27), channel_id=1, source_target_pairs={{0,8},{8,16},{16,24},{24,0},{1,9},{9,17},{17,25},{25,1},{2,10},{10... | collective-permute-start | bytes 1572872 | tf_op jit(solution)/shard_map/ppermute | solution.py:20
  52.5 26.7 %copy-start.2 = (bf16[12,8,2048]{2,1,0:T(8,128)(2,1)}, bf16[12,8,2048]{2,1,0:T(8,128)(2,1)S(1)}, u32[]{:S(2)}) copy-start(bf16[12,8,2048]{2,1,0:T(8,128)(2,1)S(1)} %all-to-all-done) | copy-start | bytes 1179652
  52.5 22.9 %collective-permute-start.4 = (bf16[2,1024,128]{2,1,0:T(8,128)(2,1)S(1)}, bf16[2,1024,128]{2,1,0:T(8,128)(2,1)S(1)}, u32[]{:S(2)}, u32[]{:S(2)}) collective-permute-start(bf16[2,1024,128]{2,1,0:T(8,128)(2,1)S(1)} %collective-permute-done.1), channel_id=1, source_target_pairs={{0,96},{32,128},{64,160},{96,384},{128,416},{160,448},{192,672},{2... | collective-permute-start | bytes 1572872 | tf_op jit(solution)/shard_map/ppermute | solution.py:34
  59.5 12.9 %collective-permute-start.2 = (bf16[96,2048]{1,0:T(8,128)(2,1)S(1)}, bf16[96,2048]{1,0:T(8,128)(2,1)S(1)}, u32[]{:S(2)}, u32[]{:S(2)}) collective-permute-start(bf16[96,2048]{1,0:T(8,128)(2,1)S(1)} %bitcast.20), channel_id=1, source_target_pairs={{0,1},{1,2},{2,3},{3,4},{4,5},{5,6},{6,7},{7,0},{8,9},{9,10},{10,1... | collective-permute-start | bytes 1179656 | tf_op jit(solution)/shard_map/ppermute | solution.py:20
  62.7 11.4 %collective-permute-start.3 = (bf16[96,2048]{1,0:T(8,128)(2,1)S(1)}, bf16[96,2048]{1,0:T(8,128)(2,1)S(1)}, u32[]{:S(2)}, u32[]{:S(2)}) collective-permute-start(bf16[96,2048]{1,0:T(8,128)(2,1)S(1)} %bitcast.21), channel_id=1, source_target_pairs={{0,7},{1,0},{2,1},{3,2},{4,3},{5,4},{6,5},{7,6},{8,15},{9,8},{10,9... | collective-permute-start | bytes 1179656 | tf_op jit(solution)/shard_map/ppermute | solution.py:20
  79.2 77.1 %all-to-all-start.1 = ((bf16[4,2048,128]{2,1,0:T(8,128)(2,1)}), bf16[4,2048,128]{2,1,0:T(8,128)(2,1)S(1)}, u32[]{:S(2)}, u32[]{:S(2)}) async-start(bf16[4,2048,128]{2,1,0:T(8,128)(2,1)} %bitcast.19), calls=%async_computation.1 | async-start | bytes 4194304 | tf_op jit(solution)/shard_map/all_to_all | solution.py:170
  83.4 36.7 %collective-permute-start.9 = (bf16[2048,128]{1,0:T(8,128)(2,1)}, bf16[2048,128]{1,0:T(8,128)(2,1)S(1)}, u32[]{:S(2)}, u32[]{:S(2)}) collective-permute-start(bf16[2048,128]{1,0:T(8,128)(2,1)} %bitcast.28), channel_id=1, source_target_pairs={{0,16},{8,24},{16,0},{24,8},{1,17},{9,25},{17,1},{25,9},{2,18},{10... | collective-permute-start | bytes 1572872 | tf_op jit(solution)/shard_map/ppermute | solution.py:20
  88.3 31.8 %collective-permute-start.7 = (bf16[96,2048]{1,0:T(8,128)(2,1)}, bf16[96,2048]{1,0:T(8,128)(2,1)S(1)}, u32[]{:S(2)}, u32[]{:S(2)}) collective-permute-start(bf16[96,2048]{1,0:T(8,128)(2,1)} %copy-done.7), channel_id=1, source_target_pairs={{0,1},{1,2},{2,3},{3,4},{4,5},{5,6},{6,7},{7,0},{8,9},{9,10},{10,1... | collective-permute-start | bytes 1179656 | tf_op jit(solution)/shard_map/ppermute | solution.py:20
  91.5 28.6 %collective-permute-start.8 = (bf16[96,2048]{1,0:T(8,128)(2,1)}, bf16[96,2048]{1,0:T(8,128)(2,1)S(1)}, u32[]{:S(2)}, u32[]{:S(2)}) collective-permute-start(bf16[96,2048]{1,0:T(8,128)(2,1)} %copy-done.8), channel_id=1, source_target_pairs={{0,7},{1,0},{2,1},{3,2},{4,3},{5,4},{6,5},{7,6},{8,15},{9,8},{10,9... | collective-permute-start | bytes 1179656 | tf_op jit(solution)/shard_map/ppermute | solution.py:20
  120.1 27.9 %copy-start.3 = (bf16[96,2048]{1,0:T(8,128)(2,1)}, bf16[96,2048]{1,0:T(8,128)(2,1)S(1)}, u32[]{:S(2)}) copy-start(bf16[96,2048]{1,0:T(8,128)(2,1)S(1)} %collective-permute-done.7.refs_7_) | copy-start | bytes 1179652
  120.9 27.1 %copy-start.4 = (bf16[96,2048]{1,0:T(8,128)(2,1)}, bf16[96,2048]{1,0:T(8,128)(2,1)S(1)}, u32[]{:S(2)}) copy-start(bf16[96,2048]{1,0:T(8,128)(2,1)S(1)} %collective-permute-done.8.refs_2_) | copy-start | bytes 1179652
  120.9 25.6 %collective-permute-start.10 = (bf16[96,2048]{1,0:T(8,128)(2,1)S(1)}, bf16[96,2048]{1,0:T(8,128)(2,1)S(1)}, u32[]{:S(2)}, u32[]{:S(2)}) collective-permute-start(bf16[96,2048]{1,0:T(8,128)(2,1)S(1)} %collective-permute-done.8.refs_2_), channel_id=1, source_target_pairs={{0,7},{1,0},{2,1},{3,2},{4,3},{5,4},{6,5},{7,6},{8,15},{9,8},{10,9... | collective-permute-start | bytes 1179656 | tf_op jit(solution)/shard_map/ppermute | solution.py:20
  126.0 22.0 %collective-permute-start.13 = (bf16[96,2048]{1,0:T(8,128)(2,1)S(1)}, bf16[96,2048]{1,0:T(8,128)(2,1)}, u32[]{:S(2)}, u32[]{:S(2)}) collective-permute-start(bf16[96,2048]{1,0:T(8,128)(2,1)S(1)} %collective-permute-done.7.refs_7_), channel_id=1, source_target_pairs={{0,1},{1,2},{2,3},{3,4},{4,5},{5,6},{6,7},{7,0},{8,9},{9,10},{10,1... | collective-permute-start | bytes 1179656 | tf_op jit(solution)/shard_map/ppermute | solution.py:20
  128.0 18.5 %collective-permute-start.11 = (bf16[48,2048]{1,0:T(8,128)(2,1)S(1)}, bf16[48,2048]{1,0:T(8,128)(2,1)S(1)}, u32[]{:S(2)}, u32[]{:S(2)}) collective-permute-start(bf16[48,2048]{1,0:T(8,128)(2,1)S(1)} %slice.6), channel_id=1, source_target_pairs={{0,2},{1,3},{2,4},{3,5},{4,6},{5,7},{6,0},{7,1},{8,10},{9,11},{10,... | collective-permute-start | bytes 589832 | tf_op jit(solution)/shard_map/ppermute | solution.py:20
  132.7 13.8 %collective-permute-start.12 = (bf16[48,2048]{1,0:T(8,128)(2,1)S(1)}, bf16[48,2048]{1,0:T(8,128)(2,1)S(1)}, u32[]{:S(2)}, u32[]{:S(2)}) collective-permute-start(bf16[48,2048]{1,0:T(8,128)(2,1)S(1)} %slice.7), channel_id=1, source_target_pairs={{0,6},{1,7},{2,0},{3,1},{4,2},{5,3},{6,4},{7,5},{8,14},{9,15},{10,... | collective-permute-start | bytes 589832 | tf_op jit(solution)/shard_map/ppermute | solution.py:20
  153.4 11.3 %collective-permute-start.14 = (bf16[8,48,512]{2,1,0:T(8,128)(2,1)}, bf16[8,48,512]{2,1,0:T(8,128)(2,1)S(1)}, u32[]{:S(2)}, u32[]{:S(2)}) collective-permute-start(bf16[8,48,512]{2,1,0:T(8,128)(2,1)} %get-tuple-element.40), channel_id=1, source_target_pairs={{0,192},{192,0},{1,193},{193,1},{2,194},{194,2},{3,195},{195,3},{4... | collective-permute-start | bytes 1179656 | tf_op jit(solution)/shard_map/ppermute | solution.py:24
  162.8 3.8 %collective-permute-start.15 = (bf16[8,48,512]{2,1,0:T(8,128)(2,1)}, bf16[8,48,512]{2,1,0:T(8,128)(2,1)S(1)}, u32[]{:S(2)}, u32[]{:S(2)}) collective-permute-start(bf16[8,48,512]{2,1,0:T(8,128)(2,1)} %get-tuple-element.44), channel_id=1, source_target_pairs={{0,192},{192,0},{1,193},{193,1},{2,194},{194,2},{3,195},{195,3},{4... | collective-permute-start | bytes 1179656 | tf_op jit(solution)/shard_map/ppermute | solution.py:24
  170.0 11.5 %all-to-all-start.2 = ((bf16[4,8,48,128]{3,2,1,0:T(8,128)(2,1)}), bf16[4,8,48,128]{3,2,1,0:T(8,128)(2,1)S(1)}, u32[]{:S(2)}, u32[]{:S(2)}) async-start(bf16[4,8,48,128]{3,2,1,0:T(8,128)(2,1)} %shard_map.81), calls=%async_computation.2 | async-start | bytes 786432 | tf_op jit(solution)/shard_map/all_to_all | solution.py:181
  (13 other events, 38.3 us)

commit v6 on v5

--- a/solution.py
+++ b/solution.py
@@ -95,53 +95,51 @@
 
 
 def product_body(*refs):
-    tokens, weights = refs[:9], refs[9:-5]
-    keep, give, rows, columns, sems = refs[-5:]
-    c, x, y = lax.axis_index("c"), lax.axis_index("x"), lax.axis_index("y")
-    copies = []
-    if len(weights) == 4:
-        for j, source in enumerate(weights):
-            copies.append((0, source, columns.at[:, pl.ds(pl.multiple_of(128 * lax.rem(x + j, 4), 128), 128)]))
-    else:
-        for j in range(4):
-            copies.append((j // 2, weights[0].at[j], columns.at[:, pl.ds(128 * j, 128)]))
+    tokens, weights = refs[:9], refs[9:11]
+    keep, give, rows, columns, sems = refs[11:]
+    c, y = lax.axis_index("c"), lax.axis_index("y")
+    sources = []
     for piece, at, length in zip(tokens, (0, 96, 192, 288, 384, 432, 480, 576, 672), (96, 96, 96, 96, 48, 48, 96, 96, 96)):
         place = lax.rem(y + at // 96, 8) * 96 + at % 96
-        copies.append((0, piece, rows.at[pl.ds(pl.multiple_of(place, 16), length)]))
-    copies.sort(key=lambda entry: entry[0])
-    started = []
-    for i, (stage, source, target) in enumerate(copies):
+        sources.append((0, piece, rows.at[pl.ds(pl.multiple_of(place, 16), length)]))
+    for kind in range(2):
+        for x in range(4):
+            target = columns.at[kind, :, pl.ds(128 * x, 128)]
+            sources.append((2 * kind + x // 2, weights[kind].at[x], target))
+    copies = []
+    for i, (stage, source, target) in enumerate(sources):
         copy = pltpu.make_async_copy(source, target, sems.at[i])
         copy.start()
-        started.append((stage, copy))
-    for pair in range(2):
-        for stage, copy in started:
-            if stage == pair:
+        copies.append((stage, copy))
+    for stage in range(4):
+        for at, copy in copies:
+            if at == stage:
                 copy.wait()
+        kind, pair = stage // 2, stage % 2
         span = slice(256 * pair, 256 * pair + 256)
         for half in range(2):
-            total = jnp.dot(rows[384 * half : 384 * half + 384], columns[:, span], preferred_element_type=F32)
+            total = jnp.dot(rows[384 * half : 384 * half + 384], columns[kind, :, span], preferred_element_type=F32)
             for s in range(4):
                 low, high = total[96 * s : 96 * s + 48], total[96 * s + 48 : 96 * s + 96]
-                keep[4 * half + s, :, span] = jnp.where(c == 0, low, high)
-                give[4 * half + s, :, span] = jnp.where(c == 0, high, low).astype(BF)
+                keep[kind, 4 * half + s, :, span] = jnp.where(c == 0, low, high).astype(BF)
+                give[kind, 4 * half + s, :, span] = jnp.where(c == 0, high, low).astype(BF)
 
 
-def product(tokens, weights):
+def product(tokens, gate, up):
     return call(
         product_body,
-        [*tokens, *weights],
-        [like((8, 48, 512), F32), like((8, 48, 512), BF)],
+        [*tokens, gate, up],
+        [like((2, 8, 48, 512), BF)] * 2,
         True,
-        [pltpu.VMEM((768, 2048), BF), pltpu.VMEM((2048, 512), BF), pltpu.SemaphoreType.DMA((13,))],
+        [pltpu.VMEM((768, 2048), BF), pltpu.VMEM((2, 2048, 512), BF), pltpu.SemaphoreType.DMA((17,))],
     )
 
 
-def gated_body(gate, gate_got, up, up_got, hidden):
+def gated_body(keep, got, hidden):
     for x in range(4):
         columns = slice(128 * x, 128 * x + 128)
-        g = gate[:, :, columns] + gate_got[:, :, columns].astype(F32)
-        u = up[:, :, columns] + up_got[:, :, columns].astype(F32)
+        g = keep[0, :, :, columns].astype(F32) + got[0, :, :, columns].astype(F32)
+        u = keep[1, :, :, columns].astype(F32) + got[1, :, :, columns].astype(F32)
         hidden[x] = (g / (1.0 + jnp.exp(-g)) * u).astype(BF)
 
 
@@ -160,24 +158,19 @@
     cut = jnp.transpose(tokens[0].reshape(8, 2, 2, 1024), (2, 0, 1, 3)).reshape(2, 1, 8, 2048)
     cut = jnp.broadcast_to(cut, (2, 6, 8, 2048)).reshape(12, 8, 2048)
     six = lax.all_to_all(cut, ("c", "z"), 0, 0).reshape(96, 2048)
-    own = lax.dynamic_index_in_dim(gate_weight.reshape(2, 2, 1024, 128), c, 1, keepdims=False).reshape(2048, 128)
+    own = lax.dynamic_index_in_dim(gate_weight.reshape(2, 2, 1024, 128), c, 1, keepdims=False).reshape(1, 2048, 128)
+    own = jnp.broadcast_to(own, (4, 2048, 128))
 
-    back = along(parts[0], 3)
-    six, back = lax.optimization_barrier((six, back))
-    first = (shift(six, "y", 1), shift(six, "y", -1), along(back, 3), shift(own, "x", -1), shift(own, "x", 1))
-    f1, b1, back, g1, g3 = lax.optimization_barrier(first)
+    back = along(parts[0], 1)
+    six, back, own = lax.optimization_barrier((six, back, own))
+    first = [along(back, 5)] + [shift(six, "y", by) for by in (2, -2, 1, -1)]
+    back, f2, b2, f1, b1, gate_all = lax.optimization_barrier((*first, lax.all_to_all(own, "x", 0, 0)))
     (up,) = call(functools.partial(update_body, 0), [back, half_done, other], [like((4, 2, 1024, 128), BF)])
     up_all = lax.all_to_all(up.reshape(4, 2048, 128), "x", 0, 0)
-    f2, b2, g2 = lax.optimization_barrier((shift(f1, "y", 1), shift(b1, "y", -1), shift(own, "x", 2)))
-    f3, b3 = shift(f2, "y", 1), shift(b2, "y", -1)
+    f3, b3 = shift(f1, "y", 2), shift(b1, "y", -2)
     f4, b4 = shift(f2[:48], "y", 2), shift(b2[48:], "y", -2)
-    pieces = [six, b1, b2, b3, f4, b4, f3, f2, f1]
-    gate, gate_give = product(pieces, [own, g1, g2, g3])
-    gate_got = flip(gate_give, "c")
-    up, up_give = product(pieces, [up_all])
-    up_got = flip(up_give, "c")
-
-    (hidden,) = call(gated_body, [gate, gate_got, up, up_got], [like((4, 8, 48, 128), BF)])
+    keep, give = product([six, b1, b2, b3, f4, b4, f3, f2, f1], gate_all, up_all)
+    (hidden,) = call(gated_body, [keep, flip(give, "c")], [like((4, 8, 48, 128), BF)])
     hidden = lax.all_to_all(hidden, "x", 0, 0)
     hidden = jnp.transpose(hidden.reshape(4, 8, 6, 8, 128), (2, 0, 1, 3, 4)).reshape(1, 1536, 128)
     new_anchor, new_momentum = call(outer_body, [back, mine, anchor, momentum], [like((1024, 128), F32)] * 2)

time: 185 us -> 163 us (0.88)
  the two profiles are of different devices: /device:TPU:1 before, /device:TPU:16 now
where the time goes in v6:
time: 163 us; the launch traced here: 162 us
  starting transfers between devices  66.4 us (41%)
  waiting for transfers between devices  65.4 us (40%)
  Pallas kernels  19.3 us (12%)
  local copies, waits for them, and re-layouts  9.75 us (6%)
    ppermute x8, waiting for transfers between devices, shift(): return lax.ppermute(value, axis, [(i, (i + by) % n) for i in range(n)])  41.7 us
    ppermute x8, starting transfers between devices, shift(): return lax.ppermute(value, axis, [(i, (i + by) % n) for i in range(n)])  29.5 us
    pallas_call x5, Pallas kernels, call(): pl.pallas_call(body, out_shape=outs, grid=(1,), in_specs=[pl.BlockSpec(me...  19.3 us
    ppermute x2, waiting for transfers between devices, along(): return lax.ppermute(value, ('zh', 'c', 'z'), pairs)  14 us
    all_to_all x1, starting transfers between devices, per_device(): six = lax.all_to_all(cut, ('c', 'z'), 0, 0).reshape(96, 2048)  12.1 us
    ppermute x2, starting transfers between devices, along(): return lax.ppermute(value, ('zh', 'c', 'z'), pairs)  6.51 us
    all_to_all x1, waiting for transfers between devices, per_device(): hidden = lax.all_to_all(hidden, 'x', 0, 0)  5.79 us
    all_to_all x1, starting transfers between devices, per_device(): up_all = lax.all_to_all(up.reshape(4, 2048, 128), 'x', 0, 0)  4.93 us
  transfers between devices with their start and end apart: 16, of which 10 were waited for; matrix products, arithmetic and copies ran while one was open for 1% of the time, Pallas kernels for 4%

profile of v6, /device:TPU:16, one launch (start us, length us, event | category | flops | bytes accessed | tf_op | source)
XLA Modules:
  0.0 161.6 jit_solution(3621065618239769051)
XLA Ops:
  3.6 12.1 %all-to-all-start = ((bf16[12,8,2048]{2,1,0:T(8,128)(2,1)}), bf16[12,8,2048]{2,1,0:T(8,128)(2,1)S(1)}, u32[]{:S(2)}, u32[]{:S(2)}) async-start(bf16[12,8,2048]{2,1,0:T(8,128)(2,1)} %bitcast.4), calls=%async_computation | async-start | bytes 786432 | tf_op jit(solution)/shard_map/all_to_all | solution.py:160
  20.4 3.1 %shard_map.76 = (bf16[2,1024,128]{2,1,0:T(8,128)(2,1)}, f32[1024,128]{1,0:T(8,128)}, f32[1024,128]{1,0:T(8,128)}, f32[1024,128]{1,0:T(8,128)}) custom-call(bf16[2,2,1024,128]{3,2,1,0:T(8,128)(2,1)} %bitcast.19, bf16[2,1024,128]{2,1,0:T(8,128)(2,1)} %copy-done.7, f32[1024,128]{1,0:T(8,128)} %refs_2_.1, f32[1024,128]{1,0:T(8,128)} %refs_3_.1), custom_call_target="tpu_custom_call" | custom-call | bytes 1024 | tf_op jit(solution)/shard_map/pallas_call | solution.py:50
  23.5 3.8 %collective-permute-start.1 = (bf16[2,1024,128]{2,1,0:T(8,128)(2,1)}, bf16[2,1024,128]{2,1,0:T(8,128)(2,1)S(1)}, u32[]{:S(2)}, u32[]{:S(2)}) collective-permute-start(bf16[2,1024,128]{2,1,0:T(8,128)(2,1)} %get-tuple-element.22), channel_id=1, source_target_pairs={{0,32},{32,64},{64,96},{96,128},{128,160},{160,384},{192,736},{224... | collective-permute-start | bytes 1572872 | tf_op jit(solution)/shard_map/ppermute | solution.py:34
  27.3 14.0 %collective-permute-done.1 = bf16[2,1024,128]{2,1,0:T(8,128)(2,1)S(1)} collective-permute-done((bf16[2,1024,128]{2,1,0:T(8,128)(2,1)}, bf16[2,1024,128]{2,1,0:T(8,128)(2,1)S(1)}, u32[]{:S(2)}, u32[]{:S(2)}) %collective-permute-start.1) | collective-permute-done | bytes 524320 | tf_op jit(solution)/shard_map/ppermute | solution.py:34
  43.0 4.3 %all-to-all-start.1 = ((bf16[4,2048,128]{2,1,0:T(8,128)(2,1)}), bf16[4,2048,128]{2,1,0:T(8,128)(2,1)S(1)}, u32[]{:S(2)}, u32[]{:S(2)}) async-start(bf16[4,2048,128]{2,1,0:T(8,128)(2,1)} %broadcast_in_dim.17), calls=%async_computation.1 | async-start | bytes 4194304 | tf_op jit(solution)/shard_map/all_to_all | solution.py:167
  47.3 2.7 %collective-permute-start.2 = (bf16[2,1024,128]{2,1,0:T(8,128)(2,1)}, bf16[2,1024,128]{2,1,0:T(8,128)(2,1)}, u32[]{:S(2)}, u32[]{:S(2)}) collective-permute-start(bf16[2,1024,128]{2,1,0:T(8,128)(2,1)} %copy-done.14), channel_id=1, source_target_pairs={{0,160},{32,384},{64,416},{96,448},{128,480},{160,512},{192,608},{... | collective-permute-start | bytes 1572872 | tf_op jit(solution)/shard_map/ppermute | solution.py:34
  50.0 5.7 %collective-permute-start.3 = (bf16[96,2048]{1,0:T(8,128)(2,1)S(1)}, bf16[96,2048]{1,0:T(8,128)(2,1)S(1)}, u32[]{:S(2)}, u32[]{:S(2)}) collective-permute-start(bf16[96,2048]{1,0:T(8,128)(2,1)S(1)} %bitcast.21), channel_id=1, source_target_pairs={{0,2},{1,3},{2,4},{3,5},{4,6},{5,7},{6,0},{7,1},{8,10},{9,11},{10,... | collective-permute-start | bytes 1179656 | tf_op jit(solution)/shard_map/ppermute | solution.py:20
  57.6 2.6 %collective-permute-start.5 = (bf16[96,2048]{1,0:T(8,128)(2,1)S(1)}, bf16[96,2048]{1,0:T(8,128)(2,1)S(1)}, u32[]{:S(2)}, u32[]{:S(2)}) collective-permute-start(bf16[96,2048]{1,0:T(8,128)(2,1)S(1)} %bitcast.23), channel_id=1, source_target_pairs={{0,1},{1,2},{2,3},{3,4},{4,5},{5,6},{6,7},{7,0},{8,9},{9,10},{10,1... | collective-permute-start | bytes 1179656 | tf_op jit(solution)/shard_map/ppermute | solution.py:20
  60.3 3.2 %collective-permute-start.6 = (bf16[96,2048]{1,0:T(8,128)(2,1)S(1)}, bf16[96,2048]{1,0:T(8,128)(2,1)S(1)}, u32[]{:S(2)}, u32[]{:S(2)}) collective-permute-start(bf16[96,2048]{1,0:T(8,128)(2,1)S(1)} %bitcast.24), channel_id=1, source_target_pairs={{0,7},{1,0},{2,1},{3,2},{4,3},{5,4},{6,5},{7,6},{8,15},{9,8},{10,9... | collective-permute-start | bytes 1179656 | tf_op jit(solution)/shard_map/ppermute | solution.py:20
  63.5 8.4 %collective-permute-done.3.refs_7_ = bf16[96,2048]{1,0:T(8,128)(2,1)S(1)} collective-permute-done((bf16[96,2048]{1,0:T(8,128)(2,1)S(1)}, bf16[96,2048]{1,0:T(8,128)(2,1)S(1)}, u32[]{:S(2)}, u32[]{:S(2)}) %collective-permute-start.3) | collective-permute-done | bytes 393248 | tf_op jit(solution)/shard_map/ppermute | solution.py:20
  71.9 6.3 %collective-permute-done.4.refs_2_ = bf16[96,2048]{1,0:T(8,128)(2,1)S(1)} collective-permute-done((bf16[96,2048]{1,0:T(8,128)(2,1)S(1)}, bf16[96,2048]{1,0:T(8,128)(2,1)S(1)}, u32[]{:S(2)}, u32[]{:S(2)}) %collective-permute-start.4) | collective-permute-done | bytes 393248 | tf_op jit(solution)/shard_map/ppermute | solution.py:20
  78.2 3.3 %collective-permute-done.5.refs_8_ = bf16[96,2048]{1,0:T(8,128)(2,1)S(1)} collective-permute-done((bf16[96,2048]{1,0:T(8,128)(2,1)S(1)}, bf16[96,2048]{1,0:T(8,128)(2,1)S(1)}, u32[]{:S(2)}, u32[]{:S(2)}) %collective-permute-start.5) | collective-permute-done | bytes 393248 | tf_op jit(solution)/shard_map/ppermute | solution.py:20
  84.5 3.7 %shard_map.78 = bf16[4,2,1024,128]{3,2,1,0:T(8,128)(2,1)} custom-call(bf16[2,1024,128]{2,1,0:T(8,128)(2,1)} %collective-permute-done.2.refs_0_.back, f32[1024,128]{1,0:T(8,128)} %get-tuple-element.35.half_done, f32[1024,128]{1,0:T(8,128)} %get-tuple-element.36.other), custom_call_target="tpu_custom_call" | custom-call | bytes 1024 | tf_op jit(solution)/shard_map/pallas_call | solution.py:50
  88.2 4.9 %all-to-all-start.2 = ((bf16[4,2048,128]{2,1,0:T(8,128)(2,1)}), bf16[4,2048,128]{2,1,0:T(8,128)(2,1)}, u32[]{:S(2)}, u32[]{:S(2)}) async-start(bf16[4,2048,128]{2,1,0:T(8,128)(2,1)} %bitcast.17), calls=%async_computation.2 | async-start | bytes 4194304 | tf_op jit(solution)/shard_map/all_to_all | solution.py:169
  93.2 6.1 %collective-permute-start.10 = (bf16[96,2048]{1,0:T(8,128)(2,1)}, bf16[96,2048]{1,0:T(8,128)(2,1)S(1)}, u32[]{:S(2)}, u32[]{:S(2)}) collective-permute-start(bf16[96,2048]{1,0:T(8,128)(2,1)} %copy-done.8), channel_id=1, source_target_pairs={{0,2},{1,3},{2,4},{3,5},{4,6},{5,7},{6,0},{7,1},{8,10},{9,11},{10,... | collective-permute-start | bytes 1179656 | tf_op jit(solution)/shard_map/ppermute | solution.py:20
  101.3 6.0 %collective-permute-start.8 = (bf16[48,2048]{1,0:T(8,128)(2,1)S(1)}, bf16[48,2048]{1,0:T(8,128)(2,1)S(1)}, u32[]{:S(2)}, u32[]{:S(2)}) collective-permute-start(bf16[48,2048]{1,0:T(8,128)(2,1)S(1)} %slice.6), channel_id=1, source_target_pairs={{0,2},{1,3},{2,4},{3,5},{4,6},{5,7},{6,0},{7,1},{8,10},{9,11},{10,... | collective-permute-start | bytes 589832 | tf_op jit(solution)/shard_map/ppermute | solution.py:20
  110.2 15.2 %collective-permute-done.8.refs_4_ = bf16[48,2048]{1,0:T(8,128)(2,1)S(1)} collective-permute-done((bf16[48,2048]{1,0:T(8,128)(2,1)S(1)}, bf16[48,2048]{1,0:T(8,128)(2,1)S(1)}, u32[]{:S(2)}, u32[]{:S(2)}) %collective-permute-start.8) | collective-permute-done | bytes 196640 | tf_op jit(solution)/shard_map/ppermute | solution.py:20
  125.4 6.2 %collective-permute-done.9.refs_5_ = bf16[48,2048]{1,0:T(8,128)(2,1)S(1)} collective-permute-done((bf16[48,2048]{1,0:T(8,128)(2,1)S(1)}, bf16[48,2048]{1,0:T(8,128)(2,1)S(1)}, u32[]{:S(2)}, u32[]{:S(2)}) %collective-permute-start.9) | collective-permute-done | bytes 196640 | tf_op jit(solution)/shard_map/ppermute | solution.py:20
  132.5 7.4 %shard_map.79 = (bf16[2,8,48,512]{3,2,1,0:T(8,128)(2,1)}, bf16[2,8,48,512]{3,2,1,0:T(8,128)(2,1)}) custom-call(bf16[96,2048]{1,0:T(8,128)(2,1)} %bitcast.25, bf16[96,2048]{1,0:T(8,128)(2,1)} %copy-done.9, bf16[96,2048]{1,0:T(8,128)(2,1)} %copy-done.5, bf16[96,2048]{1,0:T(8,128)(2,1)} %copy-done.11, bf16[48,2048]{1,0:T(8,128)(2,1)} %copy-done.12, ...), custom_call_target="tpu_custom_call" | custom-call | bytes 1024 | tf_op jit(solution)/shard_map/pallas_call | solution.py:50
  141.9 2.5 %collective-permute-done.11.got = bf16[2,8,48,512]{3,2,1,0:T(8,128)(2,1)S(1)} collective-permute-done((bf16[2,8,48,512]{3,2,1,0:T(8,128)(2,1)}, bf16[2,8,48,512]{3,2,1,0:T(8,128)(2,1)S(1)}, u32[]{:S(2)}, u32[]{:S(2)}) %collective-permute-start.11) | collective-permute-done | bytes 786464 | tf_op jit(solution)/shard_map/ppermute | solution.py:24
  145.2 2.5 %shard_map.80 = bf16[4,8,48,128]{3,2,1,0:T(8,128)(2,1)} custom-call(bf16[2,8,48,512]{3,2,1,0:T(8,128)(2,1)} %get-tuple-element.37.keep, bf16[2,8,48,512]{3,2,1,0:T(8,128)(2,1)} %copy-done.6), custom_call_target="tpu_custom_call" | custom-call | bytes 1024 | tf_op jit(solution)/shard_map/pallas_call | solution.py:50
  147.7 4.7 %all-to-all-start.3 = ((bf16[4,8,48,128]{3,2,1,0:T(8,128)(2,1)}), bf16[4,8,48,128]{3,2,1,0:T(8,128)(2,1)S(1)}, u32[]{:S(2)}, u32[]{:S(2)}) async-start(bf16[4,8,48,128]{3,2,1,0:T(8,128)(2,1)} %shard_map.80), calls=%async_computation.3 | async-start | bytes 786432 | tf_op jit(solution)/shard_map/all_to_all | solution.py:174
  152.4 2.6 %shard_map.77 = (f32[1024,128]{1,0:T(8,128)}, f32[1024,128]{1,0:T(8,128)}) custom-call(bf16[2,1024,128]{2,1,0:T(8,128)(2,1)} %collective-permute-done.2.refs_0_.back, f32[1024,128]{1,0:T(8,128)} %get-tuple-element.27.refs_1_, f32[1024,128]{1,0:T(8,128)} %refs_2_.1, f32[1024,128]{1,0:T(8,128)} %refs_3_.1), custom_call_target="tpu_custom_call" | custom-call | bytes 1024 | tf_op jit(solution)/shard_map/pallas_call | solution.py:50
  155.0 5.8 %all-to-all-done.3 = bf16[4,8,48,128]{3,2,1,0:T(8,128)(2,1)S(1)} async-done(((bf16[4,8,48,128]{3,2,1,0:T(8,128)(2,1)}), bf16[4,8,48,128]{3,2,1,0:T(8,128)(2,1)S(1)}, u32[]{:S(2)}, u32[]{:S(2)}) %all-to-all-start.3) | async-done | bytes 393248 | tf_op jit(solution)/shard_map/all_to_all | solution.py:174
  (52 shorter events, 23.6 us)
Async XLA Ops:
  0.6 26.7 %copy-start = (bf16[4096,128]{1,0:T(8,128)(2,1)S(1)}, bf16[4096,128]{1,0:T(8,128)(2,1)}, u32[]{:S(2)}) copy-start(bf16[4096,128]{1,0:T(8,128)(2,1)} %param.6) | copy-start | bytes 3145732
  3.6 37.8 %all-to-all-start = ((bf16[12,8,2048]{2,1,0:T(8,128)(2,1)}), bf16[12,8,2048]{2,1,0:T(8,128)(2,1)S(1)}, u32[]{:S(2)}, u32[]{:S(2)}) async-start(bf16[12,8,2048]{2,1,0:T(8,128)(2,1)} %bitcast.4), calls=%async_computation | async-start | bytes 786432 | tf_op jit(solution)/shard_map/all_to_all | solution.py:160
  15.7 3.9 %collective-permute-start = (bf16[2,1024,128]{2,1,0:T(8,128)(2,1)S(1)}, bf16[2,1024,128]{2,1,0:T(8,128)(2,1)S(1)}, u32[]{:S(2)}, u32[]{:S(2)}) collective-permute-start(bf16[2,1024,128]{2,1,0:T(8,128)(2,1)S(1)} %dynamic-slice_bitcast_fusion), channel_id=1, source_target_pairs={{0,192},{192,0},{1,193},{193,1},{2,194},{194,2},{3,195},{195,3},{4... | collective-permute-start | bytes 1572872 | tf_op jit(solution)/shard_map/ppermute | solution.py:24
  23.5 17.8 %collective-permute-start.1 = (bf16[2,1024,128]{2,1,0:T(8,128)(2,1)}, bf16[2,1024,128]{2,1,0:T(8,128)(2,1)S(1)}, u32[]{:S(2)}, u32[]{:S(2)}) collective-permute-start(bf16[2,1024,128]{2,1,0:T(8,128)(2,1)} %get-tuple-element.22), channel_id=1, source_target_pairs={{0,32},{32,64},{64,96},{96,128},{128,160},{160,384},{192,736},{224... | collective-permute-start | bytes 1572872 | tf_op jit(solution)/shard_map/ppermute | solution.py:34
  41.3 18.9 %copy-start.2 = (bf16[12,8,2048]{2,1,0:T(8,128)(2,1)}, bf16[12,8,2048]{2,1,0:T(8,128)(2,1)S(1)}, u32[]{:S(2)}) copy-start(bf16[12,8,2048]{2,1,0:T(8,128)(2,1)S(1)} %all-to-all-done) | copy-start | bytes 1179652
  43.0 41.6 %all-to-all-start.1 = ((bf16[4,2048,128]{2,1,0:T(8,128)(2,1)}), bf16[4,2048,128]{2,1,0:T(8,128)(2,1)S(1)}, u32[]{:S(2)}, u32[]{:S(2)}) async-start(bf16[4,2048,128]{2,1,0:T(8,128)(2,1)} %broadcast_in_dim.17), calls=%async_computation.1 | async-start | bytes 4194304 | tf_op jit(solution)/shard_map/all_to_all | solution.py:167
  47.3 37.3 %collective-permute-start.2 = (bf16[2,1024,128]{2,1,0:T(8,128)(2,1)}, bf16[2,1024,128]{2,1,0:T(8,128)(2,1)}, u32[]{:S(2)}, u32[]{:S(2)}) collective-permute-start(bf16[2,1024,128]{2,1,0:T(8,128)(2,1)} %copy-done.14), channel_id=1, source_target_pairs={{0,160},{32,384},{64,416},{96,448},{128,480},{160,512},{192,608},{... | collective-permute-start | bytes 1572872 | tf_op jit(solution)/shard_map/ppermute | solution.py:34
  50.0 21.9 %collective-permute-start.3 = (bf16[96,2048]{1,0:T(8,128)(2,1)S(1)}, bf16[96,2048]{1,0:T(8,128)(2,1)S(1)}, u32[]{:S(2)}, u32[]{:S(2)}) collective-permute-start(bf16[96,2048]{1,0:T(8,128)(2,1)S(1)} %bitcast.21), channel_id=1, source_target_pairs={{0,2},{1,3},{2,4},{3,5},{4,6},{5,7},{6,0},{7,1},{8,10},{9,11},{10,... | collective-permute-start | bytes 1179656 | tf_op jit(solution)/shard_map/ppermute | solution.py:20
  55.7 22.5 %collective-permute-start.4 = (bf16[96,2048]{1,0:T(8,128)(2,1)S(1)}, bf16[96,2048]{1,0:T(8,128)(2,1)S(1)}, u32[]{:S(2)}, u32[]{:S(2)}) collective-permute-start(bf16[96,2048]{1,0:T(8,128)(2,1)S(1)} %bitcast.22), channel_id=1, source_target_pairs={{0,6},{1,7},{2,0},{3,1},{4,2},{5,3},{6,4},{7,5},{8,14},{9,15},{10,... | collective-permute-start | bytes 1179656 | tf_op jit(solution)/shard_map/ppermute | solution.py:20
  57.6 23.9 %collective-permute-start.5 = (bf16[96,2048]{1,0:T(8,128)(2,1)S(1)}, bf16[96,2048]{1,0:T(8,128)(2,1)S(1)}, u32[]{:S(2)}, u32[]{:S(2)}) collective-permute-start(bf16[96,2048]{1,0:T(8,128)(2,1)S(1)} %bitcast.23), channel_id=1, source_target_pairs={{0,1},{1,2},{2,3},{3,4},{4,5},{5,6},{6,7},{7,0},{8,9},{9,10},{10,1... | collective-permute-start | bytes 1179656 | tf_op jit(solution)/shard_map/ppermute | solution.py:20
  60.3 23.5 %collective-permute-start.6 = (bf16[96,2048]{1,0:T(8,128)(2,1)S(1)}, bf16[96,2048]{1,0:T(8,128)(2,1)S(1)}, u32[]{:S(2)}, u32[]{:S(2)}) collective-permute-start(bf16[96,2048]{1,0:T(8,128)(2,1)S(1)} %bitcast.24), channel_id=1, source_target_pairs={{0,7},{1,0},{2,1},{3,2},{4,3},{5,4},{6,5},{7,6},{8,15},{9,8},{10,9... | collective-permute-start | bytes 1179656 | tf_op jit(solution)/shard_map/ppermute | solution.py:20
  71.9 11.9 %copy-start.3 = (bf16[96,2048]{1,0:T(8,128)(2,1)}, bf16[96,2048]{1,0:T(8,128)(2,1)S(1)}, u32[]{:S(2)}) copy-start(bf16[96,2048]{1,0:T(8,128)(2,1)S(1)} %collective-permute-done.3.refs_7_) | copy-start | bytes 1179652
  78.2 5.6 %copy-start.5 = (bf16[96,2048]{1,0:T(8,128)(2,1)}, bf16[96,2048]{1,0:T(8,128)(2,1)S(1)}, u32[]{:S(2)}) copy-start(bf16[96,2048]{1,0:T(8,128)(2,1)S(1)} %collective-permute-done.4.refs_2_) | copy-start | bytes 1179652
  81.5 2.3 %copy-start.8 = (bf16[96,2048]{1,0:T(8,128)(2,1)}, bf16[96,2048]{1,0:T(8,128)(2,1)S(1)}, u32[]{:S(2)}) copy-start(bf16[96,2048]{1,0:T(8,128)(2,1)S(1)} %collective-permute-done.5.refs_8_) | copy-start | bytes 1179652
  84.5 3.7 %copy-start.1 = (bf16[4,2048,128]{2,1,0:T(8,128)(2,1)}, bf16[4,2048,128]{2,1,0:T(8,128)(2,1)S(1)}, u32[]{:S(2)}) copy-start(bf16[4,2048,128]{2,1,0:T(8,128)(2,1)S(1)} %all-to-all-done.1.refs_9_) | copy-start | bytes 6291460
  88.2 13.0 %copy-start.4 = (bf16[96,2048]{1,0:T(8,128)(2,1)S(1)}, bf16[96,2048]{1,0:T(8,128)(2,1)}, u32[]{:S(2)}) copy-start(bf16[96,2048]{1,0:T(8,128)(2,1)} %copy-done.3) | copy-start | bytes 1179652
  88.2 43.4 %all-to-all-start.2 = ((bf16[4,2048,128]{2,1,0:T(8,128)(2,1)}), bf16[4,2048,128]{2,1,0:T(8,128)(2,1)}, u32[]{:S(2)}, u32[]{:S(2)}) async-start(bf16[4,2048,128]{2,1,0:T(8,128)(2,1)} %bitcast.17), calls=%async_computation.2 | async-start | bytes 4194304 | tf_op jit(solution)/shard_map/all_to_all | solution.py:169
  93.2 38.4 %collective-permute-start.10 = (bf16[96,2048]{1,0:T(8,128)(2,1)}, bf16[96,2048]{1,0:T(8,128)(2,1)S(1)}, u32[]{:S(2)}, u32[]{:S(2)}) collective-permute-start(bf16[96,2048]{1,0:T(8,128)(2,1)} %copy-done.8), channel_id=1, source_target_pairs={{0,2},{1,3},{2,4},{3,5},{4,6},{5,7},{6,0},{7,1},{8,10},{9,11},{10,... | collective-permute-start | bytes 1179656 | tf_op jit(solution)/shard_map/ppermute | solution.py:20
  99.3 32.3 %collective-permute-start.7 = (bf16[96,2048]{1,0:T(8,128)(2,1)}, bf16[96,2048]{1,0:T(8,128)(2,1)S(1)}, u32[]{:S(2)}, u32[]{:S(2)}) collective-permute-start(bf16[96,2048]{1,0:T(8,128)(2,1)} %copy-done.9), channel_id=1, source_target_pairs={{0,6},{1,7},{2,0},{3,1},{4,2},{5,3},{6,4},{7,5},{8,14},{9,15},{10,... | collective-permute-start | bytes 1179656 | tf_op jit(solution)/shard_map/ppermute | solution.py:20
  101.3 24.1 %collective-permute-start.8 = (bf16[48,2048]{1,0:T(8,128)(2,1)S(1)}, bf16[48,2048]{1,0:T(8,128)(2,1)S(1)}, u32[]{:S(2)}, u32[]{:S(2)}) collective-permute-start(bf16[48,2048]{1,0:T(8,128)(2,1)S(1)} %slice.6), channel_id=1, source_target_pairs={{0,2},{1,3},{2,4},{3,5},{4,6},{5,7},{6,0},{7,1},{8,10},{9,11},{10,... | collective-permute-start | bytes 589832 | tf_op jit(solution)/shard_map/ppermute | solution.py:20
  108.3 23.3 %collective-permute-start.9 = (bf16[48,2048]{1,0:T(8,128)(2,1)S(1)}, bf16[48,2048]{1,0:T(8,128)(2,1)S(1)}, u32[]{:S(2)}, u32[]{:S(2)}) collective-permute-start(bf16[48,2048]{1,0:T(8,128)(2,1)S(1)} %slice.7), channel_id=1, source_target_pairs={{0,6},{1,7},{2,0},{3,1},{4,2},{5,3},{6,4},{7,5},{8,14},{9,15},{10,... | collective-permute-start | bytes 589832 | tf_op jit(solution)/shard_map/ppermute | solution.py:20
  125.4 6.3 %copy-start.12 = (bf16[48,2048]{1,0:T(8,128)(2,1)}, bf16[48,2048]{1,0:T(8,128)(2,1)S(1)}, u32[]{:S(2)}) copy-start(bf16[48,2048]{1,0:T(8,128)(2,1)S(1)} %collective-permute-done.8.refs_4_) | copy-start | bytes 589828
  139.9 4.4 %collective-permute-start.11 = (bf16[2,8,48,512]{3,2,1,0:T(8,128)(2,1)}, bf16[2,8,48,512]{3,2,1,0:T(8,128)(2,1)S(1)}, u32[]{:S(2)}, u32[]{:S(2)}) collective-permute-start(bf16[2,8,48,512]{3,2,1,0:T(8,128)(2,1)} %get-tuple-element.38), channel_id=1, source_target_pairs={{0,192},{192,0},{1,193},{193,1},{2,194},{194,2},{3,195},{195,3},{4... | collective-permute-start | bytes 2359304 | tf_op jit(solution)/shard_map/ppermute | solution.py:24
  147.7 13.1 %all-to-all-start.3 = ((bf16[4,8,48,128]{3,2,1,0:T(8,128)(2,1)}), bf16[4,8,48,128]{3,2,1,0:T(8,128)(2,1)S(1)}, u32[]{:S(2)}, u32[]{:S(2)}) async-start(bf16[4,8,48,128]{3,2,1,0:T(8,128)(2,1)} %shard_map.80), calls=%async_computation.3 | async-start | bytes 786432 | tf_op jit(solution)/shard_map/all_to_all | solution.py:174
  (7 other events, 6.5 us)

commit v7 on v6

--- a/solution.py
+++ b/solution.py
@@ -22,16 +22,6 @@
 
 def flip(value, axis):
     return lax.ppermute(value, axis, [(0, 1), (1, 0)])
-
-
-def along(value, hops):
-    pairs = []
-    for zh in range(2):
-        for c in range(2):
-            for z in range(6):
-                to = (6 * zh + z + (hops if c == 0 else -hops)) % 12
-                pairs.append(((2 * zh + c) * 6 + z, (2 * (to // 6) + c) * 6 + to % 6))
-    return lax.ppermute(value, ("zh", "c", "z"), pairs)
 
 
 def after(value, *others):
@@ -79,9 +69,8 @@
     rows = pl.ds(ROWS * part, ROWS)
     here = (half_done[rows] - 0.3325 * back[1].astype(F32)).astype(BF)
     there = (back[0].astype(F32) - 0.3325 * other[rows]).astype(BF)
-    for x in range(4):
-        up[x, zh] = here
-        up[x, 1 - zh] = there
+    up[zh] = here
+    up[1 - zh] = there
 
 
 def outer_body(*refs):
@@ -94,41 +83,44 @@
         new_anchor[rows] = anchor[rows] - 0.7 * (mean_delta + 0.9 * moved)
 
 
-def product_body(*refs):
-    tokens, weights = refs[:9], refs[9:11]
-    keep, give, rows, columns, sems = refs[11:]
-    c, y = lax.axis_index("c"), lax.axis_index("y")
+def product_body(count, *refs):
+    tokens, weights = refs[:9], refs[9 : 9 + count]
+    keep, give, rows, columns, sems = refs[9 + count :]
+    c, x, y = lax.axis_index("c"), lax.axis_index("x"), lax.axis_index("y")
     sources = []
     for piece, at, length in zip(tokens, (0, 96, 192, 288, 384, 432, 480, 576, 672), (96, 96, 96, 96, 48, 48, 96, 96, 96)):
         place = lax.rem(y + at // 96, 8) * 96 + at % 96
         sources.append((0, piece, rows.at[pl.ds(pl.multiple_of(place, 16), length)]))
-    for kind in range(2):
-        for x in range(4):
-            target = columns.at[kind, :, pl.ds(128 * x, 128)]
-            sources.append((2 * kind + x // 2, weights[kind].at[x], target))
+    for j, source in enumerate(weights):
+        if j < 4 or count == 8:
+            lanes = pl.ds(pl.multiple_of(128 * lax.rem(x + j % 4, 4), 128), 128)
+            sources.append((j // 4, source, columns.at[j // 4, :, lanes]))
+        else:
+            for at in range(4):
+                sources.append((1, source.at[at], columns.at[1, :, pl.ds(128 * at, 128)]))
     copies = []
     for i, (stage, source, target) in enumerate(sources):
         copy = pltpu.make_async_copy(source, target, sems.at[i])
         copy.start()
         copies.append((stage, copy))
-    for stage in range(4):
+    for kind in range(2):
         for at, copy in copies:
-            if at == stage:
+            if at == kind:
                 copy.wait()
-        kind, pair = stage // 2, stage % 2
-        span = slice(256 * pair, 256 * pair + 256)
-        for half in range(2):
-            total = jnp.dot(rows[384 * half : 384 * half + 384], columns[kind, :, span], preferred_element_type=F32)
-            for s in range(4):
-                low, high = total[96 * s : 96 * s + 48], total[96 * s + 48 : 96 * s + 96]
-                keep[kind, 4 * half + s, :, span] = jnp.where(c == 0, low, high).astype(BF)
-                give[kind, 4 * half + s, :, span] = jnp.where(c == 0, high, low).astype(BF)
+        for pair in range(2):
+            span = slice(256 * pair, 256 * pair + 256)
+            for half in range(2):
+                total = jnp.dot(rows[384 * half : 384 * half + 384], columns[kind, :, span], preferred_element_type=F32)
+                for s in range(4):
+                    low, high = total[96 * s : 96 * s + 48], total[96 * s + 48 : 96 * s + 96]
+                    keep[kind, 4 * half + s, :, span] = jnp.where(c == 0, low, high).astype(BF)
+                    give[kind, 4 * half + s, :, span] = jnp.where(c == 0, high, low).astype(BF)
 
 
-def product(tokens, gate, up):
+def product(tokens, weights):
     return call(
-        product_body,
-        [*tokens, gate, up],
+        functools.partial(product_body, len(weights)),
+        [*tokens, *weights],
         [like((2, 8, 48, 512), BF)] * 2,
         True,
         [pltpu.VMEM((768, 2048), BF), pltpu.VMEM((2, 2048, 512), BF), pltpu.SemaphoreType.DMA((17,))],
@@ -154,22 +146,24 @@
         [grad, got, anchor, momentum],
         [like((2, ROWS, 128), BF)] * PARTS + [like((1024, 128), F32)] * 3,
     )
+    back = flip(parts[0], "zh")
     tokens = after(tokens, pick)
     cut = jnp.transpose(tokens[0].reshape(8, 2, 2, 1024), (2, 0, 1, 3)).reshape(2, 1, 8, 2048)
     cut = jnp.broadcast_to(cut, (2, 6, 8, 2048)).reshape(12, 8, 2048)
     six = lax.all_to_all(cut, ("c", "z"), 0, 0).reshape(96, 2048)
-    own = lax.dynamic_index_in_dim(gate_weight.reshape(2, 2, 1024, 128), c, 1, keepdims=False).reshape(1, 2048, 128)
-    own = jnp.broadcast_to(own, (4, 2048, 128))
-
-    back = along(parts[0], 1)
-    six, back, own = lax.optimization_barrier((six, back, own))
-    first = [along(back, 5)] + [shift(six, "y", by) for by in (2, -2, 1, -1)]
-    back, f2, b2, f1, b1, gate_all = lax.optimization_barrier((*first, lax.all_to_all(own, "x", 0, 0)))
-    (up,) = call(functools.partial(update_body, 0), [back, half_done, other], [like((4, 2, 1024, 128), BF)])
-    up_all = lax.all_to_all(up.reshape(4, 2048, 128), "x", 0, 0)
-    f3, b3 = shift(f1, "y", 2), shift(b1, "y", -2)
-    f4, b4 = shift(f2[:48], "y", 2), shift(b2[48:], "y", -2)
-    keep, give = product([six, b1, b2, b3, f4, b4, f3, f2, f1], gate_all, up_all)
+    six = after(six, parts[0])
+    f1, b1 = shift(six, "y", 1), shift(six, "y", -1)
+    f2, b2 = shift(f1, "y", 1), shift(b1, "y", -1)
+    (up,) = call(functools.partial(update_body, 0), [back, half_done, other], [like((2, 1024, 128), BF)])
+    ups = [up.reshape(2048, 128)]
+    ups += [shift(ups[0], "x", -j) for j in (1, 2, 3)]
+    f2, b2 = after(f2, up), after(b2, up)
+    own = lax.dynamic_index_in_dim(gate_weight.reshape(2, 2, 1024, 128), c, 1, keepdims=False).reshape(2048, 128)
+    gates = [own] + [shift(own, "x", -j) for j in (1, 2, 3)]
+    f3, b3 = shift(f2, "y", 1), shift(b2, "y", -1)
+    f3, b3, *gates = lax.optimization_barrier((f3, b3, *gates))
+    f4, b4 = shift(f3[:48], "y", 1), shift(b3[48:], "y", -1)
+    keep, give = product([six, b1, b2, b3, f4, b4, f3, f2, f1], [*gates, *ups])
     (hidden,) = call(gated_body, [keep, flip(give, "c")], [like((4, 8, 48, 128), BF)])
     hidden = lax.all_to_all(hidden, "x", 0, 0)
     hidden = jnp.transpose(hidden.reshape(4, 8, 6, 8, 128), (2, 0, 1, 3, 4)).reshape(1, 1536, 128)

time: 163 us -> 158 us (0.969)
  the two profiles are of different devices: /device:TPU:16 before, /device:TPU:216 now
where the time goes in v7:
time: 158 us; the launch traced here: 157 us
  starting transfers between devices  76.4 us (48%)
  waiting for transfers between devices  55 us (35%)
  Pallas kernels  17.8 us (11%)
  local copies, waits for them, and re-layouts  7.16 us (5%)
    ppermute x14, starting transfers between devices, shift(): return lax.ppermute(value, axis, [(i, (i + by) % n) for i in range(n)])  48 us
    ppermute x3, waiting for transfers between devices, flip(): return lax.ppermute(value, axis, [(0, 1), (1, 0)])  27.4 us
    ppermute x14, waiting for transfers between devices, shift(): return lax.ppermute(value, axis, [(i, (i + by) % n) for i in range(n)])  21.8 us
    pallas_call x5, Pallas kernels, call(): pl.pallas_call(body, out_shape=outs, grid=(1,), in_specs=[pl.BlockSpec(me...  17.8 us
    ppermute x3, starting transfers between devices, flip(): return lax.ppermute(value, axis, [(0, 1), (1, 0)])  14.6 us
    all_to_all x1, starting transfers between devices, per_device(): six = lax.all_to_all(cut, ('c', 'z'), 0, 0).reshape(96, 2048)  9.93 us
    all_to_all x1, waiting for transfers between devices, per_device(): hidden = lax.all_to_all(hidden, 'x', 0, 0)  5.79 us
    unnamed x30, local copies, waits for them, and re-layouts  4.16 us
  transfers between devices with their start and end apart: 19, of which 8 were waited for; matrix products, arithmetic and copies ran while one was open for 0% of the time, Pallas kernels for 5%

profile of v7, /device:TPU:216, one launch (start us, length us, event | category | flops | bytes accessed | tf_op | source)
XLA Modules:
  0.0 157.4 jit_solution(1806925744530210538)
XLA Ops:
  2.8 9.9 %all-to-all-start = ((bf16[12,8,2048]{2,1,0:T(8,128)(2,1)}), bf16[12,8,2048]{2,1,0:T(8,128)(2,1)S(1)}, u32[]{:S(2)}, u32[]{:S(2)}) async-start(bf16[12,8,2048]{2,1,0:T(8,128)(2,1)} %bitcast.4), calls=%async_computation | async-start | bytes 786432 | tf_op jit(solution)/shard_map/all_to_all | solution.py:153
  17.3 3.1 %shard_map.76 = (bf16[2,1024,128]{2,1,0:T(8,128)(2,1)}, f32[1024,128]{1,0:T(8,128)}, f32[1024,128]{1,0:T(8,128)}, f32[1024,128]{1,0:T(8,128)}) custom-call(bf16[2,2,1024,128]{3,2,1,0:T(8,128)(2,1)} %bitcast.20, bf16[2,1024,128]{2,1,0:T(8,128)(2,1)} %copy-done.11, f32[1024,128]{1,0:T(8,128)} %refs_2_.1, f32[1024,128]{1,0:T(8,128)} %refs_3_.1), custom_call_target="tpu_custom_call" | custom-call | bytes 1024 | tf_op jit(solution)/shard_map/pallas_call | solution.py:40
  20.4 10.6 %collective-permute-start.1 = (bf16[2,1024,128]{2,1,0:T(8,128)(2,1)}, bf16[2,1024,128]{2,1,0:T(8,128)(2,1)S(1)}, u32[]{:S(2)}, u32[]{:S(2)}) collective-permute-start(bf16[2,1024,128]{2,1,0:T(8,128)(2,1)} %get-tuple-element.21), channel_id=1, source_target_pairs={{0,384},{384,0},{1,385},{385,1},{2,386},{386,2},{3,387},{387,3},{4... | collective-permute-start | bytes 1572872 | tf_op jit(solution)/shard_map/ppermute | solution.py:24
  31.1 4.7 %collective-permute-start.4 = (bf16[96,2048]{1,0:T(8,128)(2,1)S(1)}, bf16[96,2048]{1,0:T(8,128)(2,1)}, u32[]{:S(2)}, u32[]{:S(2)}) collective-permute-start(bf16[96,2048]{1,0:T(8,128)(2,1)S(1)} %bitcast.29), channel_id=1, source_target_pairs={{0,1},{1,2},{2,3},{3,4},{4,5},{5,6},{6,7},{7,0},{8,9},{9,10},{10,1... | collective-permute-start | bytes 1179656 | tf_op jit(solution)/shard_map/ppermute | solution.py:20
  37.8 3.4 %collective-permute-start.10 = (bf16[2048,128]{1,0:T(8,128)(2,1)S(1)}, bf16[2048,128]{1,0:T(8,128)(2,1)S(1)}, u32[]{:S(2)}, u32[]{:S(2)}) collective-permute-start(bf16[2048,128]{1,0:T(8,128)(2,1)S(1)} %bitcast.21), channel_id=1, source_target_pairs={{0,8},{8,16},{16,24},{24,0},{1,9},{9,17},{17,25},{25,1},{2,10},{10... | collective-permute-start | bytes 1572872 | tf_op jit(solution)/shard_map/ppermute | solution.py:20
  41.2 4.6 %collective-permute-start.9 = (bf16[2048,128]{1,0:T(8,128)(2,1)S(1)}, bf16[2048,128]{1,0:T(8,128)(2,1)S(1)}, u32[]{:S(2)}, u32[]{:S(2)}) collective-permute-start(bf16[2048,128]{1,0:T(8,128)(2,1)S(1)} %bitcast.22), channel_id=1, source_target_pairs={{0,16},{8,24},{16,0},{24,8},{1,17},{9,25},{17,1},{25,9},{2,18},{10... | collective-permute-start | bytes 1572872 | tf_op jit(solution)/shard_map/ppermute | solution.py:20
  45.8 23.2 %collective-permute-done.1.refs_0_.back = bf16[2,1024,128]{2,1,0:T(8,128)(2,1)S(1)} collective-permute-done((bf16[2,1024,128]{2,1,0:T(8,128)(2,1)}, bf16[2,1024,128]{2,1,0:T(8,128)(2,1)S(1)}, u32[]{:S(2)}, u32[]{:S(2)}) %collective-permute-start.1) | collective-permute-done | bytes 524320 | tf_op jit(solution)/shard_map/ppermute | solution.py:24
  69.0 4.7 %collective-permute-start.8 = (bf16[2048,128]{1,0:T(8,128)(2,1)S(1)}, bf16[2048,128]{1,0:T(8,128)(2,1)S(1)}, u32[]{:S(2)}, u32[]{:S(2)}) collective-permute-start(bf16[2048,128]{1,0:T(8,128)(2,1)S(1)} %bitcast.23), channel_id=1, source_target_pairs={{0,24},{8,0},{16,8},{24,16},{1,25},{9,1},{17,9},{25,17},{2,26},{10... | collective-permute-start | bytes 1572872 | tf_op jit(solution)/shard_map/ppermute | solution.py:20
  73.7 4.7 %collective-permute-start.5 = (bf16[96,2048]{1,0:T(8,128)(2,1)}, bf16[96,2048]{1,0:T(8,128)(2,1)}, u32[]{:S(2)}, u32[]{:S(2)}) collective-permute-start(bf16[96,2048]{1,0:T(8,128)(2,1)} %collective-permute-done.4.refs_8_), channel_id=1, source_target_pairs={{0,1},{1,2},{2,3},{3,4},{4,5},{5,6},{6,7},{7,0},{8,9},{9,10},{10,1... | collective-permute-start | bytes 1179656 | tf_op jit(solution)/shard_map/ppermute | solution.py:20
  82.6 4.0 %collective-permute-done.5.refs_7_ = bf16[96,2048]{1,0:T(8,128)(2,1)} collective-permute-done((bf16[96,2048]{1,0:T(8,128)(2,1)}, bf16[96,2048]{1,0:T(8,128)(2,1)}, u32[]{:S(2)}, u32[]{:S(2)}) %collective-permute-start.5) | collective-permute-done | bytes 393248 | tf_op jit(solution)/shard_map/ppermute | solution.py:20
  86.6 5.3 %collective-permute-done.3.refs_2_ = bf16[96,2048]{1,0:T(8,128)(2,1)} collective-permute-done((bf16[96,2048]{1,0:T(8,128)(2,1)}, bf16[96,2048]{1,0:T(8,128)(2,1)}, u32[]{:S(2)}, u32[]{:S(2)}) %collective-permute-start.3) | collective-permute-done | bytes 393248 | tf_op jit(solution)/shard_map/ppermute | solution.py:20
  93.8 5.1 %collective-permute-start.6 = (bf16[96,2048]{1,0:T(8,128)(2,1)}, bf16[96,2048]{1,0:T(8,128)(2,1)S(1)}, u32[]{:S(2)}, u32[]{:S(2)}) collective-permute-start(bf16[96,2048]{1,0:T(8,128)(2,1)} %collective-permute-done.5.refs_7_), channel_id=1, source_target_pairs={{0,1},{1,2},{2,3},{3,4},{4,5},{5,6},{6,7},{7,0},{8,9},{9,10},{10,1... | collective-permute-start | bytes 1179656 | tf_op jit(solution)/shard_map/ppermute | solution.py:20
  100.9 4.2 %collective-permute-start.14 = (bf16[2048,128]{1,0:T(8,128)(2,1)}, bf16[2048,128]{1,0:T(8,128)(2,1)}, u32[]{:S(2)}, u32[]{:S(2)}) collective-permute-start(bf16[2048,128]{1,0:T(8,128)(2,1)} %bitcast.26), channel_id=1, source_target_pairs={{0,16},{8,24},{16,0},{24,8},{1,17},{9,25},{17,1},{25,9},{2,18},{10... | collective-permute-start | bytes 1572872 | tf_op jit(solution)/shard_map/ppermute | solution.py:20
  105.1 3.0 %collective-permute-start.13 = (bf16[2048,128]{1,0:T(8,128)(2,1)}, bf16[2048,128]{1,0:T(8,128)(2,1)S(1)}, u32[]{:S(2)}, u32[]{:S(2)}) collective-permute-start(bf16[2048,128]{1,0:T(8,128)(2,1)} %bitcast.27), channel_id=1, source_target_pairs={{0,24},{8,0},{16,8},{24,16},{1,25},{9,1},{17,9},{25,17},{2,26},{10... | collective-permute-start | bytes 1572872 | tf_op jit(solution)/shard_map/ppermute | solution.py:20
  109.2 2.8 %collective-permute-start.11 = (bf16[48,2048]{1,0:T(8,128)(2,1)S(1)}, bf16[48,2048]{1,0:T(8,128)(2,1)S(1)}, u32[]{:S(2)}, u32[]{:S(2)}) collective-permute-start(bf16[48,2048]{1,0:T(8,128)(2,1)S(1)} %slice.6), channel_id=1, source_target_pairs={{0,1},{1,2},{2,3},{3,4},{4,5},{5,6},{6,7},{7,0},{8,9},{9,10},{10,1... | collective-permute-start | bytes 589832 | tf_op jit(solution)/shard_map/ppermute | solution.py:20
  111.9 3.1 %collective-permute-start.12 = (bf16[48,2048]{1,0:T(8,128)(2,1)S(1)}, bf16[48,2048]{1,0:T(8,128)(2,1)S(1)}, u32[]{:S(2)}, u32[]{:S(2)}) collective-permute-start(bf16[48,2048]{1,0:T(8,128)(2,1)S(1)} %slice.7), channel_id=1, source_target_pairs={{0,7},{1,0},{2,1},{3,2},{4,3},{5,4},{6,5},{7,6},{8,15},{9,8},{10,9... | collective-permute-start | bytes 589832 | tf_op jit(solution)/shard_map/ppermute | solution.py:20
  115.0 10.0 %collective-permute-done.15.refs_16_ = bf16[2048,128]{1,0:T(8,128)(2,1)} collective-permute-done((bf16[2048,128]{1,0:T(8,128)(2,1)}, bf16[2048,128]{1,0:T(8,128)(2,1)}, u32[]{:S(2)}, u32[]{:S(2)}) %collective-permute-start.15) | collective-permute-done | bytes 524320 | tf_op jit(solution)/shard_map/ppermute | solution.py:20
  125.1 2.4 %collective-permute-done.13.refs_14_ = bf16[2048,128]{1,0:T(8,128)(2,1)S(1)} collective-permute-done((bf16[2048,128]{1,0:T(8,128)(2,1)}, bf16[2048,128]{1,0:T(8,128)(2,1)S(1)}, u32[]{:S(2)}, u32[]{:S(2)}) %collective-permute-start.13) | collective-permute-done | bytes 524320 | tf_op jit(solution)/shard_map/ppermute | solution.py:20
  129.1 7.4 %shard_map.79 = (bf16[2,8,48,512]{3,2,1,0:T(8,128)(2,1)}, bf16[2,8,48,512]{3,2,1,0:T(8,128)(2,1)}) custom-call(bf16[96,2048]{1,0:T(8,128)(2,1)} %bitcast.31, bf16[96,2048]{1,0:T(8,128)(2,1)} %collective-permute-done.2.refs_1_, bf16[96,2048]{1,0:T(8,128)(2,1)} %collective-permute-done.3.refs_2_, bf16[96,2048]{1,0:T(8,128)(2,1)} %copy-done.4, ...), custom_call_target="tpu_custom_call" | custom-call | bytes 1024 | tf_op jit(solution)/shard_map/pallas_call | solution.py:40
  138.4 2.5 %collective-permute-done.16.got = bf16[2,8,48,512]{3,2,1,0:T(8,128)(2,1)S(1)} collective-permute-done((bf16[2,8,48,512]{3,2,1,0:T(8,128)(2,1)}, bf16[2,8,48,512]{3,2,1,0:T(8,128)(2,1)S(1)}, u32[]{:S(2)}, u32[]{:S(2)}) %collective-permute-start.16) | collective-permute-done | bytes 786464 | tf_op jit(solution)/shard_map/ppermute | solution.py:24
  141.8 2.5 %shard_map.80 = bf16[4,8,48,128]{3,2,1,0:T(8,128)(2,1)} custom-call(bf16[2,8,48,512]{3,2,1,0:T(8,128)(2,1)} %get-tuple-element.37.keep, bf16[2,8,48,512]{3,2,1,0:T(8,128)(2,1)} %copy-done.6), custom_call_target="tpu_custom_call" | custom-call | bytes 1024 | tf_op jit(solution)/shard_map/pallas_call | solution.py:40
  144.2 3.9 %all-to-all-start.1 = ((bf16[4,8,48,128]{3,2,1,0:T(8,128)(2,1)}), bf16[4,8,48,128]{3,2,1,0:T(8,128)(2,1)S(1)}, u32[]{:S(2)}, u32[]{:S(2)}) async-start(bf16[4,8,48,128]{3,2,1,0:T(8,128)(2,1)} %shard_map.80), calls=%async_computation.1 | async-start | bytes 786432 | tf_op jit(solution)/shard_map/all_to_all | solution.py:168
  148.1 2.6 %shard_map.77 = (f32[1024,128]{1,0:T(8,128)}, f32[1024,128]{1,0:T(8,128)}) custom-call(bf16[2,1024,128]{2,1,0:T(8,128)(2,1)} %copy-done.2, f32[1024,128]{1,0:T(8,128)} %get-tuple-element.22.refs_1_, f32[1024,128]{1,0:T(8,128)} %refs_2_.1, f32[1024,128]{1,0:T(8,128)} %refs_3_.1), custom_call_target="tpu_custom_call" | custom-call | bytes 1024 | tf_op jit(solution)/shard_map/pallas_call | solution.py:40
  150.7 5.8 %all-to-all-done.1 = bf16[4,8,48,128]{3,2,1,0:T(8,128)(2,1)S(1)} async-done(((bf16[4,8,48,128]{3,2,1,0:T(8,128)(2,1)}), bf16[4,8,48,128]{3,2,1,0:T(8,128)(2,1)S(1)}, u32[]{:S(2)}, u32[]{:S(2)}) %all-to-all-start.1) | async-done | bytes 393248 | tf_op jit(solution)/shard_map/all_to_all | solution.py:168
  (57 shorter events, 22.8 us)
Async XLA Ops:
  0.6 37.1 %copy-start = (bf16[4096,128]{1,0:T(8,128)(2,1)S(1)}, bf16[4096,128]{1,0:T(8,128)(2,1)}, u32[]{:S(2)}) copy-start(bf16[4096,128]{1,0:T(8,128)(2,1)} %param.6) | copy-start | bytes 3145732
  2.8 28.3 %all-to-all-start = ((bf16[12,8,2048]{2,1,0:T(8,128)(2,1)}), bf16[12,8,2048]{2,1,0:T(8,128)(2,1)S(1)}, u32[]{:S(2)}, u32[]{:S(2)}) async-start(bf16[12,8,2048]{2,1,0:T(8,128)(2,1)} %bitcast.4), calls=%async_computation | async-start | bytes 786432 | tf_op jit(solution)/shard_map/all_to_all | solution.py:153
  12.7 3.8 %collective-permute-start = (bf16[2,1024,128]{2,1,0:T(8,128)(2,1)S(1)}, bf16[2,1024,128]{2,1,0:T(8,128)(2,1)S(1)}, u32[]{:S(2)}, u32[]{:S(2)}) collective-permute-start(bf16[2,1024,128]{2,1,0:T(8,128)(2,1)S(1)} %dynamic-slice_bitcast_fusion), channel_id=1, source_target_pairs={{0,192},{192,0},{1,193},{193,1},{2,194},{194,2},{3,195},{195,3},{4... | collective-permute-start | bytes 1572872 | tf_op jit(solution)/shard_map/ppermute | solution.py:24
  20.4 48.6 %collective-permute-start.1 = (bf16[2,1024,128]{2,1,0:T(8,128)(2,1)}, bf16[2,1024,128]{2,1,0:T(8,128)(2,1)S(1)}, u32[]{:S(2)}, u32[]{:S(2)}) collective-permute-start(bf16[2,1024,128]{2,1,0:T(8,128)(2,1)} %get-tuple-element.21), channel_id=1, source_target_pairs={{0,384},{384,0},{1,385},{385,1},{2,386},{386,2},{3,387},{387,3},{4... | collective-permute-start | bytes 1572872 | tf_op jit(solution)/shard_map/ppermute | solution.py:24
  31.1 42.6 %collective-permute-start.4 = (bf16[96,2048]{1,0:T(8,128)(2,1)S(1)}, bf16[96,2048]{1,0:T(8,128)(2,1)}, u32[]{:S(2)}, u32[]{:S(2)}) collective-permute-start(bf16[96,2048]{1,0:T(8,128)(2,1)S(1)} %bitcast.29), channel_id=1, source_target_pairs={{0,1},{1,2},{2,3},{3,4},{4,5},{5,6},{6,7},{7,0},{8,9},{9,10},{10,1... | collective-permute-start | bytes 1179656 | tf_op jit(solution)/shard_map/ppermute | solution.py:20
  35.8 42.6 %collective-permute-start.2 = (bf16[96,2048]{1,0:T(8,128)(2,1)S(1)}, bf16[96,2048]{1,0:T(8,128)(2,1)}, u32[]{:S(2)}, u32[]{:S(2)}) collective-permute-start(bf16[96,2048]{1,0:T(8,128)(2,1)S(1)} %bitcast.30), channel_id=1, source_target_pairs={{0,7},{1,0},{2,1},{3,2},{4,3},{5,4},{6,5},{7,6},{8,15},{9,8},{10,9... | collective-permute-start | bytes 1179656 | tf_op jit(solution)/shard_map/ppermute | solution.py:20
  37.8 44.8 %copy-start.1 = (bf16[2,1,1024,128]{3,2,1,0:T(8,128)(2,1)}, bf16[2,1,1024,128]{3,2,1,0:T(8,128)(2,1)S(1)}, u32[]{:S(2)}) copy-start(bf16[2,1,1024,128]{3,2,1,0:T(8,128)(2,1)S(1)} %constant_dynamic-slice_fusion) | copy-start | bytes 1572868
  37.8 61.2 %collective-permute-start.10 = (bf16[2048,128]{1,0:T(8,128)(2,1)S(1)}, bf16[2048,128]{1,0:T(8,128)(2,1)S(1)}, u32[]{:S(2)}, u32[]{:S(2)}) collective-permute-start(bf16[2048,128]{1,0:T(8,128)(2,1)S(1)} %bitcast.21), channel_id=1, source_target_pairs={{0,8},{8,16},{16,24},{24,0},{1,9},{9,17},{17,25},{25,1},{2,10},{10... | collective-permute-start | bytes 1572872 | tf_op jit(solution)/shard_map/ppermute | solution.py:20
  41.2 59.7 %collective-permute-start.9 = (bf16[2048,128]{1,0:T(8,128)(2,1)S(1)}, bf16[2048,128]{1,0:T(8,128)(2,1)S(1)}, u32[]{:S(2)}, u32[]{:S(2)}) collective-permute-start(bf16[2048,128]{1,0:T(8,128)(2,1)S(1)} %bitcast.22), channel_id=1, source_target_pairs={{0,16},{8,24},{16,0},{24,8},{1,17},{9,25},{17,1},{25,9},{2,18},{10... | collective-permute-start | bytes 1572872 | tf_op jit(solution)/shard_map/ppermute | solution.py:20
  69.0 36.1 %collective-permute-start.8 = (bf16[2048,128]{1,0:T(8,128)(2,1)S(1)}, bf16[2048,128]{1,0:T(8,128)(2,1)S(1)}, u32[]{:S(2)}, u32[]{:S(2)}) collective-permute-start(bf16[2048,128]{1,0:T(8,128)(2,1)S(1)} %bitcast.23), channel_id=1, source_target_pairs={{0,24},{8,0},{16,8},{24,16},{1,25},{9,1},{17,9},{25,17},{2,26},{10... | collective-permute-start | bytes 1572872 | tf_op jit(solution)/shard_map/ppermute | solution.py:20
  73.7 12.9 %collective-permute-start.5 = (bf16[96,2048]{1,0:T(8,128)(2,1)}, bf16[96,2048]{1,0:T(8,128)(2,1)}, u32[]{:S(2)}, u32[]{:S(2)}) collective-permute-start(bf16[96,2048]{1,0:T(8,128)(2,1)} %collective-permute-done.4.refs_8_), channel_id=1, source_target_pairs={{0,1},{1,2},{2,3},{3,4},{4,5},{5,6},{6,7},{7,0},{8,9},{9,10},{10,1... | collective-permute-start | bytes 1179656 | tf_op jit(solution)/shard_map/ppermute | solution.py:20
  78.4 13.5 %collective-permute-start.3 = (bf16[96,2048]{1,0:T(8,128)(2,1)}, bf16[96,2048]{1,0:T(8,128)(2,1)}, u32[]{:S(2)}, u32[]{:S(2)}) collective-permute-start(bf16[96,2048]{1,0:T(8,128)(2,1)} %collective-permute-done.2.refs_1_), channel_id=1, source_target_pairs={{0,7},{1,0},{2,1},{3,2},{4,3},{5,4},{6,5},{7,6},{8,15},{9,8},{10,9... | collective-permute-start | bytes 1179656 | tf_op jit(solution)/shard_map/ppermute | solution.py:20
  91.9 16.3 %collective-permute-start.7 = (bf16[96,2048]{1,0:T(8,128)(2,1)}, bf16[96,2048]{1,0:T(8,128)(2,1)S(1)}, u32[]{:S(2)}, u32[]{:S(2)}) collective-permute-start(bf16[96,2048]{1,0:T(8,128)(2,1)} %collective-permute-done.3.refs_2_), channel_id=1, source_target_pairs={{0,7},{1,0},{2,1},{3,2},{4,3},{5,4},{6,5},{7,6},{8,15},{9,8},{10,9... | collective-permute-start | bytes 1179656 | tf_op jit(solution)/shard_map/ppermute | solution.py:20
  93.8 14.4 %collective-permute-start.6 = (bf16[96,2048]{1,0:T(8,128)(2,1)}, bf16[96,2048]{1,0:T(8,128)(2,1)S(1)}, u32[]{:S(2)}, u32[]{:S(2)}) collective-permute-start(bf16[96,2048]{1,0:T(8,128)(2,1)} %collective-permute-done.5.refs_7_), channel_id=1, source_target_pairs={{0,1},{1,2},{2,3},{3,4},{4,5},{5,6},{6,7},{7,0},{8,9},{9,10},{10,1... | collective-permute-start | bytes 1179656 | tf_op jit(solution)/shard_map/ppermute | solution.py:20
  99.0 29.3 %copy-start.7 = (bf16[2048,128]{1,0:T(8,128)(2,1)}, bf16[2048,128]{1,0:T(8,128)(2,1)S(1)}, u32[]{:S(2)}) copy-start(bf16[2048,128]{1,0:T(8,128)(2,1)S(1)} %collective-permute-done.10.refs_12_) | copy-start | bytes 1572868
  99.0 26.1 %collective-permute-start.15 = (bf16[2048,128]{1,0:T(8,128)(2,1)}, bf16[2048,128]{1,0:T(8,128)(2,1)}, u32[]{:S(2)}, u32[]{:S(2)}) collective-permute-start(bf16[2048,128]{1,0:T(8,128)(2,1)} %bitcast.25), channel_id=1, source_target_pairs={{0,8},{8,16},{16,24},{24,0},{1,9},{9,17},{17,25},{25,1},{2,10},{10... | collective-permute-start | bytes 1572872 | tf_op jit(solution)/shard_map/ppermute | solution.py:20
  100.9 27.3 %copy-start.8 = (bf16[2048,128]{1,0:T(8,128)(2,1)}, bf16[2048,128]{1,0:T(8,128)(2,1)S(1)}, u32[]{:S(2)}) copy-start(bf16[2048,128]{1,0:T(8,128)(2,1)S(1)} %collective-permute-done.9.refs_11_) | copy-start | bytes 1572868
  100.9 24.1 %collective-permute-start.14 = (bf16[2048,128]{1,0:T(8,128)(2,1)}, bf16[2048,128]{1,0:T(8,128)(2,1)}, u32[]{:S(2)}, u32[]{:S(2)}) collective-permute-start(bf16[2048,128]{1,0:T(8,128)(2,1)} %bitcast.26), channel_id=1, source_target_pairs={{0,16},{8,24},{16,0},{24,8},{1,17},{9,25},{17,1},{25,9},{2,18},{10... | collective-permute-start | bytes 1572872 | tf_op jit(solution)/shard_map/ppermute | solution.py:20
  105.1 23.1 %copy-start.9 = (bf16[2048,128]{1,0:T(8,128)(2,1)}, bf16[2048,128]{1,0:T(8,128)(2,1)S(1)}, u32[]{:S(2)}) copy-start(bf16[2048,128]{1,0:T(8,128)(2,1)S(1)} %collective-permute-done.8.refs_10_) | copy-start | bytes 1572868
  105.1 22.4 %collective-permute-start.13 = (bf16[2048,128]{1,0:T(8,128)(2,1)}, bf16[2048,128]{1,0:T(8,128)(2,1)S(1)}, u32[]{:S(2)}, u32[]{:S(2)}) collective-permute-start(bf16[2048,128]{1,0:T(8,128)(2,1)} %bitcast.27), channel_id=1, source_target_pairs={{0,24},{8,0},{16,8},{24,16},{1,25},{9,1},{17,9},{25,17},{2,26},{10... | collective-permute-start | bytes 1572872 | tf_op jit(solution)/shard_map/ppermute | solution.py:20
  109.2 18.3 %collective-permute-start.11 = (bf16[48,2048]{1,0:T(8,128)(2,1)S(1)}, bf16[48,2048]{1,0:T(8,128)(2,1)S(1)}, u32[]{:S(2)}, u32[]{:S(2)}) collective-permute-start(bf16[48,2048]{1,0:T(8,128)(2,1)S(1)} %slice.6), channel_id=1, source_target_pairs={{0,1},{1,2},{2,3},{3,4},{4,5},{5,6},{6,7},{7,0},{8,9},{9,10},{10,1... | collective-permute-start | bytes 589832 | tf_op jit(solution)/shard_map/ppermute | solution.py:20
  111.9 16.3 %collective-permute-start.12 = (bf16[48,2048]{1,0:T(8,128)(2,1)S(1)}, bf16[48,2048]{1,0:T(8,128)(2,1)S(1)}, u32[]{:S(2)}, u32[]{:S(2)}) collective-permute-start(bf16[48,2048]{1,0:T(8,128)(2,1)S(1)} %slice.7), channel_id=1, source_target_pairs={{0,7},{1,0},{2,1},{3,2},{4,3},{5,4},{6,5},{7,6},{8,15},{9,8},{10,9... | collective-permute-start | bytes 589832 | tf_op jit(solution)/shard_map/ppermute | solution.py:20
  136.5 4.4 %collective-permute-start.16 = (bf16[2,8,48,512]{3,2,1,0:T(8,128)(2,1)}, bf16[2,8,48,512]{3,2,1,0:T(8,128)(2,1)S(1)}, u32[]{:S(2)}, u32[]{:S(2)}) collective-permute-start(bf16[2,8,48,512]{3,2,1,0:T(8,128)(2,1)} %get-tuple-element.38), channel_id=1, source_target_pairs={{0,192},{192,0},{1,193},{193,1},{2,194},{194,2},{3,195},{195,3},{4... | collective-permute-start | bytes 2359304 | tf_op jit(solution)/shard_map/ppermute | solution.py:24
  144.2 12.3 %all-to-all-start.1 = ((bf16[4,8,48,128]{3,2,1,0:T(8,128)(2,1)}), bf16[4,8,48,128]{3,2,1,0:T(8,128)(2,1)S(1)}, u32[]{:S(2)}, u32[]{:S(2)}) async-start(bf16[4,8,48,128]{3,2,1,0:T(8,128)(2,1)} %shard_map.80), calls=%async_computation.1 | async-start | bytes 786432 | tf_op jit(solution)/shard_map/all_to_all | solution.py:168
  (10 other events, 24.9 us)

commit v8 on v6

--- a/solution.py
+++ b/solution.py
@@ -120,7 +120,8 @@
         for half in range(2):
             total = jnp.dot(rows[384 * half : 384 * half + 384], columns[kind, :, span], preferred_element_type=F32)
             for s in range(4):
-                low, high = total[96 * s : 96 * s + 48], total[96 * s + 48 : 96 * s + 96]
+                mixed = total[96 * s : 96 * s + 96].reshape(6, 2, 8, 256)
+                low, high = mixed[:, 0].reshape(48, 256), mixed[:, 1].reshape(48, 256)
                 keep[kind, 4 * half + s, :, span] = jnp.where(c == 0, low, high).astype(BF)
                 give[kind, 4 * half + s, :, span] = jnp.where(c == 0, high, low).astype(BF)
 
@@ -146,28 +147,35 @@
 def per_device(tokens, gate_weight, pseudo_grad, anchor, momentum):
     c = lax.axis_index("c")
 
+    z = lax.axis_index("z")
+    own = lax.dynamic_index_in_dim(gate_weight.reshape(2, 2, 1024, 128), c, 1, keepdims=False).reshape(1, 2048, 128)
+    own = jnp.broadcast_to(own, (4, 2048, 128))
+    gate_all = lax.all_to_all(own, "x", 0, 0)
+
     grad = pseudo_grad.reshape(2, 2, 1024, 128)
-    pick = lax.dynamic_index_in_dim(grad, 1 - c, 1, keepdims=False)
-    got = flip(pick, "c")
+    got = flip(lax.dynamic_index_in_dim(grad, 1 - c, 1, keepdims=False), "c")
     *parts, half_done, mine, other = call(
         prepare_body,
         [grad, got, anchor, momentum],
         [like((2, ROWS, 128), BF)] * PARTS + [like((1024, 128), F32)] * 3,
     )
-    tokens = after(tokens, pick)
-    cut = jnp.transpose(tokens[0].reshape(8, 2, 2, 1024), (2, 0, 1, 3)).reshape(2, 1, 8, 2048)
-    cut = jnp.broadcast_to(cut, (2, 6, 8, 2048)).reshape(12, 8, 2048)
-    six = lax.all_to_all(cut, ("c", "z"), 0, 0).reshape(96, 2048)
-    own = lax.dynamic_index_in_dim(gate_weight.reshape(2, 2, 1024, 128), c, 1, keepdims=False).reshape(1, 2048, 128)
-    own = jnp.broadcast_to(own, (4, 2048, 128))
+    back = along(along(parts[0], 5), 1)
 
-    back = along(parts[0], 1)
-    six, back, own = lax.optimization_barrier((six, back, own))
-    first = [along(back, 5)] + [shift(six, "y", by) for by in (2, -2, 1, -1)]
-    back, f2, b2, f1, b1, gate_all = lax.optimization_barrier((*first, lax.all_to_all(own, "x", 0, 0)))
+    tok = tokens[0].reshape(8, 2, 2, 1024)
+    kept = lax.dynamic_index_in_dim(tok, c, 2, keepdims=False)
+    away = flip(lax.dynamic_index_in_dim(tok, 1 - c, 2, keepdims=False), "c")
+    tok = jnp.where(c == 0, jnp.stack([kept, away]), jnp.stack([away, kept])).reshape(16, 2048)
+    beside = lax.ppermute(tok, "z", [(i, i ^ 1) for i in range(6)])
+    two = jnp.where(z % 2 == 0, jnp.stack([tok, beside]), jnp.stack([beside, tok]))
+    two = after(two, parts[0])
+    three = jnp.stack([two, shift(two, "z", -2), shift(two, "z", 2)] * 2)
+    six = lax.dynamic_slice_in_dim(three, (3 - z // 2) % 3, 3, 0).reshape(96, 2048)
+    f1, b1 = shift(six, "y", 1), shift(six, "y", -1)
+    f2, b2 = shift(f1, "y", 1), shift(b1, "y", -1)
+    f2, b2, back, gate_all = lax.optimization_barrier((f2, b2, back, gate_all))
     (up,) = call(functools.partial(update_body, 0), [back, half_done, other], [like((4, 2, 1024, 128), BF)])
     up_all = lax.all_to_all(up.reshape(4, 2048, 128), "x", 0, 0)
-    f3, b3 = shift(f1, "y", 2), shift(b1, "y", -2)
+    f3, b3 = shift(f2, "y", 1), shift(b2, "y", -1)
     f4, b4 = shift(f2[:48], "y", 2), shift(b2[48:], "y", -2)
     keep, give = product([six, b1, b2, b3, f4, b4, f3, f2, f1], gate_all, up_all)
     (hidden,) = call(gated_body, [keep, flip(give, "c")], [like((4, 8, 48, 128), BF)])

time: 163 us -> 162 us (level)
  waiting for transfers between devices: 65.4 us -> 55.9 us
  starting transfers between devices: 66.4 us -> 75.2 us
    all_to_all x2 -> x1, starting transfers between devices: 16.4 us -> 4.29 us  [per_device(): gate_all = lax.all_to_all(own, 'x', 0, 0)]
    ppermute x8 -> x10, waiting for transfers between devices: 41.7 us -> 31.2 us  [shift(): return lax.ppermute(value, axis, [(i, (i + by) % n) for i in range(n)])]
    ppermute x8 -> x10, starting transfers between devices: 29.5 us -> 38.3 us  [shift(): return lax.ppermute(value, axis, [(i, (i + by) % n) for i in range(n)])]
    ppermute x2, starting transfers between devices: 6.51 us -> 12.4 us  [along(): return lax.ppermute(value, ('zh', 'c', 'z'), pairs)]
    ppermute x0 -> x1, starting transfers between devices: none -> 4.28 us  [per_device(): beside = lax.ppermute(tok, 'z', [(i, i ^ 1) for i in range(6)])]
    ppermute x2 -> x3, starting transfers between devices: 4.29 us -> 6.22 us  [flip(): return lax.ppermute(value, axis, [(0, 1), (1, 0)])]
    ppermute x2, waiting for transfers between devices: 14 us -> 15.6 us  [along(): return lax.ppermute(value, ('zh', 'c', 'z'), pairs)]
    unnamed x30 -> x29, local copies, waits for them, and re-layouts: 3.35 us -> 2.65 us
  transfers between devices with their start and end apart: 16 -> 19, of which waited for: 10 -> 9; matrix products, arithmetic and copies ran while one was open for 1% -> 3% of each run, Pallas kernels for 4% -> 4%
where the time goes in v8:
time: 162 us; the launch traced here: 161 us
  starting transfers between devices  75.2 us (46%)
  waiting for transfers between devices  55.9 us (35%)
  Pallas kernels  19.3 us (12%)
  local copies, waits for them, and re-layouts  9.86 us (6%)
    ppermute x10, starting transfers between devices, shift(): return lax.ppermute(value, axis, [(i, (i + by) % n) for i in range(n)])  38.3 us
    ppermute x10, waiting for transfers between devices, shift(): return lax.ppermute(value, axis, [(i, (i + by) % n) for i in range(n)])  31.2 us
    pallas_call x5, Pallas kernels, call(): pl.pallas_call(body, out_shape=outs, grid=(1,), in_specs=[pl.BlockSpec(me...  19.3 us
    ppermute x2, waiting for transfers between devices, along(): return lax.ppermute(value, ('zh', 'c', 'z'), pairs)  15.6 us
    ppermute x2, starting transfers between devices, along(): return lax.ppermute(value, ('zh', 'c', 'z'), pairs)  12.4 us
    ppermute x3, starting transfers between devices, flip(): return lax.ppermute(value, axis, [(0, 1), (1, 0)])  6.22 us
    all_to_all x1, waiting for transfers between devices, per_device(): hidden = lax.all_to_all(hidden, 'x', 0, 0)  5.79 us
    all_to_all x1, starting transfers between devices, per_device(): up_all = lax.all_to_all(up.reshape(4, 2048, 128), 'x', 0, 0)  4.9 us
  transfers between devices with their start and end apart: 19, of which 9 were waited for; matrix products, arithmetic and copies ran while one was open for 3% of the time, Pallas kernels for 4%

profile of v8, /device:TPU:16, one launch (start us, length us, event | category | flops | bytes accessed | tf_op | source)
XLA Modules:
  0.0 161.2 jit_solution(13223926912414432761)
XLA Ops:
  8.6 4.3 %collective-permute-start.1 = (bf16[16,2048]{1,0:T(8,128)(2,1)S(1)}, bf16[16,2048]{1,0:T(8,128)(2,1)S(1)}, u32[]{:S(2)}, u32[]{:S(2)}) collective-permute-start(bf16[16,2048]{1,0:T(8,128)(2,1)S(1)} %bitcast.39), channel_id=1, source_target_pairs={{0,32},{32,0},{64,96},{96,64},{128,160},{160,128},{1,33},{33,1},{6... | collective-permute-start | bytes 196616 | tf_op jit(solution)/shard_map/ppermute | solution.py:168
  14.5 4.3 %all-to-all-start = ((bf16[4,2048,128]{2,1,0:T(8,128)(2,1)}), bf16[4,2048,128]{2,1,0:T(8,128)(2,1)S(1)}, u32[]{:S(2)}, u32[]{:S(2)}) async-start(bf16[4,2048,128]{2,1,0:T(8,128)(2,1)} %broadcast_in_dim.8), calls=%async_computation | async-start | bytes 4194304 | tf_op jit(solution)/shard_map/all_to_all | solution.py:153
  18.9 3.1 %shard_map.76 = (bf16[2,1024,128]{2,1,0:T(8,128)(2,1)}, f32[1024,128]{1,0:T(8,128)}, f32[1024,128]{1,0:T(8,128)}, f32[1024,128]{1,0:T(8,128)}) custom-call(bf16[2,2,1024,128]{3,2,1,0:T(8,128)(2,1)} %bitcast.32, bf16[2,1024,128]{2,1,0:T(8,128)(2,1)} %collective-permute-done.2.got, f32[1024,128]{1,0:T(8,128)} %refs_2_.1, f32[1024,128]{1,0:T(8,128)} %refs_3_.1), custom_call_target="tpu_custom_call" | custom-call | bytes 1024 | tf_op jit(solution)/shard_map/pallas_call | solution.py:50
  22.0 10.9 %collective-permute-start.3 = (bf16[2,16,2048]{2,1,0:T(8,128)(2,1)S(1)}, bf16[2,16,2048]{2,1,0:T(8,128)(2,1)S(1)}, u32[]{:S(2)}, u32[]{:S(2)}) collective-permute-start(bf16[2,16,2048]{2,1,0:T(8,128)(2,1)S(1)} %maximum_select_fusion), channel_id=1, source_target_pairs={{0,128},{32,160},{64,0},{96,32},{128,64},{160,96},{1,129},{33,161}... | collective-permute-start | bytes 393224 | tf_op jit(solution)/shard_map/ppermute | solution.py:20
  34.9 7.3 %collective-permute-start.9 = (bf16[2,1024,128]{2,1,0:T(8,128)(2,1)}, bf16[2,1024,128]{2,1,0:T(8,128)(2,1)S(1)}, u32[]{:S(2)}, u32[]{:S(2)}) collective-permute-start(bf16[2,1024,128]{2,1,0:T(8,128)(2,1)} %get-tuple-element.16), channel_id=1, source_target_pairs={{0,160},{32,384},{64,416},{96,448},{128,480},{160,512},{192,608},{... | collective-permute-start | bytes 1572872 | tf_op jit(solution)/shard_map/ppermute | solution.py:34
  42.2 13.5 %collective-permute-done.4 = bf16[2,16,2048]{2,1,0:T(8,128)(2,1)S(1)} collective-permute-done((bf16[2,16,2048]{2,1,0:T(8,128)(2,1)S(1)}, bf16[2,16,2048]{2,1,0:T(8,128)(2,1)S(1)}, u32[]{:S(2)}, u32[]{:S(2)}) %collective-permute-start.4) | collective-permute-done | bytes 131104 | tf_op jit(solution)/shard_map/ppermute | solution.py:20
  55.8 3.5 %collective-permute-start.5 = (bf16[96,2048]{1,0:T(8,128)(2,1)S(1)}, bf16[96,2048]{1,0:T(8,128)(2,1)S(1)}, u32[]{:S(2)}, u32[]{:S(2)}) collective-permute-start(bf16[96,2048]{1,0:T(8,128)(2,1)S(1)} %bitcast.34), channel_id=1, source_target_pairs={{0,1},{1,2},{2,3},{3,4},{4,5},{5,6},{6,7},{7,0},{8,9},{9,10},{10,1... | collective-permute-start | bytes 1179656 | tf_op jit(solution)/shard_map/ppermute | solution.py:20
  61.6 15.6 %collective-permute-done.9 = bf16[2,1024,128]{2,1,0:T(8,128)(2,1)S(1)} collective-permute-done((bf16[2,1024,128]{2,1,0:T(8,128)(2,1)}, bf16[2,1024,128]{2,1,0:T(8,128)(2,1)S(1)}, u32[]{:S(2)}, u32[]{:S(2)}) %collective-permute-start.9) | collective-permute-done | bytes 524320 | tf_op jit(solution)/shard_map/ppermute | solution.py:34
  77.3 5.1 %collective-permute-start.10 = (bf16[2,1024,128]{2,1,0:T(8,128)(2,1)S(1)}, bf16[2,1024,128]{2,1,0:T(8,128)(2,1)}, u32[]{:S(2)}, u32[]{:S(2)}) collective-permute-start(bf16[2,1024,128]{2,1,0:T(8,128)(2,1)S(1)} %collective-permute-done.9), channel_id=1, source_target_pairs={{0,32},{32,64},{64,96},{96,128},{128,160},{160,384},{192,736},{224... | collective-permute-start | bytes 1572872 | tf_op jit(solution)/shard_map/ppermute | solution.py:34
  82.4 3.5 %collective-permute-start.6 = (bf16[96,2048]{1,0:T(8,128)(2,1)S(1)}, bf16[96,2048]{1,0:T(8,128)(2,1)S(1)}, u32[]{:S(2)}, u32[]{:S(2)}) collective-permute-start(bf16[96,2048]{1,0:T(8,128)(2,1)S(1)} %collective-permute-done.5.refs_8_), channel_id=1, source_target_pairs={{0,1},{1,2},{2,3},{3,4},{4,5},{5,6},{6,7},{7,0},{8,9},{9,10},{10,1... | collective-permute-start | bytes 1179656 | tf_op jit(solution)/shard_map/ppermute | solution.py:20
  88.3 3.8 %collective-permute-done.6.refs_7_ = bf16[96,2048]{1,0:T(8,128)(2,1)S(1)} collective-permute-done((bf16[96,2048]{1,0:T(8,128)(2,1)S(1)}, bf16[96,2048]{1,0:T(8,128)(2,1)S(1)}, u32[]{:S(2)}, u32[]{:S(2)}) %collective-permute-start.6) | collective-permute-done | bytes 393248 | tf_op jit(solution)/shard_map/ppermute | solution.py:20
  92.1 4.3 %collective-permute-done.8.refs_2_ = bf16[96,2048]{1,0:T(8,128)(2,1)S(1)} collective-permute-done((bf16[96,2048]{1,0:T(8,128)(2,1)S(1)}, bf16[96,2048]{1,0:T(8,128)(2,1)S(1)}, u32[]{:S(2)}, u32[]{:S(2)}) %collective-permute-start.8) | collective-permute-done | bytes 393248 | tf_op jit(solution)/shard_map/ppermute | solution.py:20
  97.1 3.7 %shard_map.78 = bf16[4,2,1024,128]{3,2,1,0:T(8,128)(2,1)} custom-call(bf16[2,1024,128]{2,1,0:T(8,128)(2,1)} %collective-permute-done.10.refs_0_.back, f32[1024,128]{1,0:T(8,128)} %get-tuple-element.25.half_done, f32[1024,128]{1,0:T(8,128)} %get-tuple-element.26.other), custom_call_target="tpu_custom_call" | custom-call | bytes 1024 | tf_op jit(solution)/shard_map/pallas_call | solution.py:50
  100.9 4.9 %all-to-all-start.1 = ((bf16[4,2048,128]{2,1,0:T(8,128)(2,1)}), bf16[4,2048,128]{2,1,0:T(8,128)(2,1)}, u32[]{:S(2)}, u32[]{:S(2)}) async-start(bf16[4,2048,128]{2,1,0:T(8,128)(2,1)} %bitcast.30), calls=%async_computation.1 | async-start | bytes 4194304 | tf_op jit(solution)/shard_map/all_to_all | solution.py:177
  107.7 5.1 %collective-permute-start.14 = (bf16[96,2048]{1,0:T(8,128)(2,1)}, bf16[96,2048]{1,0:T(8,128)(2,1)S(1)}, u32[]{:S(2)}, u32[]{:S(2)}) collective-permute-start(bf16[96,2048]{1,0:T(8,128)(2,1)} %copy-done.3), channel_id=1, source_target_pairs={{0,1},{1,2},{2,3},{3,4},{4,5},{5,6},{6,7},{7,0},{8,9},{9,10},{10,1... | collective-permute-start | bytes 1179656 | tf_op jit(solution)/shard_map/ppermute | solution.py:20
  114.7 4.6 %collective-permute-start.12 = (bf16[48,2048]{1,0:T(8,128)(2,1)S(1)}, bf16[48,2048]{1,0:T(8,128)(2,1)S(1)}, u32[]{:S(2)}, u32[]{:S(2)}) collective-permute-start(bf16[48,2048]{1,0:T(8,128)(2,1)S(1)} %slice.6), channel_id=1, source_target_pairs={{0,2},{1,3},{2,4},{3,5},{4,6},{5,7},{6,0},{7,1},{8,10},{9,11},{10,... | collective-permute-start | bytes 589832 | tf_op jit(solution)/shard_map/ppermute | solution.py:20
  121.5 4.7 %collective-permute-done.12.refs_4_ = bf16[48,2048]{1,0:T(8,128)(2,1)S(1)} collective-permute-done((bf16[48,2048]{1,0:T(8,128)(2,1)S(1)}, bf16[48,2048]{1,0:T(8,128)(2,1)S(1)}, u32[]{:S(2)}, u32[]{:S(2)}) %collective-permute-start.12) | collective-permute-done | bytes 196640 | tf_op jit(solution)/shard_map/ppermute | solution.py:20
  126.1 5.0 %collective-permute-done.13.refs_5_ = bf16[48,2048]{1,0:T(8,128)(2,1)S(1)} collective-permute-done((bf16[48,2048]{1,0:T(8,128)(2,1)S(1)}, bf16[48,2048]{1,0:T(8,128)(2,1)S(1)}, u32[]{:S(2)}, u32[]{:S(2)}) %collective-permute-start.13) | collective-permute-done | bytes 196640 | tf_op jit(solution)/shard_map/ppermute | solution.py:20
  132.0 7.4 %shard_map.79 = (bf16[2,8,48,512]{3,2,1,0:T(8,128)(2,1)}, bf16[2,8,48,512]{3,2,1,0:T(8,128)(2,1)}) custom-call(bf16[96,2048]{1,0:T(8,128)(2,1)} %bitcast.36, bf16[96,2048]{1,0:T(8,128)(2,1)} %copy-done.7, bf16[96,2048]{1,0:T(8,128)(2,1)} %copy-done.4, bf16[96,2048]{1,0:T(8,128)(2,1)} %copy-done.8, bf16[48,2048]{1,0:T(8,128)(2,1)} %copy-done.10, ...), custom_call_target="tpu_custom_call" | custom-call | bytes 1024 | tf_op jit(solution)/shard_map/pallas_call | solution.py:50
  141.4 2.5 %collective-permute-done.15.got = bf16[2,8,48,512]{3,2,1,0:T(8,128)(2,1)S(1)} collective-permute-done((bf16[2,8,48,512]{3,2,1,0:T(8,128)(2,1)}, bf16[2,8,48,512]{3,2,1,0:T(8,128)(2,1)S(1)}, u32[]{:S(2)}, u32[]{:S(2)}) %collective-permute-start.15) | collective-permute-done | bytes 786464 | tf_op jit(solution)/shard_map/ppermute | solution.py:24
  144.7 2.5 %shard_map.80 = bf16[4,8,48,128]{3,2,1,0:T(8,128)(2,1)} custom-call(bf16[2,8,48,512]{3,2,1,0:T(8,128)(2,1)} %get-tuple-element.27.keep, bf16[2,8,48,512]{3,2,1,0:T(8,128)(2,1)} %copy-done.5), custom_call_target="tpu_custom_call" | custom-call | bytes 1024 | tf_op jit(solution)/shard_map/pallas_call | solution.py:50
  147.2 4.8 %all-to-all-start.2 = ((bf16[4,8,48,128]{3,2,1,0:T(8,128)(2,1)}), bf16[4,8,48,128]{3,2,1,0:T(8,128)(2,1)S(1)}, u32[]{:S(2)}, u32[]{:S(2)}) async-start(bf16[4,8,48,128]{3,2,1,0:T(8,128)(2,1)} %shard_map.80), calls=%async_computation.2 | async-start | bytes 786432 | tf_op jit(solution)/shard_map/all_to_all | solution.py:182
  152.0 2.6 %shard_map.77 = (f32[1024,128]{1,0:T(8,128)}, f32[1024,128]{1,0:T(8,128)}) custom-call(bf16[2,1024,128]{2,1,0:T(8,128)(2,1)} %collective-permute-done.10.refs_0_.back, f32[1024,128]{1,0:T(8,128)} %get-tuple-element.19.refs_1_, f32[1024,128]{1,0:T(8,128)} %refs_2_.1, f32[1024,128]{1,0:T(8,128)} %refs_3_.1), custom_call_target="tpu_custom_call" | custom-call | bytes 1024 | tf_op jit(solution)/shard_map/pallas_call | solution.py:50
  154.6 5.8 %all-to-all-done.2 = bf16[4,8,48,128]{3,2,1,0:T(8,128)(2,1)S(1)} async-done(((bf16[4,8,48,128]{3,2,1,0:T(8,128)(2,1)}), bf16[4,8,48,128]{3,2,1,0:T(8,128)(2,1)S(1)}, u32[]{:S(2)}, u32[]{:S(2)}) %all-to-all-start.2) | async-done | bytes 393248 | tf_op jit(solution)/shard_map/all_to_all | solution.py:182
  (59 shorter events, 27.7 us)
Async XLA Ops:
  0.6 12.2 %copy-start = (bf16[4096,128]{1,0:T(8,128)(2,1)S(1)}, bf16[4096,128]{1,0:T(8,128)(2,1)}, u32[]{:S(2)}) copy-start(bf16[4096,128]{1,0:T(8,128)(2,1)} %param.6) | copy-start | bytes 3145732
  2.6 16.3 %collective-permute-start.2 = (bf16[2,1024,128]{2,1,0:T(8,128)(2,1)}, bf16[2,1024,128]{2,1,0:T(8,128)(2,1)}, u32[]{:S(2)}, u32[]{:S(2)}) collective-permute-start(bf16[2,1024,128]{2,1,0:T(8,128)(2,1)} %dynamic-slice_bitcast_fusion), channel_id=1, source_target_pairs={{0,192},{192,0},{1,193},{193,1},{2,194},{194,2},{3,195},{195,3},{4... | collective-permute-start | bytes 1572872 | tf_op jit(solution)/shard_map/ppermute | solution.py:24
  5.3 3.2 %collective-permute-start = (bf16[8,2,1024]{2,0,1:T(8,128)(2,1)S(1)}, bf16[8,2,1024]{2,0,1:T(8,128)(2,1)S(1)}, u32[]{:S(2)}, u32[]{:S(2)}) collective-permute-start(bf16[8,2,1024]{2,0,1:T(8,128)(2,1)S(1)} %get-tuple-element.30), channel_id=1, source_target_pairs={{0,192},{192,0},{1,193},{193,1},{2,194},{194,2},{3,195},{195,3},{4... | collective-permute-start | bytes 98312 | tf_op jit(solution)/shard_map/ppermute | solution.py:24
  8.6 10.3 %collective-permute-start.1 = (bf16[16,2048]{1,0:T(8,128)(2,1)S(1)}, bf16[16,2048]{1,0:T(8,128)(2,1)S(1)}, u32[]{:S(2)}, u32[]{:S(2)}) collective-permute-start(bf16[16,2048]{1,0:T(8,128)(2,1)S(1)} %bitcast.39), channel_id=1, source_target_pairs={{0,32},{32,0},{64,96},{96,64},{128,160},{160,128},{1,33},{33,1},{6... | collective-permute-start | bytes 196616 | tf_op jit(solution)/shard_map/ppermute | solution.py:168
  14.5 82.6 %all-to-all-start = ((bf16[4,2048,128]{2,1,0:T(8,128)(2,1)}), bf16[4,2048,128]{2,1,0:T(8,128)(2,1)S(1)}, u32[]{:S(2)}, u32[]{:S(2)}) async-start(bf16[4,2048,128]{2,1,0:T(8,128)(2,1)} %broadcast_in_dim.8), calls=%async_computation | async-start | bytes 4194304 | tf_op jit(solution)/shard_map/all_to_all | solution.py:153
  22.0 20.1 %collective-permute-start.3 = (bf16[2,16,2048]{2,1,0:T(8,128)(2,1)S(1)}, bf16[2,16,2048]{2,1,0:T(8,128)(2,1)S(1)}, u32[]{:S(2)}, u32[]{:S(2)}) collective-permute-start(bf16[2,16,2048]{2,1,0:T(8,128)(2,1)S(1)} %maximum_select_fusion), channel_id=1, source_target_pairs={{0,128},{32,160},{64,0},{96,32},{128,64},{160,96},{1,129},{33,161}... | collective-permute-start | bytes 393224 | tf_op jit(solution)/shard_map/ppermute | solution.py:20
  32.9 22.7 %collective-permute-start.4 = (bf16[2,16,2048]{2,1,0:T(8,128)(2,1)S(1)}, bf16[2,16,2048]{2,1,0:T(8,128)(2,1)S(1)}, u32[]{:S(2)}, u32[]{:S(2)}) collective-permute-start(bf16[2,16,2048]{2,1,0:T(8,128)(2,1)S(1)} %maximum_select_fusion), channel_id=1, source_target_pairs={{0,64},{32,96},{64,128},{96,160},{128,0},{160,32},{1,65},{33,97},{... | collective-permute-start | bytes 393224 | tf_op jit(solution)/shard_map/ppermute | solution.py:20
  34.9 42.4 %collective-permute-start.9 = (bf16[2,1024,128]{2,1,0:T(8,128)(2,1)}, bf16[2,1024,128]{2,1,0:T(8,128)(2,1)S(1)}, u32[]{:S(2)}, u32[]{:S(2)}) collective-permute-start(bf16[2,1024,128]{2,1,0:T(8,128)(2,1)} %get-tuple-element.16), channel_id=1, source_target_pairs={{0,160},{32,384},{64,416},{96,448},{128,480},{160,512},{192,608},{... | collective-permute-start | bytes 1572872 | tf_op jit(solution)/shard_map/ppermute | solution.py:34
  55.8 45.1 %copy-start.2 = (bf16[3,2,16,2048]{3,2,1,0:T(8,128)(2,1)}, bf16[3,2,16,2048]{3,2,1,0:T(8,128)(2,1)S(1)}, u32[]{:S(2)}) copy-start(bf16[3,2,16,2048]{3,2,1,0:T(8,128)(2,1)S(1)} %constant_dynamic-slice_fusion.1) | copy-start | bytes 1179652
  55.8 26.6 %collective-permute-start.5 = (bf16[96,2048]{1,0:T(8,128)(2,1)S(1)}, bf16[96,2048]{1,0:T(8,128)(2,1)S(1)}, u32[]{:S(2)}, u32[]{:S(2)}) collective-permute-start(bf16[96,2048]{1,0:T(8,128)(2,1)S(1)} %bitcast.34), channel_id=1, source_target_pairs={{0,1},{1,2},{2,3},{3,4},{4,5},{5,6},{6,7},{7,0},{8,9},{9,10},{10,1... | collective-permute-start | bytes 1179656 | tf_op jit(solution)/shard_map/ppermute | solution.py:20
  59.3 26.6 %collective-permute-start.7 = (bf16[96,2048]{1,0:T(8,128)(2,1)S(1)}, bf16[96,2048]{1,0:T(8,128)(2,1)S(1)}, u32[]{:S(2)}, u32[]{:S(2)}) collective-permute-start(bf16[96,2048]{1,0:T(8,128)(2,1)S(1)} %bitcast.35), channel_id=1, source_target_pairs={{0,7},{1,0},{2,1},{3,2},{4,3},{5,4},{6,5},{7,6},{8,15},{9,8},{10,9... | collective-permute-start | bytes 1179656 | tf_op jit(solution)/shard_map/ppermute | solution.py:20
  77.3 19.9 %collective-permute-start.10 = (bf16[2,1024,128]{2,1,0:T(8,128)(2,1)S(1)}, bf16[2,1024,128]{2,1,0:T(8,128)(2,1)}, u32[]{:S(2)}, u32[]{:S(2)}) collective-permute-start(bf16[2,1024,128]{2,1,0:T(8,128)(2,1)S(1)} %collective-permute-done.9), channel_id=1, source_target_pairs={{0,32},{32,64},{64,96},{96,128},{128,160},{160,384},{192,736},{224... | collective-permute-start | bytes 1572872 | tf_op jit(solution)/shard_map/ppermute | solution.py:34
  82.4 14.0 %copy-start.6 = (bf16[96,2048]{1,0:T(8,128)(2,1)}, bf16[96,2048]{1,0:T(8,128)(2,1)S(1)}, u32[]{:S(2)}) copy-start(bf16[96,2048]{1,0:T(8,128)(2,1)S(1)} %collective-permute-done.5.refs_8_) | copy-start | bytes 1179652
  82.4 9.7 %collective-permute-start.6 = (bf16[96,2048]{1,0:T(8,128)(2,1)S(1)}, bf16[96,2048]{1,0:T(8,128)(2,1)S(1)}, u32[]{:S(2)}, u32[]{:S(2)}) collective-permute-start(bf16[96,2048]{1,0:T(8,128)(2,1)S(1)} %collective-permute-done.5.refs_8_), channel_id=1, source_target_pairs={{0,1},{1,2},{2,3},{3,4},{4,5},{5,6},{6,7},{7,0},{8,9},{9,10},{10,1... | collective-permute-start | bytes 1179656 | tf_op jit(solution)/shard_map/ppermute | solution.py:20
  85.9 10.5 %copy-start.7 = (bf16[96,2048]{1,0:T(8,128)(2,1)}, bf16[96,2048]{1,0:T(8,128)(2,1)S(1)}, u32[]{:S(2)}) copy-start(bf16[96,2048]{1,0:T(8,128)(2,1)S(1)} %collective-permute-done.7.refs_1_) | copy-start | bytes 1179652
  85.9 10.4 %collective-permute-start.8 = (bf16[96,2048]{1,0:T(8,128)(2,1)S(1)}, bf16[96,2048]{1,0:T(8,128)(2,1)S(1)}, u32[]{:S(2)}, u32[]{:S(2)}) collective-permute-start(bf16[96,2048]{1,0:T(8,128)(2,1)S(1)} %collective-permute-done.7.refs_1_), channel_id=1, source_target_pairs={{0,7},{1,0},{2,1},{3,2},{4,3},{5,4},{6,5},{7,6},{8,15},{9,8},{10,9... | collective-permute-start | bytes 1179656 | tf_op jit(solution)/shard_map/ppermute | solution.py:20
  100.9 30.3 %all-to-all-start.1 = ((bf16[4,2048,128]{2,1,0:T(8,128)(2,1)}), bf16[4,2048,128]{2,1,0:T(8,128)(2,1)}, u32[]{:S(2)}, u32[]{:S(2)}) async-start(bf16[4,2048,128]{2,1,0:T(8,128)(2,1)} %bitcast.30), calls=%async_computation.1 | async-start | bytes 4194304 | tf_op jit(solution)/shard_map/all_to_all | solution.py:177
  105.8 25.3 %collective-permute-start.11 = (bf16[96,2048]{1,0:T(8,128)(2,1)}, bf16[96,2048]{1,0:T(8,128)(2,1)S(1)}, u32[]{:S(2)}, u32[]{:S(2)}) collective-permute-start(bf16[96,2048]{1,0:T(8,128)(2,1)} %copy-done.4), channel_id=1, source_target_pairs={{0,7},{1,0},{2,1},{3,2},{4,3},{5,4},{6,5},{7,6},{8,15},{9,8},{10,9... | collective-permute-start | bytes 1179656 | tf_op jit(solution)/shard_map/ppermute | solution.py:20
  107.7 23.4 %collective-permute-start.14 = (bf16[96,2048]{1,0:T(8,128)(2,1)}, bf16[96,2048]{1,0:T(8,128)(2,1)S(1)}, u32[]{:S(2)}, u32[]{:S(2)}) collective-permute-start(bf16[96,2048]{1,0:T(8,128)(2,1)} %copy-done.3), channel_id=1, source_target_pairs={{0,1},{1,2},{2,3},{3,4},{4,5},{5,6},{6,7},{7,0},{8,9},{9,10},{10,1... | collective-permute-start | bytes 1179656 | tf_op jit(solution)/shard_map/ppermute | solution.py:20
  114.7 11.4 %collective-permute-start.12 = (bf16[48,2048]{1,0:T(8,128)(2,1)S(1)}, bf16[48,2048]{1,0:T(8,128)(2,1)S(1)}, u32[]{:S(2)}, u32[]{:S(2)}) collective-permute-start(bf16[48,2048]{1,0:T(8,128)(2,1)S(1)} %slice.6), channel_id=1, source_target_pairs={{0,2},{1,3},{2,4},{3,5},{4,6},{5,7},{6,0},{7,1},{8,10},{9,11},{10,... | collective-permute-start | bytes 589832 | tf_op jit(solution)/shard_map/ppermute | solution.py:20
  119.3 11.8 %collective-permute-start.13 = (bf16[48,2048]{1,0:T(8,128)(2,1)S(1)}, bf16[48,2048]{1,0:T(8,128)(2,1)S(1)}, u32[]{:S(2)}, u32[]{:S(2)}) collective-permute-start(bf16[48,2048]{1,0:T(8,128)(2,1)S(1)} %slice.7), channel_id=1, source_target_pairs={{0,6},{1,7},{2,0},{3,1},{4,2},{5,3},{6,4},{7,5},{8,14},{9,15},{10,... | collective-permute-start | bytes 589832 | tf_op jit(solution)/shard_map/ppermute | solution.py:20
  126.1 5.0 %copy-start.10 = (bf16[48,2048]{1,0:T(8,128)(2,1)}, bf16[48,2048]{1,0:T(8,128)(2,1)S(1)}, u32[]{:S(2)}) copy-start(bf16[48,2048]{1,0:T(8,128)(2,1)S(1)} %collective-permute-done.12.refs_4_) | copy-start | bytes 589828
  139.4 4.4 %collective-permute-start.15 = (bf16[2,8,48,512]{3,2,1,0:T(8,128)(2,1)}, bf16[2,8,48,512]{3,2,1,0:T(8,128)(2,1)S(1)}, u32[]{:S(2)}, u32[]{:S(2)}) collective-permute-start(bf16[2,8,48,512]{3,2,1,0:T(8,128)(2,1)} %get-tuple-element.28), channel_id=1, source_target_pairs={{0,192},{192,0},{1,193},{193,1},{2,194},{194,2},{3,195},{195,3},{4... | collective-permute-start | bytes 2359304 | tf_op jit(solution)/shard_map/ppermute | solution.py:24
  147.2 13.2 %all-to-all-start.2 = ((bf16[4,8,48,128]{3,2,1,0:T(8,128)(2,1)}), bf16[4,8,48,128]{3,2,1,0:T(8,128)(2,1)S(1)}, u32[]{:S(2)}, u32[]{:S(2)}) async-start(bf16[4,8,48,128]{3,2,1,0:T(8,128)(2,1)} %shard_map.80), calls=%async_computation.2 | async-start | bytes 786432 | tf_op jit(solution)/shard_map/all_to_all | solution.py:182
  (7 other events, 12.1 us)

commit v9 on v7

--- a/solution.py
+++ b/solution.py
@@ -22,6 +22,16 @@
 
 def flip(value, axis):
     return lax.ppermute(value, axis, [(0, 1), (1, 0)])
+
+
+def along(value, hops):
+    pairs = []
+    for zh in range(2):
+        for c in range(2):
+            for z in range(6):
+                to = (6 * zh + z + (hops if c == 0 else -hops)) % 12
+                pairs.append(((2 * zh + c) * 6 + z, (2 * (to // 6) + c) * 6 + to % 6))
+    return lax.ppermute(value, ("zh", "c", "z"), pairs)
 
 
 def after(value, *others):
@@ -146,7 +156,7 @@
         [grad, got, anchor, momentum],
         [like((2, ROWS, 128), BF)] * PARTS + [like((1024, 128), F32)] * 3,
     )
-    back = flip(parts[0], "zh")
+    back = along(along(parts[0], 1), 5)
     tokens = after(tokens, pick)
     cut = jnp.transpose(tokens[0].reshape(8, 2, 2, 1024), (2, 0, 1, 3)).reshape(2, 1, 8, 2048)
     cut = jnp.broadcast_to(cut, (2, 6, 8, 2048)).reshape(12, 8, 2048)

time: 158 us -> 156 us (0.987)
  the two profiles are of different devices: /device:TPU:216 before, /device:TPU:192 now
where the time goes in v9:
time: 156 us; the launch traced here: 155 us
  starting transfers between devices  83.6 us (54%)
  waiting for transfers between devices  45.7 us (29%)
  Pallas kernels  17.8 us (11%)
  local copies, waits for them, and re-layouts  6.4 us (4%)
    ppermute x14, starting transfers between devices, shift(): return lax.ppermute(value, axis, [(i, (i + by) % n) for i in range(n)])  52.1 us
    ppermute x2, waiting for transfers between devices, along(): return lax.ppermute(value, ('zh', 'c', 'z'), pairs)  19.9 us
    pallas_call x5, Pallas kernels, call(): pl.pallas_call(body, out_shape=outs, grid=(1,), in_specs=[pl.BlockSpec(me...  17.8 us
    ppermute x14, waiting for transfers between devices, shift(): return lax.ppermute(value, axis, [(i, (i + by) % n) for i in range(n)])  17.6 us
    ppermute x2, starting transfers between devices, along(): return lax.ppermute(value, ('zh', 'c', 'z'), pairs)  13 us
    all_to_all x1, starting transfers between devices, per_device(): six = lax.all_to_all(cut, ('c', 'z'), 0, 0).reshape(96, 2048)  10.3 us
    all_to_all x1, waiting for transfers between devices, per_device(): hidden = lax.all_to_all(hidden, 'x', 0, 0)  5.79 us
    all_to_all x1, starting transfers between devices, per_device(): hidden = lax.all_to_all(hidden, 'x', 0, 0)  4.29 us
  transfers between devices with their start and end apart: 20, of which 7 were waited for; matrix products, arithmetic and copies ran while one was open for 1% of the time, Pallas kernels for 5%

profile of v9, /device:TPU:192, one launch (start us, length us, event | category | flops | bytes accessed | tf_op | source)
XLA Modules:
  0.0 154.6 jit_solution(9017417324024315482)
XLA Ops:
  4.7 10.3 %all-to-all-start = ((bf16[12,8,2048]{2,1,0:T(8,128)(2,1)}), bf16[12,8,2048]{2,1,0:T(8,128)(2,1)S(1)}, u32[]{:S(2)}, u32[]{:S(2)}) async-start(bf16[12,8,2048]{2,1,0:T(8,128)(2,1)} %bitcast.4), calls=%async_computation | async-start | bytes 786432 | tf_op jit(solution)/shard_map/all_to_all | solution.py:163
  15.8 3.1 %shard_map.76 = (bf16[2,1024,128]{2,1,0:T(8,128)(2,1)}, f32[1024,128]{1,0:T(8,128)}, f32[1024,128]{1,0:T(8,128)}, f32[1024,128]{1,0:T(8,128)}) custom-call(bf16[2,2,1024,128]{3,2,1,0:T(8,128)(2,1)} %bitcast.20, bf16[2,1024,128]{2,1,0:T(8,128)(2,1)} %copy-done.11, f32[1024,128]{1,0:T(8,128)} %refs_2_.1, f32[1024,128]{1,0:T(8,128)} %refs_3_.1), custom_call_target="tpu_custom_call" | custom-call | bytes 1024 | tf_op jit(solution)/shard_map/pallas_call | solution.py:50
  18.9 4.6 %collective-permute-start.1 = (bf16[2,1024,128]{2,1,0:T(8,128)(2,1)}, bf16[2,1024,128]{2,1,0:T(8,128)(2,1)}, u32[]{:S(2)}, u32[]{:S(2)}) collective-permute-start(bf16[2,1024,128]{2,1,0:T(8,128)(2,1)} %get-tuple-element.21), channel_id=1, source_target_pairs={{0,32},{32,64},{64,96},{96,128},{128,160},{160,384},{192,736},{224... | collective-permute-start | bytes 1572872 | tf_op jit(solution)/shard_map/ppermute | solution.py:34
  23.5 11.6 %collective-permute-done.1 = bf16[2,1024,128]{2,1,0:T(8,128)(2,1)} collective-permute-done((bf16[2,1024,128]{2,1,0:T(8,128)(2,1)}, bf16[2,1024,128]{2,1,0:T(8,128)(2,1)}, u32[]{:S(2)}, u32[]{:S(2)}) %collective-permute-start.1) | collective-permute-done | bytes 524320 | tf_op jit(solution)/shard_map/ppermute | solution.py:34
  35.1 8.5 %collective-permute-start.2 = (bf16[2,1024,128]{2,1,0:T(8,128)(2,1)}, bf16[2,1024,128]{2,1,0:T(8,128)(2,1)S(1)}, u32[]{:S(2)}, u32[]{:S(2)}) collective-permute-start(bf16[2,1024,128]{2,1,0:T(8,128)(2,1)} %collective-permute-done.1), channel_id=1, source_target_pairs={{0,160},{32,384},{64,416},{96,448},{128,480},{160,512},{192,608},{... | collective-permute-start | bytes 1572872 | tf_op jit(solution)/shard_map/ppermute | solution.py:34
  43.6 3.5 %collective-permute-start.5 = (bf16[96,2048]{1,0:T(8,128)(2,1)S(1)}, bf16[96,2048]{1,0:T(8,128)(2,1)}, u32[]{:S(2)}, u32[]{:S(2)}) collective-permute-start(bf16[96,2048]{1,0:T(8,128)(2,1)S(1)} %bitcast.29), channel_id=1, source_target_pairs={{0,1},{1,2},{2,3},{3,4},{4,5},{5,6},{6,7},{7,0},{8,9},{9,10},{10,1... | collective-permute-start | bytes 1179656 | tf_op jit(solution)/shard_map/ppermute | solution.py:20
  47.1 3.8 %collective-permute-start.3 = (bf16[96,2048]{1,0:T(8,128)(2,1)S(1)}, bf16[96,2048]{1,0:T(8,128)(2,1)}, u32[]{:S(2)}, u32[]{:S(2)}) collective-permute-start(bf16[96,2048]{1,0:T(8,128)(2,1)S(1)} %bitcast.30), channel_id=1, source_target_pairs={{0,7},{1,0},{2,1},{3,2},{4,3},{5,4},{6,5},{7,6},{8,15},{9,8},{10,9... | collective-permute-start | bytes 1179656 | tf_op jit(solution)/shard_map/ppermute | solution.py:20
  51.0 3.4 %collective-permute-start.11 = (bf16[2048,128]{1,0:T(8,128)(2,1)S(1)}, bf16[2048,128]{1,0:T(8,128)(2,1)S(1)}, u32[]{:S(2)}, u32[]{:S(2)}) collective-permute-start(bf16[2048,128]{1,0:T(8,128)(2,1)S(1)} %bitcast.21), channel_id=1, source_target_pairs={{0,8},{8,16},{16,24},{24,0},{1,9},{9,17},{17,25},{25,1},{2,10},{10... | collective-permute-start | bytes 1572872 | tf_op jit(solution)/shard_map/ppermute | solution.py:20
  54.4 4.6 %collective-permute-start.10 = (bf16[2048,128]{1,0:T(8,128)(2,1)S(1)}, bf16[2048,128]{1,0:T(8,128)(2,1)S(1)}, u32[]{:S(2)}, u32[]{:S(2)}) collective-permute-start(bf16[2048,128]{1,0:T(8,128)(2,1)S(1)} %bitcast.22), channel_id=1, source_target_pairs={{0,16},{8,24},{16,0},{24,8},{1,17},{9,25},{17,1},{25,9},{2,18},{10... | collective-permute-start | bytes 1572872 | tf_op jit(solution)/shard_map/ppermute | solution.py:20
  59.1 3.3 %collective-permute-start.9 = (bf16[2048,128]{1,0:T(8,128)(2,1)S(1)}, bf16[2048,128]{1,0:T(8,128)(2,1)S(1)}, u32[]{:S(2)}, u32[]{:S(2)}) collective-permute-start(bf16[2048,128]{1,0:T(8,128)(2,1)S(1)} %bitcast.23), channel_id=1, source_target_pairs={{0,24},{8,0},{16,8},{24,16},{1,25},{9,1},{17,9},{25,17},{2,26},{10... | collective-permute-start | bytes 1572872 | tf_op jit(solution)/shard_map/ppermute | solution.py:20
  64.5 8.3 %collective-permute-done.2.refs_0_.back = bf16[2,1024,128]{2,1,0:T(8,128)(2,1)S(1)} collective-permute-done((bf16[2,1024,128]{2,1,0:T(8,128)(2,1)}, bf16[2,1024,128]{2,1,0:T(8,128)(2,1)S(1)}, u32[]{:S(2)}, u32[]{:S(2)}) %collective-permute-start.2) | collective-permute-done | bytes 524320 | tf_op jit(solution)/shard_map/ppermute | solution.py:34
  72.7 5.5 %collective-permute-start.4 = (bf16[96,2048]{1,0:T(8,128)(2,1)}, bf16[96,2048]{1,0:T(8,128)(2,1)}, u32[]{:S(2)}, u32[]{:S(2)}) collective-permute-start(bf16[96,2048]{1,0:T(8,128)(2,1)} %collective-permute-done.3.refs_1_), channel_id=1, source_target_pairs={{0,7},{1,0},{2,1},{3,2},{4,3},{5,4},{6,5},{7,6},{8,15},{9,8},{10,9... | collective-permute-start | bytes 1179656 | tf_op jit(solution)/shard_map/ppermute | solution.py:20
  80.5 6.8 %collective-permute-done.4.refs_2_ = bf16[96,2048]{1,0:T(8,128)(2,1)} collective-permute-done((bf16[96,2048]{1,0:T(8,128)(2,1)}, bf16[96,2048]{1,0:T(8,128)(2,1)}, u32[]{:S(2)}, u32[]{:S(2)}) %collective-permute-start.4) | collective-permute-done | bytes 393248 | tf_op jit(solution)/shard_map/ppermute | solution.py:20
  87.4 5.6 %collective-permute-start.8 = (bf16[96,2048]{1,0:T(8,128)(2,1)}, bf16[96,2048]{1,0:T(8,128)(2,1)S(1)}, u32[]{:S(2)}, u32[]{:S(2)}) collective-permute-start(bf16[96,2048]{1,0:T(8,128)(2,1)} %collective-permute-done.4.refs_2_), channel_id=1, source_target_pairs={{0,7},{1,0},{2,1},{3,2},{4,3},{5,4},{6,5},{7,6},{8,15},{9,8},{10,9... | collective-permute-start | bytes 1179656 | tf_op jit(solution)/shard_map/ppermute | solution.py:20
  94.9 3.4 %collective-permute-start.16 = (bf16[2048,128]{1,0:T(8,128)(2,1)}, bf16[2048,128]{1,0:T(8,128)(2,1)}, u32[]{:S(2)}, u32[]{:S(2)}) collective-permute-start(bf16[2048,128]{1,0:T(8,128)(2,1)} %bitcast.25), channel_id=1, source_target_pairs={{0,8},{8,16},{16,24},{24,0},{1,9},{9,17},{17,25},{25,1},{2,10},{10... | collective-permute-start | bytes 1572872 | tf_op jit(solution)/shard_map/ppermute | solution.py:20
  98.3 4.6 %collective-permute-start.15 = (bf16[2048,128]{1,0:T(8,128)(2,1)}, bf16[2048,128]{1,0:T(8,128)(2,1)}, u32[]{:S(2)}, u32[]{:S(2)}) collective-permute-start(bf16[2048,128]{1,0:T(8,128)(2,1)} %bitcast.26), channel_id=1, source_target_pairs={{0,16},{8,24},{16,0},{24,8},{1,17},{9,25},{17,1},{25,9},{2,18},{10... | collective-permute-start | bytes 1572872 | tf_op jit(solution)/shard_map/ppermute | solution.py:20
  103.0 3.3 %collective-permute-start.14 = (bf16[2048,128]{1,0:T(8,128)(2,1)}, bf16[2048,128]{1,0:T(8,128)(2,1)S(1)}, u32[]{:S(2)}, u32[]{:S(2)}) collective-permute-start(bf16[2048,128]{1,0:T(8,128)(2,1)} %bitcast.27), channel_id=1, source_target_pairs={{0,24},{8,0},{16,8},{24,16},{1,25},{9,1},{17,9},{25,17},{2,26},{10... | collective-permute-start | bytes 1572872 | tf_op jit(solution)/shard_map/ppermute | solution.py:20
  109.2 5.1 %collective-permute-start.13 = (bf16[48,2048]{1,0:T(8,128)(2,1)S(1)}, bf16[48,2048]{1,0:T(8,128)(2,1)}, u32[]{:S(2)}, u32[]{:S(2)}) collective-permute-start(bf16[48,2048]{1,0:T(8,128)(2,1)S(1)} %slice.7), channel_id=1, source_target_pairs={{0,7},{1,0},{2,1},{3,2},{4,3},{5,4},{6,5},{7,6},{8,15},{9,8},{10,9... | collective-permute-start | bytes 589832 | tf_op jit(solution)/shard_map/ppermute | solution.py:20
  114.3 9.2 %collective-permute-done.15.refs_15_ = bf16[2048,128]{1,0:T(8,128)(2,1)} collective-permute-done((bf16[2048,128]{1,0:T(8,128)(2,1)}, bf16[2048,128]{1,0:T(8,128)(2,1)}, u32[]{:S(2)}, u32[]{:S(2)}) %collective-permute-start.15) | collective-permute-done | bytes 524320 | tf_op jit(solution)/shard_map/ppermute | solution.py:20
  125.9 7.4 %shard_map.79 = (bf16[2,8,48,512]{3,2,1,0:T(8,128)(2,1)}, bf16[2,8,48,512]{3,2,1,0:T(8,128)(2,1)}) custom-call(bf16[96,2048]{1,0:T(8,128)(2,1)} %bitcast.31, bf16[96,2048]{1,0:T(8,128)(2,1)} %collective-permute-done.3.refs_1_, bf16[96,2048]{1,0:T(8,128)(2,1)} %collective-permute-done.4.refs_2_, bf16[96,2048]{1,0:T(8,128)(2,1)} %copy-done.4, ...), custom_call_target="tpu_custom_call" | custom-call | bytes 1024 | tf_op jit(solution)/shard_map/pallas_call | solution.py:50
  138.6 2.5 %shard_map.80 = bf16[4,8,48,128]{3,2,1,0:T(8,128)(2,1)} custom-call(bf16[2,8,48,512]{3,2,1,0:T(8,128)(2,1)} %get-tuple-element.37.keep, bf16[2,8,48,512]{3,2,1,0:T(8,128)(2,1)} %copy-done.6), custom_call_target="tpu_custom_call" | custom-call | bytes 1024 | tf_op jit(solution)/shard_map/pallas_call | solution.py:50
  141.1 4.3 %all-to-all-start.1 = ((bf16[4,8,48,128]{3,2,1,0:T(8,128)(2,1)}), bf16[4,8,48,128]{3,2,1,0:T(8,128)(2,1)S(1)}, u32[]{:S(2)}, u32[]{:S(2)}) async-start(bf16[4,8,48,128]{3,2,1,0:T(8,128)(2,1)} %shard_map.80), calls=%async_computation.1 | async-start | bytes 786432 | tf_op jit(solution)/shard_map/all_to_all | solution.py:178
  145.4 2.6 %shard_map.77 = (f32[1024,128]{1,0:T(8,128)}, f32[1024,128]{1,0:T(8,128)}) custom-call(bf16[2,1024,128]{2,1,0:T(8,128)(2,1)} %copy-done.2, f32[1024,128]{1,0:T(8,128)} %get-tuple-element.22.refs_1_, f32[1024,128]{1,0:T(8,128)} %refs_2_.1, f32[1024,128]{1,0:T(8,128)} %refs_3_.1), custom_call_target="tpu_custom_call" | custom-call | bytes 1024 | tf_op jit(solution)/shard_map/pallas_call | solution.py:50
  147.9 5.8 %all-to-all-done.1 = bf16[4,8,48,128]{3,2,1,0:T(8,128)(2,1)S(1)} async-done(((bf16[4,8,48,128]{3,2,1,0:T(8,128)(2,1)}), bf16[4,8,48,128]{3,2,1,0:T(8,128)(2,1)S(1)}, u32[]{:S(2)}, u32[]{:S(2)}) %all-to-all-start.1) | async-done | bytes 393248 | tf_op jit(solution)/shard_map/all_to_all | solution.py:178
  (59 shorter events, 22.3 us)
Async XLA Ops:
  0.6 50.3 %copy-start = (bf16[4096,128]{1,0:T(8,128)(2,1)S(1)}, bf16[4096,128]{1,0:T(8,128)(2,1)}, u32[]{:S(2)}) copy-start(bf16[4096,128]{1,0:T(8,128)(2,1)} %param.6) | copy-start | bytes 3145732
  1.8 13.1 %collective-permute-start = (bf16[2,1024,128]{2,1,0:T(8,128)(2,1)S(1)}, bf16[2,1024,128]{2,1,0:T(8,128)(2,1)S(1)}, u32[]{:S(2)}, u32[]{:S(2)}) collective-permute-start(bf16[2,1024,128]{2,1,0:T(8,128)(2,1)S(1)} %dynamic-slice_bitcast_fusion), channel_id=1, source_target_pairs={{0,192},{192,0},{1,193},{193,1},{2,194},{194,2},{3,195},{195,3},{4... | collective-permute-start | bytes 1572872 | tf_op jit(solution)/shard_map/ppermute | solution.py:24
  4.7 38.9 %all-to-all-start = ((bf16[12,8,2048]{2,1,0:T(8,128)(2,1)}), bf16[12,8,2048]{2,1,0:T(8,128)(2,1)S(1)}, u32[]{:S(2)}, u32[]{:S(2)}) async-start(bf16[12,8,2048]{2,1,0:T(8,128)(2,1)} %bitcast.4), calls=%async_computation | async-start | bytes 786432 | tf_op jit(solution)/shard_map/all_to_all | solution.py:163
  18.9 16.2 %collective-permute-start.1 = (bf16[2,1024,128]{2,1,0:T(8,128)(2,1)}, bf16[2,1024,128]{2,1,0:T(8,128)(2,1)}, u32[]{:S(2)}, u32[]{:S(2)}) collective-permute-start(bf16[2,1024,128]{2,1,0:T(8,128)(2,1)} %get-tuple-element.21), channel_id=1, source_target_pairs={{0,32},{32,64},{64,96},{96,128},{128,160},{160,384},{192,736},{224... | collective-permute-start | bytes 1572872 | tf_op jit(solution)/shard_map/ppermute | solution.py:34
  35.1 37.7 %collective-permute-start.2 = (bf16[2,1024,128]{2,1,0:T(8,128)(2,1)}, bf16[2,1024,128]{2,1,0:T(8,128)(2,1)S(1)}, u32[]{:S(2)}, u32[]{:S(2)}) collective-permute-start(bf16[2,1024,128]{2,1,0:T(8,128)(2,1)} %collective-permute-done.1), channel_id=1, source_target_pairs={{0,160},{32,384},{64,416},{96,448},{128,480},{160,512},{192,608},{... | collective-permute-start | bytes 1572872 | tf_op jit(solution)/shard_map/ppermute | solution.py:34
  43.6 15.5 %collective-permute-start.5 = (bf16[96,2048]{1,0:T(8,128)(2,1)S(1)}, bf16[96,2048]{1,0:T(8,128)(2,1)}, u32[]{:S(2)}, u32[]{:S(2)}) collective-permute-start(bf16[96,2048]{1,0:T(8,128)(2,1)S(1)} %bitcast.29), channel_id=1, source_target_pairs={{0,1},{1,2},{2,3},{3,4},{4,5},{5,6},{6,7},{7,0},{8,9},{9,10},{10,1... | collective-permute-start | bytes 1179656 | tf_op jit(solution)/shard_map/ppermute | solution.py:20
  47.1 15.3 %collective-permute-start.3 = (bf16[96,2048]{1,0:T(8,128)(2,1)S(1)}, bf16[96,2048]{1,0:T(8,128)(2,1)}, u32[]{:S(2)}, u32[]{:S(2)}) collective-permute-start(bf16[96,2048]{1,0:T(8,128)(2,1)S(1)} %bitcast.30), channel_id=1, source_target_pairs={{0,7},{1,0},{2,1},{3,2},{4,3},{5,4},{6,5},{7,6},{8,15},{9,8},{10,9... | collective-permute-start | bytes 1179656 | tf_op jit(solution)/shard_map/ppermute | solution.py:20
  51.0 29.5 %copy-start.1 = (bf16[2,1,1024,128]{3,2,1,0:T(8,128)(2,1)}, bf16[2,1,1024,128]{3,2,1,0:T(8,128)(2,1)S(1)}, u32[]{:S(2)}) copy-start(bf16[2,1,1024,128]{3,2,1,0:T(8,128)(2,1)S(1)} %constant_dynamic-slice_fusion) | copy-start | bytes 1572868
  51.0 43.9 %collective-permute-start.11 = (bf16[2048,128]{1,0:T(8,128)(2,1)S(1)}, bf16[2048,128]{1,0:T(8,128)(2,1)S(1)}, u32[]{:S(2)}, u32[]{:S(2)}) collective-permute-start(bf16[2048,128]{1,0:T(8,128)(2,1)S(1)} %bitcast.21), channel_id=1, source_target_pairs={{0,8},{8,16},{16,24},{24,0},{1,9},{9,17},{17,25},{25,1},{2,10},{10... | collective-permute-start | bytes 1572872 | tf_op jit(solution)/shard_map/ppermute | solution.py:20
  54.4 43.9 %collective-permute-start.10 = (bf16[2048,128]{1,0:T(8,128)(2,1)S(1)}, bf16[2048,128]{1,0:T(8,128)(2,1)S(1)}, u32[]{:S(2)}, u32[]{:S(2)}) collective-permute-start(bf16[2048,128]{1,0:T(8,128)(2,1)S(1)} %bitcast.22), channel_id=1, source_target_pairs={{0,16},{8,24},{16,0},{24,8},{1,17},{9,25},{17,1},{25,9},{2,18},{10... | collective-permute-start | bytes 1572872 | tf_op jit(solution)/shard_map/ppermute | solution.py:20
  59.1 43.9 %collective-permute-start.9 = (bf16[2048,128]{1,0:T(8,128)(2,1)S(1)}, bf16[2048,128]{1,0:T(8,128)(2,1)S(1)}, u32[]{:S(2)}, u32[]{:S(2)}) collective-permute-start(bf16[2048,128]{1,0:T(8,128)(2,1)S(1)} %bitcast.23), channel_id=1, source_target_pairs={{0,24},{8,0},{16,8},{24,16},{1,25},{9,1},{17,9},{25,17},{2,26},{10... | collective-permute-start | bytes 1572872 | tf_op jit(solution)/shard_map/ppermute | solution.py:20
  62.4 18.1 %collective-permute-start.6 = (bf16[96,2048]{1,0:T(8,128)(2,1)}, bf16[96,2048]{1,0:T(8,128)(2,1)S(1)}, u32[]{:S(2)}, u32[]{:S(2)}) collective-permute-start(bf16[96,2048]{1,0:T(8,128)(2,1)} %collective-permute-done.5.refs_8_), channel_id=1, source_target_pairs={{0,1},{1,2},{2,3},{3,4},{4,5},{5,6},{6,7},{7,0},{8,9},{9,10},{10,1... | collective-permute-start | bytes 1179656 | tf_op jit(solution)/shard_map/ppermute | solution.py:20
  72.7 14.6 %collective-permute-start.4 = (bf16[96,2048]{1,0:T(8,128)(2,1)}, bf16[96,2048]{1,0:T(8,128)(2,1)}, u32[]{:S(2)}, u32[]{:S(2)}) collective-permute-start(bf16[96,2048]{1,0:T(8,128)(2,1)} %collective-permute-done.3.refs_1_), channel_id=1, source_target_pairs={{0,7},{1,0},{2,1},{3,2},{4,3},{5,4},{6,5},{7,6},{8,15},{9,8},{10,9... | collective-permute-start | bytes 1179656 | tf_op jit(solution)/shard_map/ppermute | solution.py:20
  80.5 45.2 %copy-start.12 = (bf16[96,2048]{1,0:T(8,128)(2,1)}, bf16[96,2048]{1,0:T(8,128)(2,1)S(1)}, u32[]{:S(2)}) copy-start(bf16[96,2048]{1,0:T(8,128)(2,1)S(1)} %collective-permute-done.6.refs_7_) | copy-start | bytes 1179652
  87.4 19.0 %collective-permute-start.8 = (bf16[96,2048]{1,0:T(8,128)(2,1)}, bf16[96,2048]{1,0:T(8,128)(2,1)S(1)}, u32[]{:S(2)}, u32[]{:S(2)}) collective-permute-start(bf16[96,2048]{1,0:T(8,128)(2,1)} %collective-permute-done.4.refs_2_), channel_id=1, source_target_pairs={{0,7},{1,0},{2,1},{3,2},{4,3},{5,4},{6,5},{7,6},{8,15},{9,8},{10,9... | collective-permute-start | bytes 1179656 | tf_op jit(solution)/shard_map/ppermute | solution.py:20
  92.9 13.4 %collective-permute-start.7 = (bf16[96,2048]{1,0:T(8,128)(2,1)S(1)}, bf16[96,2048]{1,0:T(8,128)(2,1)S(1)}, u32[]{:S(2)}, u32[]{:S(2)}) collective-permute-start(bf16[96,2048]{1,0:T(8,128)(2,1)S(1)} %collective-permute-done.6.refs_7_), channel_id=1, source_target_pairs={{0,1},{1,2},{2,3},{3,4},{4,5},{5,6},{6,7},{7,0},{8,9},{9,10},{10,1... | collective-permute-start | bytes 1179656 | tf_op jit(solution)/shard_map/ppermute | solution.py:20
  94.9 30.9 %copy-start.7 = (bf16[2048,128]{1,0:T(8,128)(2,1)}, bf16[2048,128]{1,0:T(8,128)(2,1)S(1)}, u32[]{:S(2)}) copy-start(bf16[2048,128]{1,0:T(8,128)(2,1)S(1)} %collective-permute-done.11.refs_12_) | copy-start | bytes 1572868
  94.9 19.4 %collective-permute-start.16 = (bf16[2048,128]{1,0:T(8,128)(2,1)}, bf16[2048,128]{1,0:T(8,128)(2,1)}, u32[]{:S(2)}, u32[]{:S(2)}) collective-permute-start(bf16[2048,128]{1,0:T(8,128)(2,1)} %bitcast.25), channel_id=1, source_target_pairs={{0,8},{8,16},{16,24},{24,0},{1,9},{9,17},{17,25},{25,1},{2,10},{10... | collective-permute-start | bytes 1572872 | tf_op jit(solution)/shard_map/ppermute | solution.py:20
  98.3 25.2 %collective-permute-start.15 = (bf16[2048,128]{1,0:T(8,128)(2,1)}, bf16[2048,128]{1,0:T(8,128)(2,1)}, u32[]{:S(2)}, u32[]{:S(2)}) collective-permute-start(bf16[2048,128]{1,0:T(8,128)(2,1)} %bitcast.26), channel_id=1, source_target_pairs={{0,16},{8,24},{16,0},{24,8},{1,17},{9,25},{17,1},{25,9},{2,18},{10... | collective-permute-start | bytes 1572872 | tf_op jit(solution)/shard_map/ppermute | solution.py:20
  103.0 22.0 %collective-permute-start.14 = (bf16[2048,128]{1,0:T(8,128)(2,1)}, bf16[2048,128]{1,0:T(8,128)(2,1)S(1)}, u32[]{:S(2)}, u32[]{:S(2)}) collective-permute-start(bf16[2048,128]{1,0:T(8,128)(2,1)} %bitcast.27), channel_id=1, source_target_pairs={{0,24},{8,0},{16,8},{24,16},{1,25},{9,1},{17,9},{25,17},{2,26},{10... | collective-permute-start | bytes 1572872 | tf_op jit(solution)/shard_map/ppermute | solution.py:20
  107.2 17.8 %collective-permute-start.12 = (bf16[48,2048]{1,0:T(8,128)(2,1)S(1)}, bf16[48,2048]{1,0:T(8,128)(2,1)S(1)}, u32[]{:S(2)}, u32[]{:S(2)}) collective-permute-start(bf16[48,2048]{1,0:T(8,128)(2,1)S(1)} %slice.6), channel_id=1, source_target_pairs={{0,1},{1,2},{2,3},{3,4},{4,5},{5,6},{6,7},{7,0},{8,9},{9,10},{10,1... | collective-permute-start | bytes 589832 | tf_op jit(solution)/shard_map/ppermute | solution.py:20
  109.2 16.6 %collective-permute-start.13 = (bf16[48,2048]{1,0:T(8,128)(2,1)S(1)}, bf16[48,2048]{1,0:T(8,128)(2,1)}, u32[]{:S(2)}, u32[]{:S(2)}) collective-permute-start(bf16[48,2048]{1,0:T(8,128)(2,1)S(1)} %slice.7), channel_id=1, source_target_pairs={{0,7},{1,0},{2,1},{3,2},{4,3},{5,4},{6,5},{7,6},{8,15},{9,8},{10,9... | collective-permute-start | bytes 589832 | tf_op jit(solution)/shard_map/ppermute | solution.py:20
  133.3 4.4 %collective-permute-start.17 = (bf16[2,8,48,512]{3,2,1,0:T(8,128)(2,1)}, bf16[2,8,48,512]{3,2,1,0:T(8,128)(2,1)S(1)}, u32[]{:S(2)}, u32[]{:S(2)}) collective-permute-start(bf16[2,8,48,512]{3,2,1,0:T(8,128)(2,1)} %get-tuple-element.38), channel_id=1, source_target_pairs={{0,192},{192,0},{1,193},{193,1},{2,194},{194,2},{3,195},{195,3},{4... | collective-permute-start | bytes 2359304 | tf_op jit(solution)/shard_map/ppermute | solution.py:24
  141.1 12.7 %all-to-all-start.1 = ((bf16[4,8,48,128]{3,2,1,0:T(8,128)(2,1)}), bf16[4,8,48,128]{3,2,1,0:T(8,128)(2,1)S(1)}, u32[]{:S(2)}, u32[]{:S(2)}) async-start(bf16[4,8,48,128]{3,2,1,0:T(8,128)(2,1)} %shard_map.80), calls=%async_computation.1 | async-start | bytes 786432 | tf_op jit(solution)/shard_map/all_to_all | solution.py:178
  (11 other events, 71.1 us)
